TPU v7x, 32 devices: a whole 2x2x4 slice. The times are simulated.
32 devices in a mesh: dp: 8 (over y, x, core), expert: 4 (over z).
Axes of the slice: x: 2, y: 2, z: 4, core: 2. Of those that a mesh axis runs over, the one named last changes fastest.
Arguments:
- tokens_in: bfloat16 [8192, 2048], P(('dp', 'expert')), may hold values from -6 to 6
- out_grad: bfloat16 [8192, 2048], P(('dp', 'expert')), may hold values from -6 to 6
- expert_ids: int32 [8192, 2], P(('dp', 'expert')), may hold values from 0 to 3, all different within a row; in each aligned block of 256 rows (0 to 255, 256 to 511, ...) at most 160 rows name the same one
- gate_weights: float32 [8192, 2], P(('dp', 'expert')), may hold values from 0.05 to 0.5
- w_gate_up: bfloat16 [4, 2048, 1536], P('expert'), may hold values from -0.125 to 0.125
- w_down: bfloat16 [4, 768, 2048], P('expert'), may hold values from -0.21875 to 0.21875
Outputs:
- grad_tokens: bfloat16 [8192, 2048], P(('dp', 'expert'))
- grad_gate_up: float32 [2048, 6144], P('dp', 'expert')
- grad_down: float32 [768, 8192], P('dp', 'expert')
Inputs may be any that keep to these rules, and one draw needn't show every extreme that they name: `expert_ids`: each row names 2 different experts; every expert is named somewhere. Among the 256 rows of one device (aligned blocks, in order) no expert is named more than 160 times, and in every draw some expert is named exactly 160 times in some block.
All inputs are finite; a program needn't handle non-finite values.
Results may differ from a plain program's by a relative error of at most 0.015.
Values may be sent and summed in bfloat16 or wider, within the bound.
No kernel may reach another device: no remote copies, remote signals or barrier semaphores. Data moves between devices by JAX's collectives and lax.ppermute only.
A program may use at most 128 MiB of HBM per device.

v0:
```python
import jax
import jax.numpy as jnp
from jax import lax
from jax.sharding import PartitionSpec as P


def expert_pass(arrived_inputs, arrived_grads, w_gate_up, w_down):
    hidden_units = w_down.shape[1]
    pre_act = jnp.einsum(
        "erd,edf->erf", arrived_inputs, w_gate_up, preferred_element_type=jnp.float32
    )
    gate_pre = pre_act[..., :hidden_units]
    up_pre = pre_act[..., hidden_units:]
    sigmoid_gate = jax.nn.sigmoid(gate_pre)
    swish_gate = gate_pre * sigmoid_gate
    hidden = (swish_gate * up_pre).astype(jnp.bfloat16)
    grad_hidden = jnp.einsum(
        "erd,efd->erf", arrived_grads, w_down, preferred_element_type=jnp.float32
    )
    grad_gate = grad_hidden * up_pre * sigmoid_gate * (1.0 + gate_pre * (1.0 - sigmoid_gate))
    grad_up = grad_hidden * swish_gate
    grad_pre = jnp.concatenate([grad_gate, grad_up], axis=-1).astype(jnp.bfloat16)
    return (hidden, grad_pre)


def local(tokens_in, out_grad, expert_ids, gate_weights, w_gate_up, w_down):
    tok_rows, model_width = tokens_in.shape
    top_count = expert_ids.shape[1]
    expert_group = lax.axis_size("expert")
    local_count = w_gate_up.shape[0]
    hidden_units = w_down.shape[1]
    expert_count = local_count * expert_group
    capacity = 5 * tok_rows * top_count // (4 * expert_count)
    flat_ids = expert_ids.reshape(-1)
    one_hot = (flat_ids[:, None] == jnp.arange(expert_count, dtype=jnp.int32)[None, :]).astype(
        jnp.int32
    )
    position = jnp.sum((jnp.cumsum(one_hot, axis=0) - 1) * one_hot, axis=1)
    slot_index = flat_ids * capacity + position
    scaled = (
        (gate_weights[:, :, None] * out_grad[:, None, :].astype(jnp.float32))
        .astype(jnp.bfloat16)
        .reshape(-1, model_width)
    )
    repeated = jnp.repeat(tokens_in, top_count, axis=0)
    blank_rows = jnp.zeros((expert_count * capacity, model_width), jnp.bfloat16)
    send_inputs = (
        blank_rows.at[slot_index].set(repeated).reshape(expert_count, capacity, model_width)
    )
    send_grads = blank_rows.at[slot_index].set(scaled).reshape(expert_count, capacity, model_width)
    arrived_inputs, arrived_grads = (
        lax.all_to_all(send_inputs, "expert", split_axis=0, concat_axis=0, tiled=True),
        lax.all_to_all(send_grads, "expert", split_axis=0, concat_axis=0, tiled=True),
    )
    slot_rows = expert_group * capacity
    arrived_inputs = (
        arrived_inputs.reshape(expert_group, local_count, capacity, model_width)
        .transpose(1, 0, 2, 3)
        .reshape(local_count, slot_rows, model_width)
    )
    arrived_grads = (
        arrived_grads.reshape(expert_group, local_count, capacity, model_width)
        .transpose(1, 0, 2, 3)
        .reshape(local_count, slot_rows, model_width)
    )
    hidden, grad_pre = expert_pass(arrived_inputs, arrived_grads, w_gate_up, w_down)
    back_rows = jnp.einsum(
        "erf,edf->erd", grad_pre, w_gate_up, preferred_element_type=jnp.float32
    ).astype(jnp.bfloat16)
    back_rows = (
        back_rows.reshape(local_count, expert_group, capacity, model_width)
        .transpose(1, 0, 2, 3)
        .reshape(expert_count, capacity, model_width)
    )
    returned = lax.all_to_all(back_rows, "expert", split_axis=0, concat_axis=0, tiled=True).reshape(
        expert_count * capacity, model_width
    )
    picked = returned[slot_index].reshape(tok_rows, top_count, model_width).astype(jnp.float32)
    grad_tokens = jnp.sum(picked, axis=1).astype(jnp.bfloat16)
    whole_pair = jnp.einsum(
        "erd,erj->dej", arrived_inputs, grad_pre, preferred_element_type=jnp.float32
    ).reshape(model_width, -1)
    whole_lower = jnp.einsum(
        "erf,erd->fed", hidden, arrived_grads, preferred_element_type=jnp.float32
    ).reshape(hidden_units, -1)
    pair_sum = lax.psum_scatter(
        whole_pair.astype(jnp.bfloat16), "dp", scatter_dimension=0, tiled=True
    ).astype(jnp.float32)
    lower_sum = lax.psum_scatter(
        whole_lower.astype(jnp.bfloat16), "dp", scatter_dimension=0, tiled=True
    ).astype(jnp.float32)
    return (grad_tokens, pair_sum, lower_sum)


def solution(mesh):
    in_specs = (
        P(("dp", "expert"), None),
        P(("dp", "expert"), None),
        P(("dp", "expert"), None),
        P(("dp", "expert"), None),
        P("expert", None, None),
        P("expert", None, None),
    )
    out_specs = (P(("dp", "expert"), None), P("dp", "expert"), P("dp", "expert"))
    return jax.shard_map(local, mesh=mesh, in_specs=in_specs, out_specs=out_specs, check_vma=False)
```

profile of v0, /device:TPU:0, one launch (start us, length us, event | category | flops | bytes accessed | tf_op | source)
XLA Modules:
  0.0 287.7 jit_solution(13172787374153164446)
XLA Ops:
  7.2 0.0 copy-start
  7.2 0.8 broadcast_multiply_fusion
  8.0 0.9 copy.18
  8.9 0.1 eq.29
  9.1 0.1 eq.25
  9.2 0.1 copy.17
  9.4 0.1 mul.60
  9.5 1.2 reduce-window.6
  10.8 0.2 slice_reduce_fusion
  11.0 0.2 reduce-window.9
  11.2 0.1 add_bitcast_fusion
  11.2 3.8 %broadcast_in_dim.5 = bf16[256,2,2048]{2,1,0:T(2,128)(2,1)} broadcast(bf16[256,2048]{1,0:T(8,128)(2,1)} %param.6), dimensions={0,2} | broadcast | bytes 3145728 | tf_op jit(solution)/shard_map/broadcast_in_dim | solution.py:45
  15.0 4.1 %reshape.159 = bf16[512,2048]{1,0:T(8,128)(2,1)} reshape(bf16[256,2,2048]{2,1,0:T(2,128)(2,1)} %broadcast_in_dim.5) | data formatting | bytes 4194304 | tf_op jit(solution)/shard_map/reshape | solution.py:45
  19.2 6.5 %scatter_custom_fusion.1 = bf16[640,2048]{1,0:T(8,128)(2,1)} fusion(s32[512]{0:T(512)S(1)} %bitcast.84, bf16[512,2048]{1,0:T(8,128)(2,1)} %reshape.159, bf16[]{:T(256)} %constant.6.clone.1), kind=kCustom, calls=%fused_computation.28 | custom fusion | bytes 2621952 | tf_op jit(solution)/shard_map/scatter | solution.py:48
  25.6 6.5 %all-to-all-start.1 = ((bf16[4,160,2048]{2,1,0:T(8,128)(2,1)}), bf16[4,160,2048]{2,1,0:T(8,128)(2,1)}, u32[]{:S(2)}, u32[]{:S(2)}) async-start(bf16[4,160,2048]{2,1,0:T(8,128)(2,1)} %bitcast.82), calls=%async_computation.1 | async-start | bytes 5242880 | tf_op jit(solution)/shard_map/all_to_all | solution.py:52
  32.1 0.1 copy.20
  32.2 0.1 mul.62
  32.4 5.4 %mul.64 = f32[256,2,2048]{2,1,0:T(2,128)} broadcast(bf16[256,2048]{1,0:T(8,128)(2,1)} %param.7), dimensions={0,2} | broadcast | bytes 5242880 | tf_op jit(solution)/shard_map/mul | solution.py:41
  37.8 6.1 %mul.65 = f32[512,2048]{1,0:T(8,128)} reshape(f32[256,2,2048]{2,1,0:T(2,128)} %mul.64) | data formatting | bytes 8388608 | tf_op jit(solution)/shard_map/mul | solution.py:41
  44.0 7.1 %scatter_custom_fusion = bf16[640,2048]{1,0:T(8,128)(2,1)} fusion(s32[512]{0:T(512)S(1)} %bitcast.85, f32[512,2048]{1,0:T(8,128)} %mul.65, f32[512]{0:T(512)S(1)} %mul.62, bf16[]{:T(256)} %constant.6.clone.1), kind=kCustom, calls=%fused_computation.16 | custom fusion | flops 2097152 | bytes 6817794 | tf_op jit(solution)/shard_map/scatter | solution.py:50
  51.0 40.7 %all-to-all-done.1 = bf16[4,160,2048]{2,1,0:T(8,128)(2,1)} async-done(((bf16[4,160,2048]{2,1,0:T(8,128)(2,1)}), bf16[4,160,2048]{2,1,0:T(8,128)(2,1)}, u32[]{:S(2)}, u32[]{:S(2)}) %all-to-all-start.1) | async-done | bytes 2621472 | tf_op jit(solution)/shard_map/all_to_all | solution.py:52
  91.7 4.6 %all-to-all-start = ((bf16[4,160,2048]{2,1,0:T(8,128)(2,1)}), bf16[4,160,2048]{2,1,0:T(8,128)(2,1)}, u32[]{:S(2)}, u32[]{:S(2)}) async-start(bf16[4,160,2048]{2,1,0:T(8,128)(2,1)} %bitcast.81), calls=%async_computation | async-start | bytes 5242880 | tf_op jit(solution)/shard_map/all_to_all | solution.py:53
  96.3 0.0 reduce-scatter.7.cloned.1.call-start
  96.3 9.7 %fusion.5 = f32[1,640,1536]{2,1,0:T(8,128)} fusion(bf16[640,2048]{1,0:T(8,128)(2,1)} %bitcast.8, bf16[1,2048,1536]{2,1,0:T(8,128)(2,1)} %param.10), kind=kOutput, calls=%fused_computation.10 | convolution fusion | flops 4026531840 | bytes 12845056 | tf_op jit(solution)/shard_map/erd,edf->erf/dot_general | solution.py:9
  106.1 49.1 %all-to-all-done = bf16[4,160,2048]{2,1,0:T(8,128)(2,1)} async-done(((bf16[4,160,2048]{2,1,0:T(8,128)(2,1)}), bf16[4,160,2048]{2,1,0:T(8,128)(2,1)}, u32[]{:S(2)}, u32[]{:S(2)}) %all-to-all-start) | async-done | bytes 2621472 | tf_op jit(solution)/shard_map/all_to_all | solution.py:53
  155.2 7.4 %fusion.13 = bf16[768,2048]{0,1:T(8,128)(2,1)} fusion(bf16[640,2048]{1,0:T(8,128)(2,1)} %bitcast.4, f32[1,640,1536]{2,1,0:T(8,128)} %fusion.5), kind=kOutput, calls=%fused_computation.15 | convolution fusion | flops 2017787904 | bytes 9699328 | tf_op jit(solution)/shard_map/erf,erd->fed/dot_general | solution.py:83
  162.6 4.7 %copy.23 = bf16[768,2048]{1,0:T(8,128)(2,1)} copy(bf16[768,2048]{0,1:T(8,128)(2,1)} %fusion.13) | data formatting | bytes 6291456
  167.2 0.0 reduce-scatter.7.cloned.1.call-update
  167.3 0.3 reduce-scatter.5.cloned.1.call-start
  167.5 5.7 %fusion.27 = (bf16[640,768]{1,0:T(8,128)(2,1)S(1)}, bf16[640,768]{1,0:T(8,128)(2,1)S(1)}) fusion(f32[1,640,1536]{2,1,0:T(8,128)} %fusion.5, bf16[640,2048]{1,0:T(8,128)(2,1)} %bitcast.4, bf16[1,768,2048]{2,1,0:T(8,128)(2,1)S(1)} %copy-done), kind=kOutput, calls=%fused_computation.33 | convolution fusion | flops 2019655680 | bytes 11665408 | tf_op jit(solution)/shard_map/erd,efd->erf/dot_general | solution.py:17
  173.2 0.0 copy-start.3
  173.2 0.0 copy-start.5
  173.2 0.9 copy-done.3
  174.2 0.3 copy-done.5
  174.5 8.9 %fusion = bf16[2048,1536]{0,1:T(8,128)(2,1)} fusion(bf16[640,2048]{1,0:T(8,128)(2,1)} %bitcast.8, bf16[640,768]{1,0:T(8,128)(2,1)S(1)} %get-tuple-element.13, bf16[640,768]{1,0:T(8,128)(2,1)S(1)} %get-tuple-element.12), kind=kOutput, calls=%fused_computation.4 | convolution fusion | flops 4033609728 | bytes 10878976 | tf_op jit(solution)/shard_map/erd,erj->dej/dot_general | solution.py:80
  183.4 0.0 reduce-scatter.5.cloned.1.call-update
  183.4 1.2 copy-done.4
  184.6 0.3 copy-done.6
  184.9 8.3 %fusion.8 = bf16[640,2048]{1,0:T(8,128)(2,1)} fusion(bf16[1,2048,1536]{2,1,0:T(8,128)(2,1)} %param.10, bf16[640,768]{1,0:T(8,128)(2,1)S(1)} %copy-done.6, bf16[640,768]{1,0:T(8,128)(2,1)S(1)} %copy-done.4), kind=kOutput, calls=%fused_computation.12 | convolution fusion | flops 4031774720 | bytes 10878976 | tf_op jit(solution)/shard_map/erf,edf->erd/dot_general | solution.py:67
  193.2 3.9 %all-to-all-start.2 = ((bf16[4,160,2048]{2,1,0:T(8,128)(2,1)}), bf16[4,160,2048]{2,1,0:T(8,128)(2,1)S(1)}, u32[]{:S(2)}, u32[]{:S(2)}) async-start(bf16[4,160,2048]{2,1,0:T(8,128)(2,1)} %bitcast.83), calls=%async_computation.2 | async-start | bytes 5242880 | tf_op jit(solution)/shard_map/all_to_all | solution.py:75
  197.2 58.6 %all-to-all-done.2 = bf16[4,160,2048]{2,1,0:T(8,128)(2,1)S(1)} async-done(((bf16[4,160,2048]{2,1,0:T(8,128)(2,1)}), bf16[4,160,2048]{2,1,0:T(8,128)(2,1)S(1)}, u32[]{:S(2)}, u32[]{:S(2)}) %all-to-all-start.2) | async-done | bytes 2621472 | tf_op jit(solution)/shard_map/all_to_all | solution.py:75
  255.8 3.3 %gather_fusion = bf16[512,2048]{1,0:T(8,128)(2,1)} fusion(bf16[640,2048]{1,0:T(8,128)(2,1)S(1)} %bitcast.80, s32[1024]{0:T(1024)S(1)} %pad_clamp_fusion), kind=kCustom, calls=%fused_computation | custom fusion | bytes 4196352 | tf_op jit(solution)/shard_map/gather | solution.py:78
  259.1 4.4 %reshape.137 = bf16[256,2,2048]{2,1,0:T(2,128)(2,1)} reshape(bf16[512,2048]{1,0:T(8,128)(2,1)} %gather_fusion) | data formatting | bytes 4194304 | tf_op jit(solution)/shard_map/reshape | solution.py:78
  263.5 7.8 %reduce_sum.25 = bf16[256,2048]{1,0:T(8,128)(2,1)} reduce(bf16[256,2,2048]{2,1,0:T(2,128)(2,1)} %reshape.137, bf16[]{:T(256)} %constant.6.clone.1), dimensions={1}, to_apply=%region_5.6 | reduce | flops 524288 | bytes 3145730 | tf_op jit(solution)/shard_map/reduce_sum | solution.py:79
  271.3 2.0 copy.24
  273.4 2.1 copy.22
  275.5 2.8 reduce-scatter.5.cloned.1.call-done
  278.3 2.5 copy.21
  (12 shorter events, 0.1 us)
Async XLA Ops:
  7.2 160.4 %copy-start = (bf16[1,768,2048]{2,1,0:T(8,128)(2,1)S(1)}, bf16[1,768,2048]{2,1,0:T(8,128)(2,1)}, u32[]{:S(2)}) copy-start(bf16[1,768,2048]{2,1,0:T(8,128)(2,1)} %param.11) | copy-start | bytes 9437188
  25.6 6.5 %copy-start.2 = (f32[256,2]{0,1:T(2,128)S(1)}, f32[256,2]{0,1:T(2,128)}, u32[]{:S(2)}) copy-start(f32[256,2]{0,1:T(2,128)} %param.9) | copy-start | bytes 6148
  25.6 66.1 %all-to-all-start.1 = ((bf16[4,160,2048]{2,1,0:T(8,128)(2,1)}), bf16[4,160,2048]{2,1,0:T(8,128)(2,1)}, u32[]{:S(2)}, u32[]{:S(2)}) async-start(bf16[4,160,2048]{2,1,0:T(8,128)(2,1)} %bitcast.82), calls=%async_computation.1 | async-start | bytes 5242880 | tf_op jit(solution)/shard_map/all_to_all | solution.py:52
  91.7 63.5 %all-to-all-start = ((bf16[4,160,2048]{2,1,0:T(8,128)(2,1)}), bf16[4,160,2048]{2,1,0:T(8,128)(2,1)}, u32[]{:S(2)}, u32[]{:S(2)}) async-start(bf16[4,160,2048]{2,1,0:T(8,128)(2,1)} %bitcast.81), calls=%async_computation | async-start | bytes 5242880 | tf_op jit(solution)/shard_map/all_to_all | solution.py:53
  96.3 175.1 %reduce-scatter.7.cloned.1.call-start = ((), (), s32[]{:S(2)}) async-start(), calls=%async_computation.6 | async-start | bytes 3538944
  167.3 111.0 %reduce-scatter.5.cloned.1.call-start = ((), (), s32[]{:S(2)}) async-start(), calls=%async_computation.5 | async-start | bytes 7077888 | tf_op jit(solution)/shard_map/reduce_scatter | solution.py:86
  173.2 0.9 copy-start.3
  173.2 1.3 copy-start.5
  183.4 1.2 copy-start.4
  183.4 1.5 copy-start.6
  193.2 62.6 %all-to-all-start.2 = ((bf16[4,160,2048]{2,1,0:T(8,128)(2,1)}), bf16[4,160,2048]{2,1,0:T(8,128)(2,1)S(1)}, u32[]{:S(2)}, u32[]{:S(2)}) async-start(bf16[4,160,2048]{2,1,0:T(8,128)(2,1)} %bitcast.83), calls=%async_computation.2 | async-start | bytes 5242880 | tf_op jit(solution)/shard_map/all_to_all | solution.py:75
  263.5 17.3 %copy-start.1 = (bf16[1,768,2048]{2,1,0:T(8,128)(2,1)S(1)}, bf16[1,768,2048]{2,1,0:T(8,128)(2,1)}, u32[]{:S(2)}) copy-start(bf16[1,768,2048]{2,1,0:T(8,128)(2,1)} %param.11) | copy-start | bytes 9437188
Sparse Core Ops, SparseCore 0:
  167.4 45.3 reduce-scatter.6
  216.5 61.7 reduce-scatter.4
where the time goes:
time: 289 us; the launch traced here: 288 us
  waiting for transfers between devices  151 us (52%)
  local copies, waits for them, and re-layouts  49.7 us (17%)
  matrix products  40 us (14%)
  other arithmetic  17.2 us (6%)
  starting transfers between devices  15.2 us (5%)
  between operations  14.2 us (5%)
    all_to_all x1, waiting for transfers between devices, local(): lax.all_to_all(back_rows, 'expert', split_axis=0, concat_axis=0, tiled=True)  58.6 us
    all_to_all x1, waiting for transfers between devices, local(): lax.all_to_all(send_grads, 'expert', split_axis=0, concat_axis=0, tiled=T...  49.1 us
    all_to_all x1, waiting for transfers between devices, local(): lax.all_to_all(send_inputs, 'expert', split_axis=0, concat_axis=0, tiled=...  40.7 us
    unnamed x20, local copies, waits for them, and re-layouts  15.2 us
    mul x3, local copies, waits for them, and re-layouts, local(): gate_weights[:, :, None] * out_grad[:, None, :].astype(jnp.float32)  11.7 us
    dot_general x1, matrix products, expert_pass(): jnp.einsum('erd,edf->erf', arrived_inputs, w_gate_up, preferred_element_t...  9.74 us
    dot_general x1, matrix products, local(): jnp.einsum('erd,erj->dej', arrived_inputs, grad_pre, preferred_element_ty...  8.94 us
    dot_general x1, matrix products, local(): jnp.einsum('erf,edf->erd', grad_pre, w_gate_up, preferred_element_type=jn...  8.31 us
  transfers between devices with their start and end apart: 5, of which 4 were waited for; matrix products, arithmetic and copies ran while one was open for 25% of the time, Pallas kernels for 0%

commit v1 on v0

v1 whole, which is shorter than its diff:
```python
import functools
import math

import jax
import jax.numpy as jnp
from jax import lax
from jax.experimental import pallas as pl
from jax.experimental.pallas import tpu as pltpu
from jax.sharding import PartitionSpec as P

F32 = jnp.float32
BF16 = jnp.bfloat16
MIB = 1024 * 1024


def params(grid_rank, mebibytes):
    return pltpu.CompilerParams(
        dimension_semantics=("arbitrary",) * grid_rank, vmem_limit_bytes=mebibytes * MIB
    )


FREE = pl.CostEstimate(flops=1, bytes_accessed=1, transcendentals=0)


def whole(array):
    rank = array.ndim
    return pl.BlockSpec(
        array.shape, lambda *at: (0,) * rank, pipeline_mode=pl.Buffered(buffer_count=1)
    )


def dot(a, b):
    return lax.dot_general(a, b, (((1,), (0,)), ((), ())), preferred_element_type=F32)


def dot_nt(a, b):
    return lax.dot_general(a, b, (((1,), (1,)), ((), ())), preferred_element_type=F32)


def pick_matrices(me, ids, offsets, capacity):
    top, rows = ids.shape
    lines = max(8, max(offsets) + 1)
    wanted = (lax.broadcasted_iota(jnp.int32, (lines, rows), 0) ^ me).astype(F32)
    named = ids[0:1, :] == wanted
    for k in range(1, top):
        named = named | (ids[k : k + 1, :] == wanted)
    named = named.astype(F32)
    before = lax.broadcasted_iota(jnp.int32, (rows, rows), 0) <= lax.broadcasted_iota(
        jnp.int32, (rows, rows), 1
    )
    place = dot(named.astype(BF16), before.astype(F32).astype(BF16))
    place = jnp.where(named > 0, place - 1.0, -1.0)
    slots = lax.broadcasted_iota(jnp.int32, (capacity, rows), 0).astype(F32)
    return [(place[m : m + 1, :] == slots).astype(F32) for m in offsets]


def pack_kernel(offsets, joint, me_ref, meta_ref, tokens_ref, grads_ref, *rest):
    outs, pick, gain = rest[:-2], rest[-2], rest[-1]
    capacity = pick.shape[1]

    @pl.when(pl.program_id(0) == 0)
    def _():
        me, meta = me_ref[0], meta_ref[...]
        top = meta.shape[0] // 2
        ids, gates = meta[:top], meta[top:]
        for at, matrix in enumerate(pick_matrices(me, ids, offsets, capacity)):
            pick[at] = matrix.astype(BF16)
            chosen = jnp.where(ids == (me ^ offsets[at]).astype(F32), gates, 0.0)
            weight = jnp.sum(chosen, axis=0, keepdims=True)
            gain[at] = jnp.broadcast_to(
                jnp.sum(matrix * weight, axis=1, keepdims=True), gain.shape[1:]
            )

    outs = list(outs)
    for at, m in enumerate(offsets):
        row = dot(pick[at], tokens_ref[...]).astype(BF16)
        grad = (dot(pick[at], grads_ref[...]) * gain[at][:, 0:1]).astype(BF16)
        if m in joint:
            out = outs.pop(0)
            out[0], out[1] = row, grad
        else:
            outs.pop(0)[...] = row
            outs.pop(0)[...] = grad


def pack(me, meta, tokens, grads, offsets, joint, capacity):
    rows, width = tokens.shape
    block = min(width, 512)
    out_specs, out_shape = [], []
    for m in offsets:
        if m in joint:
            out_specs.append(pl.BlockSpec((2, capacity, block), lambda i: (0, 0, i)))
            out_shape.append(jax.ShapeDtypeStruct((2, capacity, width), BF16))
        else:
            out_specs += [pl.BlockSpec((capacity, block), lambda i: (0, i))] * 2
            out_shape += [jax.ShapeDtypeStruct((capacity, width), BF16)] * 2
    count = len(offsets)
    return pl.pallas_call(
        functools.partial(pack_kernel, offsets, joint),
        grid=(width // block,),
        in_specs=[
            pl.BlockSpec(memory_space=pltpu.SMEM),
            pl.BlockSpec(meta.shape, lambda i: (0, 0)),
            pl.BlockSpec((rows, block), lambda i: (0, i)),
            pl.BlockSpec((rows, block), lambda i: (0, i)),
        ],
        out_specs=out_specs,
        out_shape=out_shape,
        scratch_shapes=[
            pltpu.VMEM((count, capacity, rows), BF16),
            pltpu.VMEM((count, capacity, 128), F32),
        ],
        compiler_params=params(1, 14),
        cost_estimate=FREE,
        name="pack",
    )(me, meta, tokens, grads)


def combine_kernel(group, me_ref, meta_ref, *refs):
    blocks, out, pick = refs[:group], refs[group], refs[group + 1]
    capacity = blocks[0].shape[0]

    @pl.when(pl.program_id(0) == 0)
    def _():
        ids = meta_ref[...][: meta_ref.shape[0] // 2]
        matrices = pick_matrices(me_ref[0], ids, list(range(group)), capacity)
        for m, matrix in enumerate(matrices):
            pick[m] = matrix.T.astype(BF16)

    total = dot(pick[0], blocks[0][...])
    for m in range(1, group):
        total += dot(pick[m], blocks[m][...])
    out[...] = total.astype(BF16)


def combine(me, meta, blocks):
    group, (capacity, width) = len(blocks), blocks[0].shape
    rows = meta.shape[1]
    block = min(width, 512)
    return pl.pallas_call(
        functools.partial(combine_kernel, group),
        grid=(width // block,),
        in_specs=[
            pl.BlockSpec(memory_space=pltpu.SMEM),
            pl.BlockSpec(meta.shape, lambda i: (0, 0)),
        ]
        + [pl.BlockSpec((capacity, block), lambda i: (0, i))] * group,
        out_specs=pl.BlockSpec((rows, block), lambda i: (0, i)),
        out_shape=jax.ShapeDtypeStruct((rows, width), BF16),
        scratch_shapes=[pltpu.VMEM((group, rows, capacity), BF16)],
        compiler_params=params(1, 10),
        cost_estimate=FREE,
        name="combine",
    )(me, meta, *blocks)


def padded(rows):
    return -(-rows // 128) * 128


def gather_rows(parts, sizes, held):
    at, parts = 0, list(parts)
    for size in sizes:
        mine, parts = parts[:size], parts[size:]
        rows = mine[0][...]
        for other in mine[1:]:
            rows = rows + other[...]
        held[at : at + rows.shape[0], :] = rows
        at += rows.shape[0]
    if at < held.shape[0]:
        held[at:, :] = jnp.zeros((held.shape[0] - at, held.shape[1]), held.dtype)


def part_spec(array, capacity, which):
    width = array.shape[-1]
    once = pl.Buffered(buffer_count=1)
    if array.ndim == 2:
        return pl.BlockSpec((capacity, width), lambda i: (0, 0), pipeline_mode=once)
    return pl.BlockSpec((None, capacity, width), lambda i: (which, 0, 0), pipeline_mode=once)


def forward_kernel(sizes, *refs):
    count = sum(sizes)
    gate_w, up_w = refs[count : count + 2]
    gate_out, up_out, hidden_out, flipped, held = refs[-5:]

    @pl.when(pl.program_id(0) == 0)
    def _():
        gather_rows(refs[:count], sizes, held)
        step = min(held.shape[1], 256)
        for d in range(0, held.shape[1], step):
            flipped[d : d + step, :] = held[:, d : d + step].T

    gate, up = dot(held[...], gate_w[...]), dot(held[...], up_w[...])
    sigmoid = jax.nn.sigmoid(gate)
    swish = gate * sigmoid
    gate_out[...] = (up * sigmoid * (1.0 + gate * (1.0 - sigmoid))).astype(BF16)
    up_out[...] = swish.astype(BF16)
    hidden_out[...] = (swish * up).T.astype(BF16)


def forward(half, sources, w_pair, before):
    arrays, sizes = sum(sources, []), [len(s) for s in sources]
    capacity, width = arrays[0].shape[-2:]
    units = w_pair.shape[1] // 2
    tile = math.gcd(units, 256)
    tiles = units // tile
    rows = padded(len(sources) * capacity)
    shapes = [
        jax.ShapeDtypeStruct((rows, units), BF16),
        jax.ShapeDtypeStruct((rows, units), BF16),
        jax.ShapeDtypeStruct((units, 2 * rows), BF16),
        jax.ShapeDtypeStruct((width, 2 * rows), BF16),
    ]
    first = len(arrays) + 2
    return pl.pallas_call(
        functools.partial(forward_kernel, sizes),
        grid=(tiles,),
        in_specs=[part_spec(a, capacity, 0) for a in arrays]
        + [
            pl.BlockSpec((width, tile), lambda j: (0, j)),
            pl.BlockSpec((width, tile), lambda j: (0, tiles + j)),
        ]
        + [pl.BlockSpec(memory_space=pl.ANY) for _ in before],
        out_specs=[
            pl.BlockSpec((rows, tile), lambda j: (0, j)),
            pl.BlockSpec((rows, tile), lambda j: (0, j)),
            pl.BlockSpec((tile, rows), lambda j: (j, half)),
            pl.BlockSpec((width, rows), lambda j: (0, half)),
        ],
        out_shape=shapes,
        scratch_shapes=[pltpu.VMEM((rows, width), BF16)],
        input_output_aliases={first + i: 2 + i for i in range(len(before))},
        compiler_params=params(1, 20),
        cost_estimate=FREE,
        name="forward",
    )(*arrays, w_pair, w_pair, *before)


def inner_kernel(sizes, tiles, rows, *refs):
    count, sources = sum(sizes), len(sizes)
    down_w, gate_d, up_d, w_ref = refs[count : count + 4]
    outs, (grads, gate_out, up_out, grad_pre) = refs[-4 - sources : -4], refs[-4:]
    step = pl.program_id(0)
    units = grad_pre.shape[1] // 2

    @pl.when(step == 0)
    def _():
        gather_rows(refs[:count], sizes, grads)

    for j in range(tiles):

        @pl.when(step == j)
        def _():
            grad_hidden = dot_nt(grads[:rows, :], down_w[...])
            tile = grad_hidden.shape[1]
            for at, slope, out in ((0, gate_d, gate_out), (units, up_d, up_out)):
                value = (grad_hidden * slope[:rows, :].astype(F32)).astype(BF16)
                grad_pre[:, at + j * tile : at + (j + 1) * tile] = value
                out[:rows, :] = value
                if rows < out.shape[0]:
                    out[rows:, :] = jnp.zeros((out.shape[0] - rows, tile), BF16)

    @pl.when(step >= tiles)
    def _():
        back = dot_nt(grad_pre[...], w_ref[...])
        capacity = rows // sources
        for m, out in enumerate(outs):
            out[...] = back[m * capacity : (m + 1) * capacity, :].astype(BF16)


def inner(half, sources, w_down, gate_d, up_d, w_pair, before):
    arrays, sizes = sum(sources, []), [len(s) for s in sources]
    capacity, width = arrays[0].shape[-2:]
    units = w_down.shape[0]
    tile = math.gcd(units, 256)
    tiles = units // tile
    block = min(width, 512)
    rows = len(sources) * capacity
    held = padded(rows)

    def tile_at(i):
        return jnp.minimum(i, tiles - 1)

    def block_at(i):
        return jnp.maximum(i - tiles, 0)

    first, outs = len(arrays) + 4, len(sources)
    return pl.pallas_call(
        functools.partial(inner_kernel, sizes, tiles, rows),
        grid=(tiles + width // block,),
        in_specs=[part_spec(a, capacity, 1) for a in arrays]
        + [
            pl.BlockSpec((tile, width), lambda i: (tile_at(i), 0)),
            pl.BlockSpec((held, tile), lambda i: (0, tile_at(i))),
            pl.BlockSpec((held, tile), lambda i: (0, tile_at(i))),
            pl.BlockSpec((block, 2 * units), lambda i: (block_at(i), 0)),
        ]
        + [pl.BlockSpec(memory_space=pl.ANY) for _ in before],
        out_specs=[pl.BlockSpec((capacity, block), lambda i: (0, block_at(i)))] * outs
        + [
            pl.BlockSpec((held, width), lambda i: (half, 0)),
            pl.BlockSpec((held, tile), lambda i: (half, tile_at(i))),
            pl.BlockSpec((held, tile), lambda i: (half, tile_at(i))),
        ],
        out_shape=[jax.ShapeDtypeStruct((capacity, width), BF16)] * outs
        + [
            jax.ShapeDtypeStruct((2 * held, width), BF16),
            jax.ShapeDtypeStruct((2 * held, units), BF16),
            jax.ShapeDtypeStruct((2 * held, units), BF16),
        ],
        scratch_shapes=[pltpu.VMEM((rows, 2 * units), BF16)],
        input_output_aliases={first + i: outs + i for i in range(len(before))},
        compiler_params=params(1, 20),
        cost_estimate=FREE,
        name="inner",
    )(*arrays, w_down, gate_d, up_d, w_pair, *before)


def pair_chunks(flipped_rows, sides, chunk):
    for side in sides:
        for c in range(0, side.shape[1], chunk):
            yield dot(flipped_rows, side[:, c : c + chunk])


def lower_share(rows, chunk):
    return jnp.concatenate([rows[:, c : c + chunk] for c in range(0, rows.shape[1], chunk)], axis=0)


def hold_lower(which, shares, hidden_ref, rows, lower):
    own = hidden_ref.shape[1]
    stacked = jnp.concatenate(
        [hidden_ref[which(r)].astype(F32) for r in range(shares)], axis=0
    ).astype(BF16)
    lower[...] = dot(stacked, rows).reshape(shares, own, rows.shape[1])


def give_kernel(shares, chunk, which_ref, flip_ref, hidden_ref, grads, gate, up, out, lower):
    step = pl.program_id(0)

    @pl.when(step == 0)
    def _():
        hold_lower(lambda r: which_ref[r], shares, hidden_ref, grads[...], lower)

    at = 0
    for piece in pair_chunks(flip_ref[0], (gate[...], up[...]), chunk):
        out[0, at : at + piece.shape[0]] = piece.astype(BF16)
        at += piece.shape[0]
    out[0, at:] = lower_share(lower[step], chunk).astype(BF16)


def shared_operands(flipped, hidden, replicas):
    width, rows = flipped.shape
    units = hidden.shape[0]
    return (
        flipped.reshape(replicas, width // replicas, rows),
        hidden.reshape(replicas, units // replicas, rows),
    )


def give(which, flipped, hidden, grads, gate, up, replicas, chunk):
    rows, width = grads.shape
    units = gate.shape[1]
    shares = replicas // 2
    share_rows = (2 * units * (width // replicas) + (units // replicas) * width) // chunk
    flipped, hidden = shared_operands(flipped, hidden, replicas)
    return pl.pallas_call(
        functools.partial(give_kernel, shares, chunk),
        grid_spec=pltpu.PrefetchScalarGridSpec(
            num_scalar_prefetch=1,
            grid=(shares,),
            in_specs=[pl.BlockSpec((1, width // replicas, rows), lambda i, w: (w[i], 0, 0))]
            + [whole(a) for a in (hidden, grads, gate, up)],
            out_specs=pl.BlockSpec((1, share_rows, chunk), lambda i, w: (i, 0, 0)),
            scratch_shapes=[pltpu.VMEM((shares, units // replicas, width), F32)],
        ),
        out_shape=jax.ShapeDtypeStruct((shares, share_rows, chunk), BF16),
        compiler_params=params(1, 18),
        cost_estimate=FREE,
        name="give",
    )(which, flipped, hidden, grads, gate, up)


def split_kernel(kinds, plan_ref, own, came, *outs):
    step = pl.program_id(0)
    total = own[0].astype(F32) + came[0].astype(F32)
    half = total.shape[0] // 2

    def emit(first, second):
        first[0] = total[:half].astype(BF16)
        second[0] = total[half:].astype(BF16)

    for kind in sorted(set(kinds)):
        chosen = [step == i for i, other in enumerate(kinds) if other == kind]
        pl.when(functools.reduce(jnp.logical_or, chosen))(
            functools.partial(emit, outs[kind[0]], outs[2 + kind[1]])
        )


def without(bits, dropped, r):
    return sum(((r >> bit) & 1) << at for at, bit in enumerate(b for b in bits if b != dropped))


def split(own, came, first_bit, second_bit):
    shares, share_rows, chunk = came.shape
    half = share_rows // 2
    bits = range(shares.bit_length() - 1)

    def kind(r):
        return ((r >> first_bit) & 1, (r >> second_bit) & 1)

    order = sorted(range(shares), key=lambda r: (kind(r), r), reverse=True)
    plan = [order]
    for which, bit in ((0, first_bit), (1, second_bit)):
        for side in (0, 1):
            places = [without(bits, bit, r) if kind(r)[which] == side else None for r in order]
            last = next(p for p in places if p is not None)
            held = []
            for place in places:
                last = last if place is None else place
                held.append(last)
            plan.append(held)
    share = pl.BlockSpec((1, share_rows, chunk), lambda i, p: (p[0, i], 0, 0))
    return pl.pallas_call(
        functools.partial(split_kernel, [kind(r) for r in order]),
        grid_spec=pltpu.PrefetchScalarGridSpec(
            num_scalar_prefetch=1,
            grid=(shares,),
            in_specs=[share, share],
            out_specs=[
                pl.BlockSpec((1, half, chunk), lambda i, p, n=n: (p[n, i], 0, 0))
                for n in range(1, 5)
            ],
        ),
        out_shape=[jax.ShapeDtypeStruct((shares // 2, half, chunk), BF16)] * 4,
        compiler_params=params(1, 14),
        cost_estimate=FREE,
        name="split",
    )(jnp.asarray(plan, jnp.int32), own, came)


def halvings(kept, sent, bits):
    present = sorted(bits, reverse=True)
    rest = [bit for bit in present if bit != bits[0]]
    tail = kept.shape[1:]
    terms = [(kept.reshape((2,) * len(rest) + tail), rest)]
    done = set()
    for bit in bits:
        if bit == bits[0]:
            give, left = sent.reshape((2,) * len(rest) + tail), rest
        else:
            left = [other for other in present if other not in done and other != bit]
            parts = []
            for array, axes in terms:
                index = tuple(1 if b == bit else 0 if b in done else slice(None) for b in axes)
                parts.append(array[index].astype(F32))
            give = sum(parts).astype(BF16)
        pairs = [(i, i ^ (2 << bit)) for i in range(lax.axis_size("dp"))]
        terms.append((lax.ppermute(give, "dp", pairs), left))
        done.add(bit)
    return [array for array, _ in terms]


def finish_kernel(count, chunk, *refs):
    halves, (pair, lower) = (refs[:count], refs[count : 2 * count]), refs[2 * count :]
    totals = []
    for terms in halves:
        total = terms[0][...].astype(F32)
        for term in terms[1:]:
            total += term[...].astype(F32)
        totals.append(total)
    half = totals[0].shape[0]
    at = 0
    for out in (pair, lower):
        rows, columns = out.shape
        for c in range(0, columns, chunk):
            cut = min(max(half - at, 0), rows)
            if cut:
                out[:cut, c : c + chunk] = totals[0][at : at + cut]
            if cut < rows:
                out[cut:, c : c + chunk] = totals[1][at + cut - half : at + rows - half]
            at += rows


def finish(firsts, seconds, pair_shape, lower_shape):
    half, chunk = firsts[0].shape[-2:]

    def leading(array):
        lead = array.ndim - 2
        return pl.BlockSpec((None,) * lead + (half, chunk), lambda i, n=lead: (0,) * (n + 2))

    return pl.pallas_call(
        functools.partial(finish_kernel, len(firsts), chunk),
        grid=(1,),
        in_specs=[leading(a) for a in firsts + seconds],
        out_specs=[
            pl.BlockSpec(pair_shape, lambda i: (0, 0)),
            pl.BlockSpec(lower_shape, lambda i: (0, 0)),
        ],
        out_shape=[
            jax.ShapeDtypeStruct(pair_shape, F32),
            jax.ShapeDtypeStruct(lower_shape, F32),
        ],
        compiler_params=params(1, 24),
        name="finish",
    )(*firsts, *seconds)


def local(tokens_in, out_grad, expert_ids, gate_weights, w_gate_up, w_down):
    tok_rows, width = tokens_in.shape
    top = expert_ids.shape[1]
    group = lax.axis_size("expert")
    replicas = lax.axis_size("dp")
    units = w_down.shape[1]
    capacity = 5 * tok_rows * top // (4 * group)
    chunk = math.gcd(units, width)
    me = lax.axis_index("expert").astype(jnp.int32)
    replica = lax.axis_index("dp").astype(jnp.int32)
    place = me.reshape(1)
    meta = jnp.concatenate([expert_ids.astype(F32), gate_weights], axis=1).T
    w_pair, w_lower = w_gate_up[0], w_down[0]

    def move(array, pairs):
        return lax.ppermute(array, "expert", pairs)

    def swap(array, m):
        return move(array, [(i, i ^ m) for i in range(group)])

    def after(array, *others):
        return lax.optimization_barrier((array, *others))[0]

    if group == 4 and tok_rows < 2 * capacity:
        far = [(0, 2), (3, 1)]
        far_meta, far_rows, far_grads = move(meta, far), move(tokens_in, far), move(out_grad, far)
        x0, g0, pair1, x2, g2, x3, g3 = pack(
            place, meta, tokens_in, out_grad, [0, 1, 2, 3], [1], capacity
        )
        pair1 = swap(after(pair1, far_rows), 1)
        cx, cg, onward = pack(place, far_meta, far_rows, far_grads, [0, 1], [1], capacity)
        onward = move(onward, [(2, 3), (1, 0)])
        x3 = move(x3, [(1, 2), (2, 1)])
        x2 = move(x2, [(1, 3), (2, 0)])
        g3 = move(after(g3, x3), [(1, 2), (2, 1)])
        g2 = move(after(g2, x2), [(1, 3), (2, 0)])
        inputs = [[x0], [pair1], [cx, x2], [onward, x3]]
        grads = [[g0], [pair1], [cg, g2], [onward, g3]]
    else:
        offsets = list(range(group))
        packed = pack(place, meta, tokens_in, out_grad, offsets, [], capacity)
        moved = [packed[2 * m : 2 * m + 2] for m in offsets]
        moved = [moved[0]] + [[swap(a, m) for a in moved[m]] for m in offsets[1:]]
        inputs, grads = [[a] for a, _ in moved], [[b] for _, b in moved]

    lead = group // 2
    early_d = forward(0, inputs[:lead], w_pair, [])
    late_d = forward(1, inputs[lead:], w_pair, early_d[2:])
    early = inner(0, grads[:lead], w_lower, *early_d[:2], w_pair, [])
    late = inner(1, grads[lead:], w_lower, *late_d[:2], w_pair, early[lead:])
    blocks = list(early[:lead]) + list(late[:lead])
    returned = [blocks[0]] + [swap(blocks[m], m) for m in range(1, group)]

    shares = replicas // 2
    own = [replica ^ (2 * r) for r in range(shares)]
    operands = (late_d[3], late_d[2], *late[lead:])
    given = give(jnp.stack(own) ^ 1, *operands, replicas, chunk)
    came = lax.ppermute(given, "dp", [(i, i ^ 1) for i in range(replicas)])
    mine = give(after(jnp.stack(own), given), *operands, replicas, chunk)
    bits = list(range(shares.bit_length() - 1))
    middle = len(bits) // 2
    first_bits, second_bits = bits, bits[middle:] + bits[:middle]
    kept_a, sent_a, kept_b, sent_b = split(mine, came, first_bits[0], second_bits[0])
    firsts = halvings(kept_a, sent_a, first_bits)
    seconds = halvings(kept_b, sent_b, second_bits)
    *returned, firsts[1], seconds[1] = lax.optimization_barrier((*returned, firsts[1], seconds[1]))
    grad_tokens = combine(place, meta, returned)
    pair_sum, lower_sum = finish(
        firsts, seconds, (width // replicas, 2 * units), (units // replicas, width)
    )
    return (grad_tokens, pair_sum, lower_sum)


def solution(mesh):
    in_specs = (
        P(("dp", "expert"), None),
        P(("dp", "expert"), None),
        P(("dp", "expert"), None),
        P(("dp", "expert"), None),
        P("expert", None, None),
        P("expert", None, None),
    )
    out_specs = (P(("dp", "expert"), None), P("dp", "expert"), P("dp", "expert"))
    return jax.shard_map(local, mesh=mesh, in_specs=in_specs, out_specs=out_specs, check_vma=False)
```

time: 289 us -> 209 us (0.72)
  the two profiles are of different devices: /device:TPU:0 before, /device:TPU:8 now
where the time goes in v1:
time: 209 us; the launch traced here: 208 us
  waiting for transfers between devices  114 us (55%)
  Pallas kernels  47.5 us (23%)
  starting transfers between devices  33.7 us (16%)
  local copies, waits for them, and re-layouts  10.6 us (5%)
    ppermute x12, waiting for transfers between devices, move(): return lax.ppermute(array, 'expert', pairs)  90 us
    ppermute x12, starting transfers between devices, move(): return lax.ppermute(array, 'expert', pairs)  27.4 us
    ppermute x4, waiting for transfers between devices, halvings(): terms.append((lax.ppermute(give, 'dp', pairs), left))  21 us
    pallas_call x2, Pallas kernels, inner(): pl.pallas_call(functools.partial(inner_kernel, sizes, tiles, rows), grid=...  11.7 us
    unnamed x38, local copies, waits for them, and re-layouts  10.6 us
    pallas_call x2, Pallas kernels, give(): pl.pallas_call(functools.partial(give_kernel, shares, chunk), grid_spec=p...  10.2 us
    pallas_call x2, Pallas kernels, forward(): pl.pallas_call(functools.partial(forward_kernel, sizes), grid=(tiles,), i...  9.27 us
    pallas_call x2, Pallas kernels, pack(): pl.pallas_call(functools.partial(pack_kernel, offsets, joint), grid=(widt...  8.23 us
  transfers between devices with their start and end apart: 17, of which 10 were waited for; matrix products, arithmetic and copies ran while one was open for 1% of the time, Pallas kernels for 15%

profile of v1, /device:TPU:8, one launch (start us, length us, event | category | flops | bytes accessed | tf_op | source)
XLA Modules:
  0.0 208.4 jit_solution(2074167645486639669)
XLA Ops:
  0.6 1.3 collective-permute-start
  1.9 1.3 collective-permute-start.4
  3.2 0.7 convert_element_type.31
  3.9 0.7 maximum_bitcast_fusion.meta_ref
  4.6 1.3 collective-permute-start.3
  5.9 1.2 copy-done.2
  7.1 1.2 copy-done.3
  8.4 3.8 %pack.2 = (bf16[160,2048]{1,0:T(8,128)(2,1)S(1)}, bf16[160,2048]{1,0:T(8,128)(2,1)S(1)}, bf16[2,160,2048]{2,1,0:T(8,128)(2,1)}, bf16[160,2048]{1,0:T(8,128)(2,1)...) custom-call(s32[1]{0:T(128)} %bitcast.me_ref, ...), custom_call_target="tpu_custom_call" | custom-call | flops 1 | bytes 1 | tf_op jit(solution)/shard_map/pack/pallas_call | solution.py:98
  12.1 0.8 copy-done.6
  13.0 0.8 copy-done.8
  13.8 15.9 %collective-permute-done.tokens_ref = bf16[256,2048]{1,0:T(8,128)(2,1)S(1)} collective-permute-done((bf16[256,2048]{1,0:T(8,128)(2,1)}, bf16[256,2048]{1,0:T(8,128)(2,1)S(1)}, u32[]{:S(2)}, u32[]{:S(2)}) %collective-permute-start) | collective-permute-done | bytes 1048608 | tf_op jit(solution)/shard_map/ppermute | solution.py:524
  29.7 5.0 %collective-permute-start.5 = (bf16[160,2048]{1,0:T(8,128)(2,1)S(1)}, bf16[160,2048]{1,0:T(8,128)(2,1)S(1)}, u32[]{:S(2)}, u32[]{:S(2)}) collective-permute-start(bf16[160,2048]{1,0:T(8,128)(2,1)S(1)} %get-tuple-element.57), channel_id=1, source_target_pairs={{1,3},{2,0},{5,7},{6,4},{9,11},{10,8},{13,15},{14,12},{17,19},{18,... | collective-permute-start | bytes 1966088 | tf_op jit(solution)/shard_map/ppermute | solution.py:524
  34.7 17.6 %collective-permute-done.3.meta_ref = f32[4,256]{1,0:T(4,128)S(1)} collective-permute-done((f32[4,256]{1,0:T(4,128)S(1)}, f32[4,256]{1,0:T(4,128)S(1)}, u32[]{:S(2)}, u32[]{:S(2)}) %collective-permute-start.3) | collective-permute-done | bytes 4128 | tf_op jit(solution)/shard_map/ppermute | solution.py:524
  52.3 4.5 %pack.3 = (bf16[160,2048]{1,0:T(8,128)(2,1)S(1)}, bf16[160,2048]{1,0:T(8,128)(2,1)S(1)}, bf16[2,160,2048]{2,1,0:T(8,128)(2,1)}) custom-call(s32[1]{0:T(128)} %bitcast.me_ref, f32[4,256]{1,0:T(4,128)S(1)} %collective-permute-done.3.meta_ref, bf16[256,2048]{1,0:T(8,128)(2,1)S(1)} %collective-permute-done.tokens_ref, ...), custom_call_target="tpu_custom_call" | custom-call | flops 1 | bytes 1 | tf_op jit(solution)/shard_map/pack/pallas_call | solution.py:98
  56.8 0.8 copy-done.10
  57.6 1.6 collective-permute-start.7
  59.2 3.2 %collective-permute-start.8 = (bf16[160,2048]{1,0:T(8,128)(2,1)S(1)}, bf16[160,2048]{1,0:T(8,128)(2,1)S(1)}, u32[]{:S(2)}, u32[]{:S(2)}) collective-permute-start(bf16[160,2048]{1,0:T(8,128)(2,1)S(1)} %get-tuple-element.61), channel_id=1, source_target_pairs={{1,2},{2,1},{5,6},{6,5},{9,10},{10,9},{13,14},{14,13},{17,18},{18,... | collective-permute-start | bytes 1966088 | tf_op jit(solution)/shard_map/ppermute | solution.py:524
  62.5 1.9 collective-permute-done.5.refs_1_
  64.4 0.9 copy-done.4
  65.2 6.1 %collective-permute-start.6 = (bf16[160,2048]{1,0:T(8,128)(2,1)}, bf16[160,2048]{1,0:T(8,128)(2,1)}, u32[]{:S(2)}, u32[]{:S(2)}) collective-permute-start(bf16[160,2048]{1,0:T(8,128)(2,1)} %get-tuple-element.58), channel_id=1, source_target_pairs={{1,3},{2,0},{5,7},{6,4},{9,11},{10,8},{13,15},{14,12},{17,19},{18,... | collective-permute-start | bytes 1966088 | tf_op jit(solution)/shard_map/ppermute | solution.py:524
  71.4 7.9 %collective-permute-done.8.refs_3_ = bf16[160,2048]{1,0:T(8,128)(2,1)S(1)} collective-permute-done((bf16[160,2048]{1,0:T(8,128)(2,1)S(1)}, bf16[160,2048]{1,0:T(8,128)(2,1)S(1)}, u32[]{:S(2)}, u32[]{:S(2)}) %collective-permute-start.8) | collective-permute-done | bytes 655392 | tf_op jit(solution)/shard_map/ppermute | solution.py:524
  79.3 0.9 copy-done.12
  80.2 3.7 %collective-permute-start.9 = (bf16[160,2048]{1,0:T(8,128)(2,1)}, bf16[160,2048]{1,0:T(8,128)(2,1)}, u32[]{:S(2)}, u32[]{:S(2)}) collective-permute-start(bf16[160,2048]{1,0:T(8,128)(2,1)} %get-tuple-element.62), channel_id=1, source_target_pairs={{1,2},{2,1},{5,6},{6,5},{9,10},{10,9},{13,14},{14,13},{17,18},{18,... | collective-permute-start | bytes 1966088 | tf_op jit(solution)/shard_map/ppermute | solution.py:524
  83.9 2.8 %copy-done = bf16[1,2048,1536]{2,1,0:T(8,128)(2,1)S(1)} copy-done((bf16[1,2048,1536]{2,1,0:T(8,128)(2,1)S(1)}, bf16[1,2048,1536]{2,1,0:T(8,128)(2,1)}, u32[]{:S(2)}) %copy-start) | copy-done | bytes 6291480
  86.7 1.1 copy-done.9
  87.8 4.6 %forward.2 = (bf16[384,768]{1,0:T(8,128)(2,1)S(1)}, bf16[384,768]{1,0:T(8,128)(2,1)S(1)}, bf16[768,768]{1,0:T(8,128)(2,1)S(1)}, bf16[2048,768]{1,0:T(8,128)(2,1)S(1)}) custom-call(bf16[160,2048]{1,0:T(8,128)(2,1)S(1)} %copy-done.9, bf16[2,160,2048]{2,1,0:T(8,128)(2,1)S(1)} %collective-permute-done.1.refs_1_, bf16[2048,1536]{1,0:T(8,128)(2,1)S(1)} %bitcast.15, ...), custom_call_target="tpu_custom_call" | custom-call | flops 1 | bytes 1 | tf_op jit(solution)/shard_map/forward/pallas_call | solution.py:216
  92.5 5.1 %inner.2 = (bf16[160,2048]{1,0:T(8,128)(2,1)S(1)}, bf16[160,2048]{1,0:T(8,128)(2,1)S(1)}, bf16[768,2048]{1,0:T(8,128)(2,1)S(1)}, bf16[768,768]{1,0:T(8,128)(2,1)S(1)}, bf16[768,768]{1,0:T(8,128)(2,1)S(1)}) custom-call(bf16[160,2048]{1,0:T(8,128)(2,1)S(1)} %copy-done.7, bf16[2,160,2048]{2,1,0:T(8,128)(2,1)S(1)} %collective-permute-done.1.refs_1_, ...), custom_call_target="tpu_custom_call" | custom-call | flops 1 | bytes 1 | tf_op jit(solution)/shard_map/inner/pallas_call | solution.py:289
  97.7 14.8 %collective-permute-done.7.refs_2_ = bf16[2,160,2048]{2,1,0:T(8,128)(2,1)S(1)} collective-permute-done((bf16[2,160,2048]{2,1,0:T(8,128)(2,1)}, bf16[2,160,2048]{2,1,0:T(8,128)(2,1)S(1)}, u32[]{:S(2)}, u32[]{:S(2)}) %collective-permute-start.7) | collective-permute-done | bytes 1310752 | tf_op jit(solution)/shard_map/ppermute | solution.py:524
  112.5 4.7 %forward.3 = (bf16[384,768]{1,0:T(8,128)(2,1)S(1)}, bf16[384,768]{1,0:T(8,128)(2,1)S(1)}, bf16[768,768]{1,0:T(8,128)(2,1)S(1)}, bf16[2048,768]{1,0:T(8,128)(2,1)S(1)}) custom-call(bf16[160,2048]{1,0:T(8,128)(2,1)S(1)} %copy-done.11, bf16[160,2048]{1,0:T(8,128)(2,1)S(1)} %copy-done.5, ...), custom_call_target="tpu_custom_call", output_to_operand_aliasing={{2}: (6, {}), {3}: (7, {})} | custom-call | flops 1 | bytes 1 | tf_op jit(solution)/shard_map/forward/pallas_call | solution.py:216
  117.2 6.6 %inner.3 = (bf16[160,2048]{1,0:T(8,128)(2,1)S(1)}, bf16[160,2048]{1,0:T(8,128)(2,1)S(1)}, bf16[768,2048]{1,0:T(8,128)(2,1)S(1)}, bf16[768,768]{1,0:T(8,128)(2,1)S(1)}, bf16[768,768]{1,0:T(8,128)(2,1)S(1)}) custom-call(bf16[160,2048]{1,0:T(8,128)(2,1)S(1)} %get-tuple-element.55.refs_0_, ...), custom_call_target="tpu_custom_call", output_to_operand_aliasing={{2}: (8, {}), {3}: (9, {}), {4}: (10, {})} | custom-call | flops 1 | bytes 1 | tf_op jit(solution)/shard_map/inner/pallas_call | solution.py:289
  123.8 5.1 %give.2 = bf16[4,2304,256]{2,1,0:T(8,128)(2,1)S(1)} custom-call(s32[4]{0:T(128)S(1)} %get-tuple-element.91.which_ref, bf16[8,256,768]{2,1,0:T(8,128)(2,1)S(1)} %bitcast.23, bf16[8,96,768]{2,1,0:T(8,128)(2,1)S(1)} %bitcast.27, bf16[768,2048]{1,0:T(8,128)(2,1)S(1)} %get-tuple-element.75.grads, bf16[768,768]{1,0:T(8,128)(2,1)S(1)} %get-tuple-element.76.gate, ...), custom_call_target="tpu_custom_call" | custom-call | flops 1 | bytes 1 | tf_op jit(solution)/shard_map/give/pallas_call | solution.py:367
  129.0 5.1 %give.3.own = bf16[4,2304,256]{2,1,0:T(8,128)(2,1)S(1)} custom-call(s32[4]{0:T(128)S(1)} %get-tuple-element.78.which_ref, bf16[8,256,768]{2,1,0:T(8,128)(2,1)S(1)} %bitcast.24, bf16[8,96,768]{2,1,0:T(8,128)(2,1)S(1)} %bitcast.28, bf16[768,2048]{1,0:T(8,128)(2,1)S(1)} %get-tuple-element.75.grads, bf16[768,768]{1,0:T(8,128)(2,1)S(1)} %get-tuple-element.76.gate, ...), custom_call_target="tpu_custom_call" | custom-call | flops 1 | bytes 1 | tf_op jit(solution)/shard_map/give/pallas_call | solution.py:367
  134.1 2.7 %collective-permute-done.12.came = bf16[4,2304,256]{2,1,0:T(8,128)(2,1)S(1)} collective-permute-done((bf16[4,2304,256]{2,1,0:T(8,128)(2,1)S(1)}, bf16[4,2304,256]{2,1,0:T(8,128)(2,1)S(1)}, u32[]{:S(2)}, u32[]{:S(2)}) %collective-permute-start.12) | collective-permute-done | bytes 4718624 | tf_op jit(solution)/shard_map/ppermute | solution.py:566
  136.9 3.2 %split.1 = (bf16[2,1152,256]{2,1,0:T(8,128)(2,1)S(1)}, bf16[2,1152,256]{2,1,0:T(8,128)(2,1)S(1)}, bf16[2,1152,256]{2,1,0:T(8,128)(2,1)S(1)}, bf16[2,1152,256]{2,1,0:T(8,128)(2,1)S(1)}) custom-call(s32[5,4]{1,0:T(8,128)S(1)} %copy-done.14, bf16[4,2304,256]{2,1,0:T(8,128)(2,1)S(1)} %give.3.own, bf16[4,2304,256]{2,1,0:T(8,128)(2,1)S(1)} %collective-permute-done.12.came), custom_call_target="tpu_custom_call" | custom-call | flops 1 | bytes 1 | tf_op jit(solution)/shard_map/split/pallas_call | solution.py:424
  140.1 1.6 collective-permute-start.13
  141.7 1.5 collective-permute-start.14
  143.2 2.4 %collective-permute-start.2 = (bf16[160,2048]{1,0:T(8,128)(2,1)S(1)}, bf16[160,2048]{1,0:T(8,128)(2,1)S(1)}, u32[]{:S(2)}, u32[]{:S(2)}) collective-permute-start(bf16[160,2048]{1,0:T(8,128)(2,1)S(1)} %copy-done.16), channel_id=1, source_target_pairs={{0,1},{1,0},{2,3},{3,2},{4,5},{5,4},{6,7},{7,6},{8,9},{9,8},{10,11... | collective-permute-start | bytes 1966088 | tf_op jit(solution)/shard_map/ppermute | solution.py:524
  145.6 1.0 collective-permute-start.10
  146.6 0.6 collective-permute-start.11
  147.1 21.0 %collective-permute-done.13.refs_1_ = bf16[2,1152,256]{2,1,0:T(8,128)(2,1)S(1)} collective-permute-done((bf16[2,1152,256]{2,1,0:T(8,128)(2,1)S(1)}, bf16[2,1152,256]{2,1,0:T(8,128)(2,1)S(1)}, u32[]{:S(2)}, u32[]{:S(2)}) %collective-permute-start.13) | collective-permute-done | bytes 1179680 | tf_op jit(solution)/shard_map/ppermute | solution.py:459
  168.3 1.6 collective-permute-start.15
  169.9 0.2 fusion.1
  170.1 1.6 collective-permute-start.16
  171.7 0.9 collective-permute-done.2.refs_1_
  172.5 17.3 %collective-permute-done.10.refs_2_ = bf16[160,2048]{1,0:T(8,128)(2,1)S(1)} collective-permute-done((bf16[160,2048]{1,0:T(8,128)(2,1)S(1)}, bf16[160,2048]{1,0:T(8,128)(2,1)S(1)}, u32[]{:S(2)}, u32[]{:S(2)}) %collective-permute-start.10) | collective-permute-done | bytes 655392 | tf_op jit(solution)/shard_map/ppermute | solution.py:524
  189.8 13.7 %collective-permute-done.11.refs_3_ = bf16[160,2048]{1,0:T(8,128)(2,1)S(1)} collective-permute-done((bf16[160,2048]{1,0:T(8,128)(2,1)S(1)}, bf16[160,2048]{1,0:T(8,128)(2,1)S(1)}, u32[]{:S(2)}, u32[]{:S(2)}) %collective-permute-start.11) | collective-permute-done | bytes 655392 | tf_op jit(solution)/shard_map/ppermute | solution.py:524
  203.5 3.2 %combine.1 = bf16[256,2048]{1,0:T(8,128)(2,1)} custom-call(s32[1]{0:T(128)} %bitcast.me_ref, f32[4,256]{1,0:T(4,128)S(1)} %maximum_bitcast_fusion.meta_ref, bf16[160,2048]{1,0:T(8,128)(2,1)S(1)} %get-tuple-element.81.refs_0_, bf16[160,2048]{1,0:T(8,128)(2,1)S(1)} %collective-permute-done.2.refs_1_, bf16[160,2048]{1,0:T(8,128)(2,1)S(1)} %collective-permute-done.10.refs_2_, ...), custom_call_target="tpu_custom_call" | custom-call | flops 1 | bytes 1 | tf_op jit(solution)/shard_map/combine/pallas_call | solution.py:140
  206.7 1.7 finish.1
  (41 shorter events, 0.4 us)
Async XLA Ops:
  0.6 29.1 %collective-permute-start = (bf16[256,2048]{1,0:T(8,128)(2,1)}, bf16[256,2048]{1,0:T(8,128)(2,1)S(1)}, u32[]{:S(2)}, u32[]{:S(2)}) collective-permute-start(bf16[256,2048]{1,0:T(8,128)(2,1)} %tokens_ref.1), channel_id=1, source_target_pairs={{0,2},{3,1},{4,6},{7,5},{8,10},{11,9},{12,14},{15,13},{16,18},{19,... | collective-permute-start | bytes 3145736 | tf_op jit(solution)/shard_map/ppermute | solution.py:524
  1.9 50.4 %collective-permute-start.4 = (bf16[256,2048]{1,0:T(8,128)(2,1)}, bf16[256,2048]{1,0:T(8,128)(2,1)}, u32[]{:S(2)}, u32[]{:S(2)}) collective-permute-start(bf16[256,2048]{1,0:T(8,128)(2,1)} %grads_ref.1), channel_id=1, source_target_pairs={{0,2},{3,1},{4,6},{7,5},{8,10},{11,9},{12,14},{15,13},{16,18},{19,... | collective-permute-start | bytes 3145736 | tf_op jit(solution)/shard_map/ppermute | solution.py:524
  4.6 47.7 %collective-permute-start.3 = (f32[4,256]{1,0:T(4,128)S(1)}, f32[4,256]{1,0:T(4,128)S(1)}, u32[]{:S(2)}, u32[]{:S(2)}) collective-permute-start(f32[4,256]{1,0:T(4,128)S(1)} %maximum_bitcast_fusion.meta_ref), channel_id=1, source_target_pairs={{0,2},{3,1},{4,6},{7,5},{8,10},{11,9},{12,14},{15,13},{16,18},{19,... | collective-permute-start | bytes 12296 | tf_op jit(solution)/shard_map/ppermute | solution.py:524
  5.9 1.2 copy-start.2
  7.1 1.2 copy-start.3
  12.1 0.8 copy-start.6
  13.0 0.8 copy-start.8
  29.7 54.2 %collective-permute-start.1 = (bf16[2,160,2048]{2,1,0:T(8,128)(2,1)}, bf16[2,160,2048]{2,1,0:T(8,128)(2,1)S(1)}, u32[]{:S(2)}, u32[]{:S(2)}) collective-permute-start(bf16[2,160,2048]{2,1,0:T(8,128)(2,1)} %get-tuple-element.49), channel_id=1, source_target_pairs={{0,1},{1,0},{2,3},{3,2},{4,5},{5,4},{6,7},{7,6},{8,9},{9,8},{10,11... | collective-permute-start | bytes 3932168 | tf_op jit(solution)/shard_map/ppermute | solution.py:524
  29.7 34.7 %collective-permute-start.5 = (bf16[160,2048]{1,0:T(8,128)(2,1)S(1)}, bf16[160,2048]{1,0:T(8,128)(2,1)S(1)}, u32[]{:S(2)}, u32[]{:S(2)}) collective-permute-start(bf16[160,2048]{1,0:T(8,128)(2,1)S(1)} %get-tuple-element.57), channel_id=1, source_target_pairs={{1,3},{2,0},{5,7},{6,4},{9,11},{10,8},{13,15},{14,12},{17,19},{18,... | collective-permute-start | bytes 1966088 | tf_op jit(solution)/shard_map/ppermute | solution.py:524
  56.8 0.8 copy-start.10
  57.6 54.9 %collective-permute-start.7 = (bf16[2,160,2048]{2,1,0:T(8,128)(2,1)}, bf16[2,160,2048]{2,1,0:T(8,128)(2,1)S(1)}, u32[]{:S(2)}, u32[]{:S(2)}) collective-permute-start(bf16[2,160,2048]{2,1,0:T(8,128)(2,1)} %get-tuple-element.59), channel_id=1, source_target_pairs={{2,3},{1,0},{6,7},{5,4},{10,11},{9,8},{14,15},{13,12},{18,19},{17,... | collective-permute-start | bytes 3932168 | tf_op jit(solution)/shard_map/ppermute | solution.py:524
  59.2 20.1 %collective-permute-start.8 = (bf16[160,2048]{1,0:T(8,128)(2,1)S(1)}, bf16[160,2048]{1,0:T(8,128)(2,1)S(1)}, u32[]{:S(2)}, u32[]{:S(2)}) collective-permute-start(bf16[160,2048]{1,0:T(8,128)(2,1)S(1)} %get-tuple-element.61), channel_id=1, source_target_pairs={{1,2},{2,1},{5,6},{6,5},{9,10},{10,9},{13,14},{14,13},{17,18},{18,... | collective-permute-start | bytes 1966088 | tf_op jit(solution)/shard_map/ppermute | solution.py:524
  64.4 0.9 copy-start.4
  65.2 52.0 %collective-permute-start.6 = (bf16[160,2048]{1,0:T(8,128)(2,1)}, bf16[160,2048]{1,0:T(8,128)(2,1)}, u32[]{:S(2)}, u32[]{:S(2)}) collective-permute-start(bf16[160,2048]{1,0:T(8,128)(2,1)} %get-tuple-element.58), channel_id=1, source_target_pairs={{1,3},{2,0},{5,7},{6,4},{9,11},{10,8},{13,15},{14,12},{17,19},{18,... | collective-permute-start | bytes 1966088 | tf_op jit(solution)/shard_map/ppermute | solution.py:524
  79.3 0.9 copy-start.12
  80.2 37.0 %collective-permute-start.9 = (bf16[160,2048]{1,0:T(8,128)(2,1)}, bf16[160,2048]{1,0:T(8,128)(2,1)}, u32[]{:S(2)}, u32[]{:S(2)}) collective-permute-start(bf16[160,2048]{1,0:T(8,128)(2,1)} %get-tuple-element.62), channel_id=1, source_target_pairs={{1,2},{2,1},{5,6},{6,5},{9,10},{10,9},{13,14},{14,13},{17,18},{18,... | collective-permute-start | bytes 1966088 | tf_op jit(solution)/shard_map/ppermute | solution.py:524
  83.9 2.8 %copy-start = (bf16[1,2048,1536]{2,1,0:T(8,128)(2,1)S(1)}, bf16[1,2048,1536]{2,1,0:T(8,128)(2,1)}, u32[]{:S(2)}) copy-start(bf16[1,2048,1536]{2,1,0:T(8,128)(2,1)} %param.11) | copy-start | bytes 18874372
  86.7 1.1 copy-start.9
  87.8 4.6 %copy-start.1 = (bf16[1,768,2048]{2,1,0:T(8,128)(2,1)S(1)}, bf16[1,768,2048]{2,1,0:T(8,128)(2,1)}, u32[]{:S(2)}) copy-start(bf16[1,768,2048]{2,1,0:T(8,128)(2,1)} %param.12) | copy-start | bytes 9437188
  87.8 4.6 %copy-start.7 = (bf16[160,2048]{1,0:T(8,128)(2,1)S(1)}, bf16[160,2048]{1,0:T(8,128)(2,1)}, u32[]{:S(2)}) copy-start(bf16[160,2048]{1,0:T(8,128)(2,1)} %copy-done.6) | copy-start | bytes 1966084
  92.4 20.1 %slice-start = ((s8[6291456]{0:T(1024)(128)(4,1)}), s8[4194304]{0:T(1024)(128)(4,1)S(1)}, s32[]{:S(2)}) async-start(s8[6291456]{0:T(1024)(128)(4,1)} %bitcast.18), calls=%async_computation | async-start | bytes 8388608
  92.4 20.0 %slice-start.1 = ((s8[6291456]{0:T(1024)(128)(4,1)}), s8[2097152]{0:T(1024)(128)(4,1)S(1)}, s32[]{:S(2)}) async-start(s8[6291456]{0:T(1024)(128)(4,1)} %bitcast.18), calls=%async_computation.1 | async-start | bytes 4194304
  92.5 20.0 %copy-start.5 = (bf16[160,2048]{1,0:T(8,128)(2,1)S(1)}, bf16[160,2048]{1,0:T(8,128)(2,1)}, u32[]{:S(2)}) copy-start(bf16[160,2048]{1,0:T(8,128)(2,1)} %copy-done.4) | copy-start | bytes 1966084
  92.5 20.0 %copy-start.11 = (bf16[160,2048]{1,0:T(8,128)(2,1)S(1)}, bf16[160,2048]{1,0:T(8,128)(2,1)}, u32[]{:S(2)}) copy-start(bf16[160,2048]{1,0:T(8,128)(2,1)} %copy-done.10) | copy-start | bytes 1966084
  92.5 20.0 %copy-start.13 = (bf16[160,2048]{1,0:T(8,128)(2,1)S(1)}, bf16[160,2048]{1,0:T(8,128)(2,1)}, u32[]{:S(2)}) copy-start(bf16[160,2048]{1,0:T(8,128)(2,1)} %copy-done.12) | copy-start | bytes 1966084
  97.6 19.5 %copy-start.15 = (bf16[160,2048]{1,0:T(8,128)(2,1)}, bf16[160,2048]{1,0:T(8,128)(2,1)S(1)}, u32[]{:S(2)}) copy-start(bf16[160,2048]{1,0:T(8,128)(2,1)S(1)} %get-tuple-element.54) | copy-start | bytes 1966084
  128.9 8.0 %collective-permute-start.12 = (bf16[4,2304,256]{2,1,0:T(8,128)(2,1)S(1)}, bf16[4,2304,256]{2,1,0:T(8,128)(2,1)S(1)}, u32[]{:S(2)}, u32[]{:S(2)}) collective-permute-start(bf16[4,2304,256]{2,1,0:T(8,128)(2,1)S(1)} %give.2), channel_id=1, source_target_pairs={{0,4},{4,0},{8,12},{12,8},{16,20},{20,16},{24,28},{28,24},{1,5},{5... | collective-permute-start | bytes 14155784 | tf_op jit(solution)/shard_map/ppermute | solution.py:566
  129.0 7.9 %copy-start.14 = (s32[5,4]{1,0:T(8,128)S(1)}, s32[5,4]{1,0:T(8,128)}, u32[]{:S(2)}) copy-start(s32[5,4]{1,0:T(8,128)} %constant.19.clone.plan_ref) | copy-start | bytes 244
  134.1 9.0 %copy-start.16 = (bf16[160,2048]{1,0:T(8,128)(2,1)S(1)}, bf16[160,2048]{1,0:T(8,128)(2,1)}, u32[]{:S(2)}) copy-start(bf16[160,2048]{1,0:T(8,128)(2,1)} %copy-done.15) | copy-start | bytes 1966084
  140.1 28.1 %collective-permute-start.13 = (bf16[2,1152,256]{2,1,0:T(8,128)(2,1)S(1)}, bf16[2,1152,256]{2,1,0:T(8,128)(2,1)S(1)}, u32[]{:S(2)}, u32[]{:S(2)}) collective-permute-start(bf16[2,1152,256]{2,1,0:T(8,128)(2,1)S(1)} %get-tuple-element.79), channel_id=1, source_target_pairs={{0,8},{4,12},{8,0},{12,4},{16,24},{20,28},{24,16},{28,20},{1,9},{5... | collective-permute-start | bytes 3538952 | tf_op jit(solution)/shard_map/ppermute | solution.py:459
  141.7 28.3 %collective-permute-start.14 = (bf16[2,1152,256]{2,1,0:T(8,128)(2,1)S(1)}, bf16[2,1152,256]{2,1,0:T(8,128)(2,1)S(1)}, u32[]{:S(2)}, u32[]{:S(2)}) collective-permute-start(bf16[2,1152,256]{2,1,0:T(8,128)(2,1)S(1)} %get-tuple-element.80), channel_id=1, source_target_pairs={{0,16},{4,20},{8,24},{12,28},{16,0},{20,4},{24,8},{28,12},{1,17},{... | collective-permute-start | bytes 3538952 | tf_op jit(solution)/shard_map/ppermute | solution.py:459
  143.2 29.3 %collective-permute-start.2 = (bf16[160,2048]{1,0:T(8,128)(2,1)S(1)}, bf16[160,2048]{1,0:T(8,128)(2,1)S(1)}, u32[]{:S(2)}, u32[]{:S(2)}) collective-permute-start(bf16[160,2048]{1,0:T(8,128)(2,1)S(1)} %copy-done.16), channel_id=1, source_target_pairs={{0,1},{1,0},{2,3},{3,2},{4,5},{5,4},{6,7},{7,6},{8,9},{9,8},{10,11... | collective-permute-start | bytes 1966088 | tf_op jit(solution)/shard_map/ppermute | solution.py:524
  145.6 44.3 %collective-permute-start.10 = (bf16[160,2048]{1,0:T(8,128)(2,1)S(1)}, bf16[160,2048]{1,0:T(8,128)(2,1)S(1)}, u32[]{:S(2)}, u32[]{:S(2)}) collective-permute-start(bf16[160,2048]{1,0:T(8,128)(2,1)S(1)} %get-tuple-element.71), channel_id=1, source_target_pairs={{0,2},{1,3},{2,0},{3,1},{4,6},{5,7},{6,4},{7,5},{8,10},{9,11},{10,... | collective-permute-start | bytes 1966088 | tf_op jit(solution)/shard_map/ppermute | solution.py:524
  146.6 56.9 %collective-permute-start.11 = (bf16[160,2048]{1,0:T(8,128)(2,1)S(1)}, bf16[160,2048]{1,0:T(8,128)(2,1)S(1)}, u32[]{:S(2)}, u32[]{:S(2)}) collective-permute-start(bf16[160,2048]{1,0:T(8,128)(2,1)S(1)} %get-tuple-element.72), channel_id=1, source_target_pairs={{0,3},{1,2},{2,1},{3,0},{4,7},{5,6},{6,5},{7,4},{8,11},{9,10},{10,... | collective-permute-start | bytes 1966088 | tf_op jit(solution)/shard_map/ppermute | solution.py:524
  168.3 38.4 %collective-permute-start.15 = (bf16[1152,256]{1,0:T(8,128)(2,1)S(1)}, bf16[1152,256]{1,0:T(8,128)(2,1)S(1)}, u32[]{:S(2)}, u32[]{:S(2)}) collective-permute-start(bf16[1152,256]{1,0:T(8,128)(2,1)S(1)} %fusion), channel_id=1, source_target_pairs={{0,16},{4,20},{8,24},{12,28},{16,0},{20,4},{24,8},{28,12},{1,17},{... | collective-permute-start | bytes 1769480 | tf_op jit(solution)/shard_map/ppermute | solution.py:459
  170.1 36.6 %collective-permute-start.16 = (bf16[1152,256]{1,0:T(8,128)(2,1)S(1)}, bf16[1152,256]{1,0:T(8,128)(2,1)S(1)}, u32[]{:S(2)}, u32[]{:S(2)}) collective-permute-start(bf16[1152,256]{1,0:T(8,128)(2,1)S(1)} %fusion.1), channel_id=1, source_target_pairs={{0,8},{4,12},{8,0},{12,4},{16,24},{20,28},{24,16},{28,20},{1,9},{5... | collective-permute-start | bytes 1769480 | tf_op jit(solution)/shard_map/ppermute | solution.py:459

commit v2 on v1

--- a/solution.py
+++ b/solution.py
@@ -17,6 +17,10 @@
     return pltpu.CompilerParams(
         dimension_semantics=("arbitrary",) * grid_rank, vmem_limit_bytes=mebibytes * MIB
     )
+
+
+def cost(macs):
+    return pl.CostEstimate(flops=2 * macs, bytes_accessed=1, transcendentals=0)
 
 
 FREE = pl.CostEstimate(flops=1, bytes_accessed=1, transcendentals=0)
@@ -54,15 +58,30 @@
     return [(place[m : m + 1, :] == slots).astype(F32) for m in offsets]
 
 
-def pack_kernel(offsets, joint, me_ref, meta_ref, tokens_ref, grads_ref, *rest):
-    outs, pick, gain = rest[:-2], rest[-2], rest[-1]
+def pieces_of(ids, gates):
+    lines, rest = [ids.T.astype(BF16)], gates.T
+    for _ in range(3):
+        term = lax.reduce_precision(rest, 8, 7)
+        lines.append(term.astype(BF16))
+        rest = rest - term
+    lines = jnp.concatenate(lines, axis=0)
+    return jnp.pad(lines, ((0, -lines.shape[0] % 16), (0, 0)))
+
+
+def ids_and_gates(meta, top):
+    meta = meta.astype(F32)
+    terms = [meta[top * (1 + i) : top * (2 + i)] for i in range(3)]
+    return meta[:top], (terms[2] + terms[1]) + terms[0]
+
+
+def pack_kernel(offsets, joint, top, kinds, me_ref, meta_ref, *rest):
+    sources, outs, (pick, gain) = rest[: len(kinds)], list(rest[len(kinds) : -2]), rest[-2:]
     capacity = pick.shape[1]
 
     @pl.when(pl.program_id(0) == 0)
     def _():
-        me, meta = me_ref[0], meta_ref[...]
-        top = meta.shape[0] // 2
-        ids, gates = meta[:top], meta[top:]
+        me = me_ref[0]
+        ids, gates = ids_and_gates(meta_ref[...], top)
         for at, matrix in enumerate(pick_matrices(me, ids, offsets, capacity)):
             pick[at] = matrix.astype(BF16)
             chosen = jnp.where(ids == (me ^ offsets[at]).astype(F32), gates, 0.0)
@@ -71,39 +90,39 @@
                 jnp.sum(matrix * weight, axis=1, keepdims=True), gain.shape[1:]
             )
 
-    outs = list(outs)
     for at, m in enumerate(offsets):
-        row = dot(pick[at], tokens_ref[...]).astype(BF16)
-        grad = (dot(pick[at], grads_ref[...]) * gain[at][:, 0:1]).astype(BF16)
-        if m in joint:
-            out = outs.pop(0)
-            out[0], out[1] = row, grad
-        else:
-            outs.pop(0)[...] = row
-            outs.pop(0)[...] = grad
-
-
-def pack(me, meta, tokens, grads, offsets, joint, capacity):
-    rows, width = tokens.shape
+        out = outs.pop(0) if m in joint else None
+        for which, (kind, source) in enumerate(zip(kinds, sources, strict=True)):
+            rows = dot(pick[at], source[...])
+            if kind == "grads":
+                rows = rows * gain[at][:, 0:1]
+            if out is None:
+                outs.pop(0)[...] = rows.astype(BF16)
+            else:
+                out[which] = rows.astype(BF16)
+
+
+def pack(me, meta, sources, offsets, joint, capacity, top):
+    rows, width = next(iter(sources.values())).shape
     block = min(width, 512)
+    count = len(offsets)
     out_specs, out_shape = [], []
     for m in offsets:
         if m in joint:
-            out_specs.append(pl.BlockSpec((2, capacity, block), lambda i: (0, 0, i)))
-            out_shape.append(jax.ShapeDtypeStruct((2, capacity, width), BF16))
+            lead = len(sources)
+            out_specs.append(pl.BlockSpec((lead, capacity, block), lambda i: (0, 0, i)))
+            out_shape.append(jax.ShapeDtypeStruct((lead, capacity, width), BF16))
         else:
-            out_specs += [pl.BlockSpec((capacity, block), lambda i: (0, i))] * 2
-            out_shape += [jax.ShapeDtypeStruct((capacity, width), BF16)] * 2
-    count = len(offsets)
+            out_specs += [pl.BlockSpec((capacity, block), lambda i: (0, i))] * len(sources)
+            out_shape += [jax.ShapeDtypeStruct((capacity, width), BF16)] * len(sources)
     return pl.pallas_call(
-        functools.partial(pack_kernel, offsets, joint),
+        functools.partial(pack_kernel, offsets, joint, top, list(sources)),
         grid=(width // block,),
         in_specs=[
             pl.BlockSpec(memory_space=pltpu.SMEM),
             pl.BlockSpec(meta.shape, lambda i: (0, 0)),
-            pl.BlockSpec((rows, block), lambda i: (0, i)),
-            pl.BlockSpec((rows, block), lambda i: (0, i)),
-        ],
+        ]
+        + [pl.BlockSpec((rows, block), lambda i: (0, i))] * len(sources),
         out_specs=out_specs,
         out_shape=out_shape,
         scratch_shapes=[
@@ -113,16 +132,16 @@
         compiler_params=params(1, 14),
         cost_estimate=FREE,
         name="pack",
-    )(me, meta, tokens, grads)
-
-
-def combine_kernel(group, me_ref, meta_ref, *refs):
+    )(me, meta, *sources.values())
+
+
+def combine_kernel(group, top, me_ref, meta_ref, *refs):
     blocks, out, pick = refs[:group], refs[group], refs[group + 1]
     capacity = blocks[0].shape[0]
 
     @pl.when(pl.program_id(0) == 0)
     def _():
-        ids = meta_ref[...][: meta_ref.shape[0] // 2]
+        ids, _ = ids_and_gates(meta_ref[...], top)
         matrices = pick_matrices(me_ref[0], ids, list(range(group)), capacity)
         for m, matrix in enumerate(matrices):
             pick[m] = matrix.T.astype(BF16)
@@ -133,12 +152,12 @@
     out[...] = total.astype(BF16)
 
 
-def combine(me, meta, blocks):
+def combine(me, meta, blocks, top):
     group, (capacity, width) = len(blocks), blocks[0].shape
     rows = meta.shape[1]
     block = min(width, 512)
     return pl.pallas_call(
-        functools.partial(combine_kernel, group),
+        functools.partial(combine_kernel, group, top),
         grid=(width // block,),
         in_specs=[
             pl.BlockSpec(memory_space=pltpu.SMEM),
@@ -154,8 +173,10 @@
     )(me, meta, *blocks)
 
 
-def padded(rows):
-    return -(-rows // 128) * 128
+def parts_of(capacity, group):
+    own = -(-capacity // 128) * 128
+    others = -(-(group - 1) * capacity // own) * own
+    return own + others, {True: (own, others // own), False: (others, 0)}
 
 
 def gather_rows(parts, sizes, held):
@@ -171,12 +192,9 @@
         held[at:, :] = jnp.zeros((held.shape[0] - at, held.shape[1]), held.dtype)
 
 
-def part_spec(array, capacity, which):
-    width = array.shape[-1]
-    once = pl.Buffered(buffer_count=1)
-    if array.ndim == 2:
-        return pl.BlockSpec((capacity, width), lambda i: (0, 0), pipeline_mode=once)
-    return pl.BlockSpec((None, capacity, width), lambda i: (which, 0, 0), pipeline_mode=once)
+def part_spec(array, capacity):
+    block = (capacity, array.shape[1])
+    return pl.BlockSpec(block, lambda i: (0, 0), pipeline_mode=pl.Buffered(buffer_count=1))
 
 
 def forward_kernel(sizes, *refs):
@@ -199,24 +217,25 @@
     hidden_out[...] = (swish * up).T.astype(BF16)
 
 
-def forward(half, sources, w_pair, before):
+def forward(group, sources, w_pair, before):
     arrays, sizes = sum(sources, []), [len(s) for s in sources]
-    capacity, width = arrays[0].shape[-2:]
+    capacity, width = min(a.shape[0] for a in arrays), arrays[0].shape[1]
     units = w_pair.shape[1] // 2
     tile = math.gcd(units, 256)
     tiles = units // tile
-    rows = padded(len(sources) * capacity)
+    total, parts = parts_of(capacity, group)
+    rows, part = parts[not before]
     shapes = [
         jax.ShapeDtypeStruct((rows, units), BF16),
         jax.ShapeDtypeStruct((rows, units), BF16),
-        jax.ShapeDtypeStruct((units, 2 * rows), BF16),
-        jax.ShapeDtypeStruct((width, 2 * rows), BF16),
+        jax.ShapeDtypeStruct((units, total), BF16),
+        jax.ShapeDtypeStruct((width, total), BF16),
     ]
     first = len(arrays) + 2
     return pl.pallas_call(
         functools.partial(forward_kernel, sizes),
         grid=(tiles,),
-        in_specs=[part_spec(a, capacity, 0) for a in arrays]
+        in_specs=[part_spec(a, capacity) for a in arrays]
         + [
             pl.BlockSpec((width, tile), lambda j: (0, j)),
             pl.BlockSpec((width, tile), lambda j: (0, tiles + j)),
@@ -225,14 +244,14 @@
         out_specs=[
             pl.BlockSpec((rows, tile), lambda j: (0, j)),
             pl.BlockSpec((rows, tile), lambda j: (0, j)),
-            pl.BlockSpec((tile, rows), lambda j: (j, half)),
-            pl.BlockSpec((width, rows), lambda j: (0, half)),
+            pl.BlockSpec((tile, rows), lambda j: (j, part)),
+            pl.BlockSpec((width, rows), lambda j: (0, part)),
         ],
         out_shape=shapes,
         scratch_shapes=[pltpu.VMEM((rows, width), BF16)],
         input_output_aliases={first + i: 2 + i for i in range(len(before))},
         compiler_params=params(1, 20),
-        cost_estimate=FREE,
+        cost_estimate=cost(rows * width * units),
         name="forward",
     )(*arrays, w_pair, w_pair, *before)
 
@@ -269,15 +288,16 @@
             out[...] = back[m * capacity : (m + 1) * capacity, :].astype(BF16)
 
 
-def inner(half, sources, w_down, gate_d, up_d, w_pair, before):
+def inner(group, sources, w_down, gate_d, up_d, w_pair, before):
     arrays, sizes = sum(sources, []), [len(s) for s in sources]
-    capacity, width = arrays[0].shape[-2:]
+    capacity, width = min(a.shape[0] for a in arrays), arrays[0].shape[1]
     units = w_down.shape[0]
     tile = math.gcd(units, 256)
     tiles = units // tile
     block = min(width, 512)
     rows = len(sources) * capacity
-    held = padded(rows)
+    total, parts = parts_of(capacity, group)
+    held, part = parts[not before]
 
     def tile_at(i):
         return jnp.minimum(i, tiles - 1)
@@ -289,7 +309,7 @@
     return pl.pallas_call(
         functools.partial(inner_kernel, sizes, tiles, rows),
         grid=(tiles + width // block,),
-        in_specs=[part_spec(a, capacity, 1) for a in arrays]
+        in_specs=[part_spec(a, capacity) for a in arrays]
         + [
             pl.BlockSpec((tile, width), lambda i: (tile_at(i), 0)),
             pl.BlockSpec((held, tile), lambda i: (0, tile_at(i))),
@@ -299,15 +319,15 @@
         + [pl.BlockSpec(memory_space=pl.ANY) for _ in before],
         out_specs=[pl.BlockSpec((capacity, block), lambda i: (0, block_at(i)))] * outs
         + [
-            pl.BlockSpec((held, width), lambda i: (half, 0)),
-            pl.BlockSpec((held, tile), lambda i: (half, tile_at(i))),
-            pl.BlockSpec((held, tile), lambda i: (half, tile_at(i))),
+            pl.BlockSpec((held, width), lambda i: (part, 0)),
+            pl.BlockSpec((held, tile), lambda i: (part, tile_at(i))),
+            pl.BlockSpec((held, tile), lambda i: (part, tile_at(i))),
         ],
         out_shape=[jax.ShapeDtypeStruct((capacity, width), BF16)] * outs
         + [
-            jax.ShapeDtypeStruct((2 * held, width), BF16),
-            jax.ShapeDtypeStruct((2 * held, units), BF16),
-            jax.ShapeDtypeStruct((2 * held, units), BF16),
+            jax.ShapeDtypeStruct((total, width), BF16),
+            jax.ShapeDtypeStruct((total, units), BF16),
+            jax.ShapeDtypeStruct((total, units), BF16),
         ],
         scratch_shapes=[pltpu.VMEM((rows, 2 * units), BF16)],
         input_output_aliases={first + i: outs + i for i in range(len(before))},
@@ -381,84 +401,47 @@
     )(which, flipped, hidden, grads, gate, up)
 
 
-def split_kernel(kinds, plan_ref, own, came, *outs):
+def split_kernel(shares, own, came, *outs):
     step = pl.program_id(0)
     total = own[0].astype(F32) + came[0].astype(F32)
     half = total.shape[0] // 2
-
-    def emit(first, second):
-        first[0] = total[:half].astype(BF16)
-        second[0] = total[half:].astype(BF16)
-
-    for kind in sorted(set(kinds)):
-        chosen = [step == i for i, other in enumerate(kinds) if other == kind]
-        pl.when(functools.reduce(jnp.logical_or, chosen))(
-            functools.partial(emit, outs[kind[0]], outs[2 + kind[1]])
-        )
-
-
-def without(bits, dropped, r):
-    return sum(((r >> bit) & 1) << at for at, bit in enumerate(b for b in bits if b != dropped))
-
-
-def split(own, came, first_bit, second_bit):
+    for r in range(shares):
+
+        @pl.when(step == r)
+        def _():
+            outs[2 * r][...] = total[:half].astype(BF16)
+            outs[2 * r + 1][...] = total[half:].astype(BF16)
+
+
+def split(own, came):
     shares, share_rows, chunk = came.shape
     half = share_rows // 2
-    bits = range(shares.bit_length() - 1)
-
-    def kind(r):
-        return ((r >> first_bit) & 1, (r >> second_bit) & 1)
-
-    order = sorted(range(shares), key=lambda r: (kind(r), r), reverse=True)
-    plan = [order]
-    for which, bit in ((0, first_bit), (1, second_bit)):
-        for side in (0, 1):
-            places = [without(bits, bit, r) if kind(r)[which] == side else None for r in order]
-            last = next(p for p in places if p is not None)
-            held = []
-            for place in places:
-                last = last if place is None else place
-                held.append(last)
-            plan.append(held)
-    share = pl.BlockSpec((1, share_rows, chunk), lambda i, p: (p[0, i], 0, 0))
-    return pl.pallas_call(
-        functools.partial(split_kernel, [kind(r) for r in order]),
-        grid_spec=pltpu.PrefetchScalarGridSpec(
-            num_scalar_prefetch=1,
-            grid=(shares,),
-            in_specs=[share, share],
-            out_specs=[
-                pl.BlockSpec((1, half, chunk), lambda i, p, n=n: (p[n, i], 0, 0))
-                for n in range(1, 5)
-            ],
-        ),
-        out_shape=[jax.ShapeDtypeStruct((shares // 2, half, chunk), BF16)] * 4,
-        compiler_params=params(1, 14),
+    share = pl.BlockSpec((1, share_rows, chunk), lambda i: (i, 0, 0))
+    halves = pl.pallas_call(
+        functools.partial(split_kernel, shares),
+        grid=(shares,),
+        in_specs=[share, share],
+        out_specs=[pl.BlockSpec((half, chunk), lambda i: (0, 0))] * (2 * shares),
+        out_shape=[jax.ShapeDtypeStruct((half, chunk), BF16)] * (2 * shares),
+        compiler_params=params(1, 18),
         cost_estimate=FREE,
         name="split",
-    )(jnp.asarray(plan, jnp.int32), own, came)
-
-
-def halvings(kept, sent, bits):
-    present = sorted(bits, reverse=True)
-    rest = [bit for bit in present if bit != bits[0]]
-    tail = kept.shape[1:]
-    terms = [(kept.reshape((2,) * len(rest) + tail), rest)]
-    done = set()
+    )(own, came)
+    return halves[::2], halves[1::2]
+
+
+def halvings(shares, bits, before_last):
+    terms = {r: [share] for r, share in enumerate(shares)}
     for bit in bits:
-        if bit == bits[0]:
-            give, left = sent.reshape((2,) * len(rest) + tail), rest
-        else:
-            left = [other for other in present if other not in done and other != bit]
-            parts = []
-            for array, axes in terms:
-                index = tuple(1 if b == bit else 0 if b in done else slice(None) for b in axes)
-                parts.append(array[index].astype(F32))
-            give = sum(parts).astype(BF16)
         pairs = [(i, i ^ (2 << bit)) for i in range(lax.axis_size("dp"))]
-        terms.append((lax.ppermute(give, "dp", pairs), left))
-        done.add(bit)
-    return [array for array, _ in terms]
+        for r in sorted((r for r in terms if (r >> bit) & 1), reverse=True):
+            mine = terms.pop(r)
+            if len(mine) > 1:
+                mine = [sum(term.astype(F32) for term in mine).astype(BF16)]
+            if bit == bits[-1]:
+                mine = lax.optimization_barrier((mine[0], before_last))
+            terms[r ^ (1 << bit)].append(lax.ppermute(mine[0], "dp", pairs))
+    return terms[0]
 
 
 def finish_kernel(count, chunk, *refs):
@@ -483,16 +466,11 @@
 
 
 def finish(firsts, seconds, pair_shape, lower_shape):
-    half, chunk = firsts[0].shape[-2:]
-
-    def leading(array):
-        lead = array.ndim - 2
-        return pl.BlockSpec((None,) * lead + (half, chunk), lambda i, n=lead: (0,) * (n + 2))
-
+    chunk = firsts[0].shape[1]
     return pl.pallas_call(
         functools.partial(finish_kernel, len(firsts), chunk),
         grid=(1,),
-        in_specs=[leading(a) for a in firsts + seconds],
+        in_specs=[pl.BlockSpec(a.shape, lambda i: (0, 0)) for a in firsts + seconds],
         out_specs=[
             pl.BlockSpec(pair_shape, lambda i: (0, 0)),
             pl.BlockSpec(lower_shape, lambda i: (0, 0)),
@@ -502,6 +480,7 @@
             jax.ShapeDtypeStruct(lower_shape, F32),
         ],
         compiler_params=params(1, 24),
+        cost_estimate=FREE,
         name="finish",
     )(*firsts, *seconds)
 
@@ -517,7 +496,7 @@
     me = lax.axis_index("expert").astype(jnp.int32)
     replica = lax.axis_index("dp").astype(jnp.int32)
     place = me.reshape(1)
-    meta = jnp.concatenate([expert_ids.astype(F32), gate_weights], axis=1).T
+    meta = pieces_of(expert_ids, gate_weights)
     w_pair, w_lower = w_gate_up[0], w_down[0]
 
     def move(array, pairs):
@@ -530,52 +509,55 @@
         return lax.optimization_barrier((array, *others))[0]
 
     if group == 4 and tok_rows < 2 * capacity:
-        far = [(0, 2), (3, 1)]
-        far_meta, far_rows, far_grads = move(meta, far), move(tokens_in, far), move(out_grad, far)
-        x0, g0, pair1, x2, g2, x3, g3 = pack(
-            place, meta, tokens_in, out_grad, [0, 1, 2, 3], [1], capacity
+        far, near, cross = [(0, 2), (3, 1)], [(1, 2), (2, 1)], [(1, 3), (2, 0)]
+        far_meta = move(meta, far)
+        far_rows = move(after(tokens_in, far_meta), far)
+        x0, g0, x1, g1, x2, g2, x3, g3 = pack(
+            place, meta, dict(tokens=tokens_in, grads=out_grad), [0, 1, 2, 3], [], capacity, top
         )
-        pair1 = swap(after(pair1, far_rows), 1)
-        cx, cg, onward = pack(place, far_meta, far_rows, far_grads, [0, 1], [1], capacity)
+        x1, x3, x2 = swap(x1, 1), move(x3, near), move(x2, cross)
+        cx, onward = pack(place, far_meta, dict(tokens=far_rows), [0, 1], [], capacity + 16, top)
         onward = move(onward, [(2, 3), (1, 0)])
-        x3 = move(x3, [(1, 2), (2, 1)])
-        x2 = move(x2, [(1, 3), (2, 0)])
-        g3 = move(after(g3, x3), [(1, 2), (2, 1)])
-        g2 = move(after(g2, x2), [(1, 3), (2, 0)])
-        inputs = [[x0], [pair1], [cx, x2], [onward, x3]]
-        grads = [[g0], [pair1], [cg, g2], [onward, g3]]
+        g1 = swap(after(g1, x1), 1)
+        g2 = swap(after(g2, x3), 2)
+        g3 = swap(after(g3, x2), 3)
+        inputs, grads = [[x0], [x1], [cx, x2], [onward, x3]], [[g0], [g1], [g2], [g3]]
     else:
         offsets = list(range(group))
-        packed = pack(place, meta, tokens_in, out_grad, offsets, [], capacity)
+        packed = pack(
+            place, meta, dict(tokens=tokens_in, grads=out_grad), offsets, [], capacity, top
+        )
         moved = [packed[2 * m : 2 * m + 2] for m in offsets]
         moved = [moved[0]] + [[swap(a, m) for a in moved[m]] for m in offsets[1:]]
         inputs, grads = [[a] for a, _ in moved], [[b] for _, b in moved]
 
-    lead = group // 2
-    early_d = forward(0, inputs[:lead], w_pair, [])
-    late_d = forward(1, inputs[lead:], w_pair, early_d[2:])
-    early = inner(0, grads[:lead], w_lower, *early_d[:2], w_pair, [])
-    late = inner(1, grads[lead:], w_lower, *late_d[:2], w_pair, early[lead:])
-    blocks = list(early[:lead]) + list(late[:lead])
-    returned = [blocks[0]] + [swap(blocks[m], m) for m in range(1, group)]
+    own_d = forward(group, inputs[:1], w_pair, [])
+    others_d = forward(group, inputs[1:], w_pair, own_d[2:])
+    own_back, *own_grads = inner(group, grads[:1], w_lower, *own_d[:2], w_pair, [])
+    late = inner(group, grads[1:], w_lower, *others_d[:2], w_pair, own_grads)
+    returned = [own_back, *late[: group - 1]]
+    for m in range(group - 1, 0, -1):
+        ahead = returned[m + 1 :] if 2 * m >= group else []
+        returned[m] = swap(after(returned[m], *ahead), m)
 
     shares = replicas // 2
     own = [replica ^ (2 * r) for r in range(shares)]
-    operands = (late_d[3], late_d[2], *late[lead:])
-    given = give(jnp.stack(own) ^ 1, *operands, replicas, chunk)
+    operands = (others_d[3], others_d[2], *late[group - 1 :])
+    first_own = jnp.stack(own) ^ 1
+    given = give(first_own, *operands, replicas, chunk)
     came = lax.ppermute(given, "dp", [(i, i ^ 1) for i in range(replicas)])
     mine = give(after(jnp.stack(own), given), *operands, replicas, chunk)
     bits = list(range(shares.bit_length() - 1))
     middle = len(bits) // 2
     first_bits, second_bits = bits, bits[middle:] + bits[:middle]
-    kept_a, sent_a, kept_b, sent_b = split(mine, came, first_bits[0], second_bits[0])
-    firsts = halvings(kept_a, sent_a, first_bits)
-    seconds = halvings(kept_b, sent_b, second_bits)
-    *returned, firsts[1], seconds[1] = lax.optimization_barrier((*returned, firsts[1], seconds[1]))
-    grad_tokens = combine(place, meta, returned)
+    first, second = split(mine, came)
+    firsts = halvings(first, first_bits, returned[-1])
+    seconds = halvings(second, second_bits, returned[-1])
     pair_sum, lower_sum = finish(
         firsts, seconds, (width // replicas, 2 * units), (units // replicas, width)
     )
+    *returned, pair_sum, lower_sum = lax.optimization_barrier((*returned, pair_sum, lower_sum))
+    grad_tokens = combine(place, meta, returned, top)
     return (grad_tokens, pair_sum, lower_sum)
 
 

time: 209 us -> 197 us (0.943)
  the two profiles are of different devices: /device:TPU:8 before, /device:TPU:0 now
where the time goes in v2:
time: 197 us; the launch traced here: 196 us
  waiting for transfers between devices  68.4 us (35%)
  starting transfers between devices  51 us (26%)
  Pallas kernels  47.6 us (24%)
  local copies, waits for them, and re-layouts  26.2 us (13%)
    ppermute x12, waiting for transfers between devices, move(): return lax.ppermute(array, 'expert', pairs)  44.3 us
    ppermute x12, starting transfers between devices, move(): return lax.ppermute(array, 'expert', pairs)  42.8 us
    unnamed x52, local copies, waits for them, and re-layouts  26.2 us
    ppermute x6, waiting for transfers between devices, halvings(): terms[r ^ 1 << bit].append(lax.ppermute(mine[0], 'dp', pairs))  23.8 us
    pallas_call x2, Pallas kernels, inner(): pl.pallas_call(functools.partial(inner_kernel, sizes, tiles, rows), grid=...  13.3 us
    pallas_call x2, Pallas kernels, forward(): pl.pallas_call(functools.partial(forward_kernel, sizes), grid=(tiles,), i...  10.3 us
    pallas_call x2, Pallas kernels, give(): pl.pallas_call(functools.partial(give_kernel, shares, chunk), grid_spec=p...  10.2 us
    ppermute x6, starting transfers between devices, halvings(): terms[r ^ 1 << bit].append(lax.ppermute(mine[0], 'dp', pairs))  8.15 us
  transfers between devices with their start and end apart: 19, of which 10 were waited for; matrix products, arithmetic and copies ran while one was open for 0% of the time, Pallas kernels for 16%

profile of v2, /device:TPU:0, one launch (start us, length us, event | category | flops | bytes accessed | tf_op | source)
XLA Modules:
  0.0 195.9 jit_solution(10537669474635888128)
XLA Ops:
  2.0 5.9 %collective-permute-start.6 = (bf16[16,256]{1,0:T(8,128)(2,1)S(1)}, bf16[16,256]{1,0:T(8,128)(2,1)S(1)}, u32[]{:S(2)}, u32[]{:S(2)}) collective-permute-start(bf16[16,256]{1,0:T(8,128)(2,1)S(1)} %fusion.6.meta_ref), channel_id=1, source_target_pairs={{0,2},{3,1},{4,6},{7,5},{8,10},{11,9},{12,14},{15,13},{16,18},{19,... | collective-permute-start | bytes 24584 | tf_op jit(solution)/shard_map/ppermute | solution.py:503
  8.0 1.3 collective-permute-done.6.meta_ref
  9.3 5.1 %collective-permute-start.7 = (bf16[256,2048]{1,0:T(8,128)(2,1)}, bf16[256,2048]{1,0:T(8,128)(2,1)S(1)}, u32[]{:S(2)}, u32[]{:S(2)}) collective-permute-start(bf16[256,2048]{1,0:T(8,128)(2,1)} %rest_0_.1), channel_id=1, source_target_pairs={{0,2},{3,1},{4,6},{7,5},{8,10},{11,9},{12,14},{15,13},{16,18},{19,... | collective-permute-start | bytes 3145736 | tf_op jit(solution)/shard_map/ppermute | solution.py:503
  14.5 1.2 copy-done.14
  15.7 1.2 copy-done.15
  16.9 3.9 %pack.2 = (bf16[160,2048]{1,0:T(8,128)(2,1)S(1)}, bf16[160,2048]{1,0:T(8,128)(2,1)S(1)}, bf16[160,2048]{1,0:T(8,128)(2,1)S(1)}, bf16[160,2048]{1,0:T(8,128)(2,1)...) custom-call(s32[1]{0:T(128)} %bitcast.me_ref, ...), custom_call_target="tpu_custom_call" | custom-call | flops 1 | bytes 1 | tf_op jit(solution)/shard_map/pack/pallas_call | solution.py:118
  21.5 1.3 collective-permute-start.4
  22.8 15.5 %collective-permute-done.7.rest_0_ = bf16[256,2048]{1,0:T(8,128)(2,1)S(1)} collective-permute-done((bf16[256,2048]{1,0:T(8,128)(2,1)}, bf16[256,2048]{1,0:T(8,128)(2,1)S(1)}, u32[]{:S(2)}, u32[]{:S(2)}) %collective-permute-start.7) | collective-permute-done | bytes 1048608 | tf_op jit(solution)/shard_map/ppermute | solution.py:503
  38.4 2.4 %pack.3 = (bf16[176,2048]{1,0:T(8,128)(2,1)S(1)}, bf16[176,2048]{1,0:T(8,128)(2,1)}) custom-call(s32[1]{0:T(128)} %bitcast.me_ref, bf16[16,256]{1,0:T(8,128)(2,1)S(1)} %collective-permute-done.6.meta_ref, bf16[256,2048]{1,0:T(8,128)(2,1)S(1)} %collective-permute-done.7.rest_0_), custom_call_target="tpu_custom_call" | custom-call | flops 1 | bytes 1 | tf_op jit(solution)/shard_map/pack/pallas_call | solution.py:118
  41.6 1.3 collective-permute-start.8
  42.9 7.0 %collective-permute-done.refs_0_ = bf16[160,2048]{1,0:T(8,128)(2,1)S(1)} collective-permute-done((bf16[160,2048]{1,0:T(8,128)(2,1)S(1)}, bf16[160,2048]{1,0:T(8,128)(2,1)S(1)}, u32[]{:S(2)}, u32[]{:S(2)}) %collective-permute-start) | collective-permute-done | bytes 655392 | tf_op jit(solution)/shard_map/ppermute | solution.py:503
  50.8 2.5 %collective-permute-start.1 = (bf16[160,2048]{1,0:T(8,128)(2,1)}, bf16[160,2048]{1,0:T(8,128)(2,1)}, u32[]{:S(2)}, u32[]{:S(2)}) collective-permute-start(bf16[160,2048]{1,0:T(8,128)(2,1)} %get-tuple-element.62), channel_id=1, source_target_pairs={{0,1},{1,0},{2,3},{3,2},{4,5},{5,4},{6,7},{7,6},{8,9},{9,8},{10,11... | collective-permute-start | bytes 1966088 | tf_op jit(solution)/shard_map/ppermute | solution.py:503
  54.2 13.6 %collective-permute-done.4.refs_2_ = bf16[160,2048]{1,0:T(8,128)(2,1)S(1)} collective-permute-done((bf16[160,2048]{1,0:T(8,128)(2,1)S(1)}, bf16[160,2048]{1,0:T(8,128)(2,1)S(1)}, u32[]{:S(2)}, u32[]{:S(2)}) %collective-permute-start.4) | collective-permute-done | bytes 655392 | tf_op jit(solution)/shard_map/ppermute | solution.py:503
  68.8 2.5 %collective-permute-start.5 = (bf16[160,2048]{1,0:T(8,128)(2,1)}, bf16[160,2048]{1,0:T(8,128)(2,1)}, u32[]{:S(2)}, u32[]{:S(2)}) collective-permute-start(bf16[160,2048]{1,0:T(8,128)(2,1)} %get-tuple-element.68), channel_id=1, source_target_pairs={{0,3},{1,2},{2,1},{3,0},{4,7},{5,6},{6,5},{7,4},{8,11},{9,10},{10,... | collective-permute-start | bytes 1966088 | tf_op jit(solution)/shard_map/ppermute | solution.py:503
  71.2 2.8 %copy-done = bf16[1,2048,1536]{2,1,0:T(8,128)(2,1)S(1)} copy-done((bf16[1,2048,1536]{2,1,0:T(8,128)(2,1)S(1)}, bf16[1,2048,1536]{2,1,0:T(8,128)(2,1)}, u32[]{:S(2)}) %copy-start) | copy-done | bytes 6291480
  74.0 3.4 %forward.2 = (bf16[256,768]{1,0:T(8,128)(2,1)S(1)}, bf16[256,768]{1,0:T(8,128)(2,1)S(1)}, bf16[768,768]{1,0:T(8,128)(2,1)S(1)}, bf16[2048,768]{1,0:T(8,128)(2,1)S(1)}) custom-call(bf16[160,2048]{1,0:T(8,128)(2,1)S(1)} %get-tuple-element.56.refs_0_, bf16[2048,1536]{1,0:T(8,128)(2,1)S(1)} %bitcast.18, bf16[2048,1536]{1,0:T(8,128)(2,1)S(1)} %bitcast.19), custom_call_target="tpu_custom_call" | custom-call | flops 805306368 | bytes 1 | tf_op jit(solution)/shard_map/forward/pallas_call | solution.py:235
  77.5 1.6 copy-done.2
  79.1 1.0 copy-done.12
  80.1 4.7 %inner.2 = (bf16[160,2048]{1,0:T(8,128)(2,1)S(1)}, bf16[768,2048]{1,0:T(8,128)(2,1)S(1)}, bf16[768,768]{1,0:T(8,128)(2,1)S(1)}, bf16[768,768]{1,0:T(8,128)(2,1)S(1)}) custom-call(bf16[160,2048]{1,0:T(8,128)(2,1)S(1)} %get-tuple-element.55.refs_0_, bf16[768,2048]{1,0:T(8,128)(2,1)S(1)} %bitcast.26, bf16[256,768]{1,0:T(8,128)(2,1)S(1)} %get-tuple-element.57.refs_2_, ...), custom_call_target="tpu_custom_call" | custom-call | flops 1 | bytes 1 | tf_op jit(solution)/shard_map/inner/pallas_call | solution.py:309
  84.8 1.0 copy-done.8
  85.8 1.0 copy-done.10
  87.8 2.8 %copy-done.1 = bf16[1,2048,1536]{2,1,0:T(8,128)(2,1)S(1)} copy-done((bf16[1,2048,1536]{2,1,0:T(8,128)(2,1)S(1)}, bf16[1,2048,1536]{2,1,0:T(8,128)(2,1)}, u32[]{:S(2)}) %copy-start.1) | copy-done | bytes 6291480
  90.6 1.9 copy-done.3
  92.5 1.3 copy-done.13
  93.8 1.1 copy-done.17
  94.9 1.1 copy-done.19
  96.0 1.1 copy-done.21
  97.0 1.1 copy-done.23
  98.1 6.9 %forward.3 = (bf16[512,768]{1,0:T(8,128)(2,1)S(1)}, bf16[512,768]{1,0:T(8,128)(2,1)S(1)}, bf16[768,768]{1,0:T(8,128)(2,1)S(1)}, bf16[2048,768]{1,0:T(8,128)(2,1)S(1)}) custom-call(bf16[160,2048]{1,0:T(8,128)(2,1)S(1)} %copy-done.19, bf16[176,2048]{1,0:T(8,128)(2,1)S(1)} %copy-done.17, ...), custom_call_target="tpu_custom_call", output_to_operand_aliasing={{2}: (7, {}), {3}: (8, {})} | custom-call | flops 1610612736 | bytes 1 | tf_op jit(solution)/shard_map/forward/pallas_call | solution.py:235
  105.1 1.6 copy-done.4
  106.7 6.8 %collective-permute-done.1.refs_0_ = bf16[160,2048]{1,0:T(8,128)(2,1)} collective-permute-done((bf16[160,2048]{1,0:T(8,128)(2,1)}, bf16[160,2048]{1,0:T(8,128)(2,1)}, u32[]{:S(2)}, u32[]{:S(2)}) %collective-permute-start.1) | collective-permute-done | bytes 655392 | tf_op jit(solution)/shard_map/ppermute | solution.py:503
  113.5 8.6 %inner.3 = (bf16[160,2048]{1,0:T(8,128)(2,1)S(1)}, bf16[160,2048]{1,0:T(8,128)(2,1)S(1)}, bf16[160,2048]{1,0:T(8,128)(2,1)S(1)}, bf16[768,2048]{1,0:T(8,128)(2,1...) custom-call(bf16[160,2048]{1,0:T(8,128)(2,1)} %collective-permute-do, ...), custom_call_target="tpu_custom_call", output_to_operand_aliasing={{3}: (7, {}), {4}: (8, {}), {5}: (9, {})} | custom-call | flops 1 | bytes 1 | tf_op jit(solution)/shard_map/inner/pallas_call | solution.py:309
  122.1 5.1 %give.2 = bf16[4,2304,256]{2,1,0:T(8,128)(2,1)S(1)} custom-call(s32[4]{0:T(128)S(1)} %get-tuple-element.107.which_ref, bf16[8,256,768]{2,1,0:T(8,128)(2,1)S(1)} %bitcast.24, bf16[8,96,768]{2,1,0:T(8,128)(2,1)S(1)} %bitcast.28, bf16[768,2048]{1,0:T(8,128)(2,1)S(1)} %get-tuple-element.85.grads, bf16[768,768]{1,0:T(8,128)(2,1)S(1)} %get-tuple-element.86.gate, ...), custom_call_target="tpu_custom_call" | custom-call | flops 1 | bytes 1 | tf_op jit(solution)/shard_map/give/pallas_call | solution.py:387
  127.3 2.4 %collective-permute-start.10 = (bf16[160,2048]{1,0:T(8,128)(2,1)S(1)}, bf16[160,2048]{1,0:T(8,128)(2,1)S(1)}, u32[]{:S(2)}, u32[]{:S(2)}) collective-permute-start(bf16[160,2048]{1,0:T(8,128)(2,1)S(1)} %get-tuple-element.81), channel_id=1, source_target_pairs={{0,3},{1,2},{2,1},{3,0},{4,7},{5,6},{6,5},{7,4},{8,11},{9,10},{10,... | collective-permute-start | bytes 1966088 | tf_op jit(solution)/shard_map/ppermute | solution.py:503
  129.8 5.1 %give.3.own = bf16[4,2304,256]{2,1,0:T(8,128)(2,1)S(1)} custom-call(s32[4]{0:T(128)S(1)} %get-tuple-element.88.which_ref, bf16[8,256,768]{2,1,0:T(8,128)(2,1)S(1)} %bitcast.25, bf16[8,96,768]{2,1,0:T(8,128)(2,1)S(1)} %bitcast.29, bf16[768,2048]{1,0:T(8,128)(2,1)S(1)} %get-tuple-element.85.grads, bf16[768,768]{1,0:T(8,128)(2,1)S(1)} %get-tuple-element.86.gate, ...), custom_call_target="tpu_custom_call" | custom-call | flops 1 | bytes 1 | tf_op jit(solution)/shard_map/give/pallas_call | solution.py:387
  135.2 2.6 %split.1 = (bf16[1152,256]{1,0:T(8,128)(2,1)S(1)}, bf16[1152,256]{1,0:T(8,128)(2,1)S(1)}, bf16[1152,256]{1,0:T(8,128)(2,1)S(1)}, bf16[1152,256]{1,0:T(8,128)(2,1...) custom-call(bf16[4,2304,256]{2,1,0:T(8,128)(2,1)S(1)} %give.3.own, ...), custom_call_target="tpu_custom_call" | custom-call | flops 1 | bytes 1 | tf_op jit(solution)/shard_map/split/pallas_call | solution.py:420
  137.8 1.6 collective-permute-start.14
  139.4 1.5 collective-permute-start.17
  140.9 9.2 %collective-permute-start.9 = (bf16[160,2048]{1,0:T(8,128)(2,1)S(1)}, bf16[160,2048]{1,0:T(8,128)(2,1)S(1)}, u32[]{:S(2)}, u32[]{:S(2)}) collective-permute-start(bf16[160,2048]{1,0:T(8,128)(2,1)S(1)} %get-tuple-element.79), channel_id=1, source_target_pairs={{0,1},{1,0},{2,3},{3,2},{4,5},{5,4},{6,7},{7,6},{8,9},{9,8},{10,11... | collective-permute-start | bytes 1966088 | tf_op jit(solution)/shard_map/ppermute | solution.py:503
  150.1 11.7 %collective-permute-start.11 = (bf16[160,2048]{1,0:T(8,128)(2,1)S(1)}, bf16[160,2048]{1,0:T(8,128)(2,1)S(1)}, u32[]{:S(2)}, u32[]{:S(2)}) collective-permute-start(bf16[160,2048]{1,0:T(8,128)(2,1)S(1)} %get-tuple-element.82), channel_id=1, source_target_pairs={{0,2},{1,3},{2,0},{3,1},{4,6},{5,7},{6,4},{7,5},{8,10},{9,11},{10,... | collective-permute-start | bytes 1966088 | tf_op jit(solution)/shard_map/ppermute | solution.py:503
  161.8 1.5 collective-permute-start.13
  163.3 1.5 collective-permute-start.16
  165.7 11.1 %collective-permute-done.13.refs_1_ = bf16[1152,256]{1,0:T(8,128)(2,1)S(1)} collective-permute-done((bf16[1152,256]{1,0:T(8,128)(2,1)S(1)}, bf16[1152,256]{1,0:T(8,128)(2,1)S(1)}, u32[]{:S(2)}, u32[]{:S(2)}) %collective-permute-start.13) | collective-permute-done | bytes 589856 | tf_op jit(solution)/shard_map/ppermute | solution.py:443
  176.8 1.5 collective-permute-start.18
  178.3 1.2 collective-permute-done.16.refs_4_
  179.6 11.1 %collective-permute-done.15.refs_2_ = bf16[1152,256]{1,0:T(8,128)(2,1)S(1)} collective-permute-done((bf16[1152,256]{1,0:T(8,128)(2,1)S(1)}, bf16[1152,256]{1,0:T(8,128)(2,1)S(1)}, u32[]{:S(2)}, u32[]{:S(2)}) %collective-permute-start.15) | collective-permute-done | bytes 589856 | tf_op jit(solution)/shard_map/ppermute | solution.py:443
  191.0 1.7 finish.1
  192.6 3.2 %combine.1 = bf16[256,2048]{1,0:T(8,128)(2,1)} custom-call(s32[1]{0:T(128)} %bitcast.me_ref, bf16[16,256]{1,0:T(8,128)(2,1)S(1)} %fusion.6.meta_ref, bf16[160,2048]{1,0:T(8,128)(2,1)S(1)} %copy-done.25, bf16[160,2048]{1,0:T(8,128)(2,1)S(1)} %collective-permute-done.9.refs_1_, bf16[160,2048]{1,0:T(8,128)(2,1)S(1)} %collective-permute-done.11.refs_2_, ...), custom_call_target="tpu_custom_call" | custom-call | flops 1 | bytes 1 | tf_op jit(solution)/shard_map/combine/pallas_call | solution.py:159
  (59 shorter events, 8.2 us)
Async XLA Ops:
  2.0 7.3 %collective-permute-start.6 = (bf16[16,256]{1,0:T(8,128)(2,1)S(1)}, bf16[16,256]{1,0:T(8,128)(2,1)S(1)}, u32[]{:S(2)}, u32[]{:S(2)}) collective-permute-start(bf16[16,256]{1,0:T(8,128)(2,1)S(1)} %fusion.6.meta_ref), channel_id=1, source_target_pairs={{0,2},{3,1},{4,6},{7,5},{8,10},{11,9},{12,14},{15,13},{16,18},{19,... | collective-permute-start | bytes 24584 | tf_op jit(solution)/shard_map/ppermute | solution.py:503
  9.3 29.0 %collective-permute-start.7 = (bf16[256,2048]{1,0:T(8,128)(2,1)}, bf16[256,2048]{1,0:T(8,128)(2,1)S(1)}, u32[]{:S(2)}, u32[]{:S(2)}) collective-permute-start(bf16[256,2048]{1,0:T(8,128)(2,1)} %rest_0_.1), channel_id=1, source_target_pairs={{0,2},{3,1},{4,6},{7,5},{8,10},{11,9},{12,14},{15,13},{16,18},{19,... | collective-permute-start | bytes 3145736 | tf_op jit(solution)/shard_map/ppermute | solution.py:503
  14.5 1.2 copy-start.14
  15.7 1.2 copy-start.15
  20.8 29.1 %collective-permute-start = (bf16[160,2048]{1,0:T(8,128)(2,1)S(1)}, bf16[160,2048]{1,0:T(8,128)(2,1)S(1)}, u32[]{:S(2)}, u32[]{:S(2)}) collective-permute-start(bf16[160,2048]{1,0:T(8,128)(2,1)S(1)} %get-tuple-element.61), channel_id=1, source_target_pairs={{0,1},{1,0},{2,3},{3,2},{4,5},{5,4},{6,7},{7,6},{8,9},{9,8},{10,11... | collective-permute-start | bytes 1966088 | tf_op jit(solution)/shard_map/ppermute | solution.py:503
  20.8 32.4 %collective-permute-start.2 = (bf16[160,2048]{1,0:T(8,128)(2,1)S(1)}, bf16[160,2048]{1,0:T(8,128)(2,1)S(1)}, u32[]{:S(2)}, u32[]{:S(2)}) collective-permute-start(bf16[160,2048]{1,0:T(8,128)(2,1)S(1)} %get-tuple-element.64), channel_id=1, source_target_pairs={{1,2},{2,1},{5,6},{6,5},{9,10},{10,9},{13,14},{14,13},{17,18},{18,... | collective-permute-start | bytes 1966088 | tf_op jit(solution)/shard_map/ppermute | solution.py:503
  21.5 46.3 %collective-permute-start.4 = (bf16[160,2048]{1,0:T(8,128)(2,1)S(1)}, bf16[160,2048]{1,0:T(8,128)(2,1)S(1)}, u32[]{:S(2)}, u32[]{:S(2)}) collective-permute-start(bf16[160,2048]{1,0:T(8,128)(2,1)S(1)} %get-tuple-element.67), channel_id=1, source_target_pairs={{1,3},{2,0},{5,7},{6,4},{9,11},{10,8},{13,15},{14,12},{17,19},{18,... | collective-permute-start | bytes 1966088 | tf_op jit(solution)/shard_map/ppermute | solution.py:503
  40.8 0.9 copy-start.16
  41.6 46.2 %collective-permute-start.8 = (bf16[176,2048]{1,0:T(8,128)(2,1)}, bf16[176,2048]{1,0:T(8,128)(2,1)}, u32[]{:S(2)}, u32[]{:S(2)}) collective-permute-start(bf16[176,2048]{1,0:T(8,128)(2,1)} %get-tuple-element.71), channel_id=1, source_target_pairs={{2,3},{1,0},{6,7},{5,4},{10,11},{9,8},{14,15},{13,12},{18,19},{17,... | collective-permute-start | bytes 2162696 | tf_op jit(solution)/shard_map/ppermute | solution.py:503
  49.9 0.8 copy-start.18
  50.8 62.7 %collective-permute-start.1 = (bf16[160,2048]{1,0:T(8,128)(2,1)}, bf16[160,2048]{1,0:T(8,128)(2,1)}, u32[]{:S(2)}, u32[]{:S(2)}) collective-permute-start(bf16[160,2048]{1,0:T(8,128)(2,1)} %get-tuple-element.62), channel_id=1, source_target_pairs={{0,1},{1,0},{2,3},{3,2},{4,5},{5,4},{6,7},{7,6},{8,9},{9,8},{10,11... | collective-permute-start | bytes 1966088 | tf_op jit(solution)/shard_map/ppermute | solution.py:503
  53.3 0.8 copy-start.20
  54.1 59.3 %collective-permute-start.3 = (bf16[160,2048]{1,0:T(8,128)(2,1)}, bf16[160,2048]{1,0:T(8,128)(2,1)}, u32[]{:S(2)}, u32[]{:S(2)}) collective-permute-start(bf16[160,2048]{1,0:T(8,128)(2,1)} %get-tuple-element.65), channel_id=1, source_target_pairs={{0,2},{1,3},{2,0},{3,1},{4,6},{5,7},{6,4},{7,5},{8,10},{9,11},{10,... | collective-permute-start | bytes 1966088 | tf_op jit(solution)/shard_map/ppermute | solution.py:503
  67.9 0.9 copy-start.22
  68.8 44.7 %collective-permute-start.5 = (bf16[160,2048]{1,0:T(8,128)(2,1)}, bf16[160,2048]{1,0:T(8,128)(2,1)}, u32[]{:S(2)}, u32[]{:S(2)}) collective-permute-start(bf16[160,2048]{1,0:T(8,128)(2,1)} %get-tuple-element.68), channel_id=1, source_target_pairs={{0,3},{1,2},{2,1},{3,0},{4,7},{5,6},{6,5},{7,4},{8,11},{9,10},{10,... | collective-permute-start | bytes 1966088 | tf_op jit(solution)/shard_map/ppermute | solution.py:503
  71.2 2.8 %copy-start = (bf16[1,2048,1536]{2,1,0:T(8,128)(2,1)S(1)}, bf16[1,2048,1536]{2,1,0:T(8,128)(2,1)}, u32[]{:S(2)}) copy-start(bf16[1,2048,1536]{2,1,0:T(8,128)(2,1)} %param.10) | copy-start | bytes 18874372
  74.0 6.1 %copy-start.6 = (bf16[1,768,2048]{2,1,0:T(8,128)(2,1)S(1)}, bf16[1,768,2048]{2,1,0:T(8,128)(2,1)}, u32[]{:S(2)}) copy-start(bf16[1,768,2048]{2,1,0:T(8,128)(2,1)} %param.11) | copy-start | bytes 9437188
  77.5 1.6 copy-start.2
  79.1 1.0 copy-start.12
  84.8 1.0 copy-start.8
  85.8 1.0 copy-start.10
  86.9 0.9 copy-start.24
  87.8 2.8 %copy-start.1 = (bf16[1,2048,1536]{2,1,0:T(8,128)(2,1)S(1)}, bf16[1,2048,1536]{2,1,0:T(8,128)(2,1)}, u32[]{:S(2)}) copy-start(bf16[1,2048,1536]{2,1,0:T(8,128)(2,1)} %param.10) | copy-start | bytes 18874372
  90.6 1.9 copy-start.3
  92.5 1.3 copy-start.13
  93.8 1.1 copy-start.17
  94.9 1.1 copy-start.19
  96.0 1.1 copy-start.21
  97.0 1.1 copy-start.23
  98.1 15.3 %copy-start.7 = (bf16[1,768,2048]{2,1,0:T(8,128)(2,1)S(1)}, bf16[1,768,2048]{2,1,0:T(8,128)(2,1)}, u32[]{:S(2)}) copy-start(bf16[1,768,2048]{2,1,0:T(8,128)(2,1)} %param.11) | copy-start | bytes 9437188
  98.1 15.3 %copy-start.9 = (bf16[768,768]{1,0:T(8,128)(2,1)S(1)}, bf16[768,768]{1,0:T(8,128)(2,1)}, u32[]{:S(2)}) copy-start(bf16[768,768]{1,0:T(8,128)(2,1)} %copy-done.8) | copy-start | bytes 3538948
  98.1 15.3 %copy-start.11 = (bf16[768,768]{1,0:T(8,128)(2,1)S(1)}, bf16[768,768]{1,0:T(8,128)(2,1)}, u32[]{:S(2)}) copy-start(bf16[768,768]{1,0:T(8,128)(2,1)} %copy-done.10) | copy-start | bytes 3538948
  105.0 1.6 copy-start.4
  113.5 8.6 %copy-start.5 = (bf16[2048,768]{1,0:T(8,128)(2,1)S(1)}, bf16[2048,768]{1,0:T(8,128)(2,1)}, u32[]{:S(2)}) copy-start(bf16[2048,768]{1,0:T(8,128)(2,1)} %copy-done.4) | copy-start | bytes 9437188
  127.3 8.0 %collective-permute-start.12 = (bf16[4,2304,256]{2,1,0:T(8,128)(2,1)S(1)}, bf16[4,2304,256]{2,1,0:T(8,128)(2,1)S(1)}, u32[]{:S(2)}, u32[]{:S(2)}) collective-permute-start(bf16[4,2304,256]{2,1,0:T(8,128)(2,1)S(1)} %give.2), channel_id=1, source_target_pairs={{0,4},{4,0},{8,12},{12,8},{16,20},{20,16},{24,28},{28,24},{1,5},{5... | collective-permute-start | bytes 14155784 | tf_op jit(solution)/shard_map/ppermute | solution.py:548
  127.3 22.8 %collective-permute-start.10 = (bf16[160,2048]{1,0:T(8,128)(2,1)S(1)}, bf16[160,2048]{1,0:T(8,128)(2,1)S(1)}, u32[]{:S(2)}, u32[]{:S(2)}) collective-permute-start(bf16[160,2048]{1,0:T(8,128)(2,1)S(1)} %get-tuple-element.81), channel_id=1, source_target_pairs={{0,3},{1,2},{2,1},{3,0},{4,7},{5,6},{6,5},{7,4},{8,11},{9,10},{10,... | collective-permute-start | bytes 1966088 | tf_op jit(solution)/shard_map/ppermute | solution.py:503
  137.8 25.5 %collective-permute-start.14 = (bf16[1152,256]{1,0:T(8,128)(2,1)S(1)}, bf16[1152,256]{1,0:T(8,128)(2,1)S(1)}, u32[]{:S(2)}, u32[]{:S(2)}) collective-permute-start(bf16[1152,256]{1,0:T(8,128)(2,1)S(1)} %get-tuple-element.92), channel_id=1, source_target_pairs={{0,8},{4,12},{8,0},{12,4},{16,24},{20,28},{24,16},{28,20},{1,9},{5... | collective-permute-start | bytes 1769480 | tf_op jit(solution)/shard_map/ppermute | solution.py:443
  139.4 25.6 %collective-permute-start.17 = (bf16[1152,256]{1,0:T(8,128)(2,1)S(1)}, bf16[1152,256]{1,0:T(8,128)(2,1)S(1)}, u32[]{:S(2)}, u32[]{:S(2)}) collective-permute-start(bf16[1152,256]{1,0:T(8,128)(2,1)S(1)} %get-tuple-element.97), channel_id=1, source_target_pairs={{0,16},{4,20},{8,24},{12,28},{16,0},{20,4},{24,8},{28,12},{1,17},{... | collective-permute-start | bytes 1769480 | tf_op jit(solution)/shard_map/ppermute | solution.py:443
  140.9 51.7 %collective-permute-start.9 = (bf16[160,2048]{1,0:T(8,128)(2,1)S(1)}, bf16[160,2048]{1,0:T(8,128)(2,1)S(1)}, u32[]{:S(2)}, u32[]{:S(2)}) collective-permute-start(bf16[160,2048]{1,0:T(8,128)(2,1)S(1)} %get-tuple-element.79), channel_id=1, source_target_pairs={{0,1},{1,0},{2,3},{3,2},{4,5},{5,4},{6,7},{7,6},{8,9},{9,8},{10,11... | collective-permute-start | bytes 1966088 | tf_op jit(solution)/shard_map/ppermute | solution.py:503
  150.1 42.5 %collective-permute-start.11 = (bf16[160,2048]{1,0:T(8,128)(2,1)S(1)}, bf16[160,2048]{1,0:T(8,128)(2,1)S(1)}, u32[]{:S(2)}, u32[]{:S(2)}) collective-permute-start(bf16[160,2048]{1,0:T(8,128)(2,1)S(1)} %get-tuple-element.82), channel_id=1, source_target_pairs={{0,2},{1,3},{2,0},{3,1},{4,6},{5,7},{6,4},{7,5},{8,10},{9,11},{10,... | collective-permute-start | bytes 1966088 | tf_op jit(solution)/shard_map/ppermute | solution.py:503
  161.8 15.0 %collective-permute-start.13 = (bf16[1152,256]{1,0:T(8,128)(2,1)S(1)}, bf16[1152,256]{1,0:T(8,128)(2,1)S(1)}, u32[]{:S(2)}, u32[]{:S(2)}) collective-permute-start(bf16[1152,256]{1,0:T(8,128)(2,1)S(1)} %get-tuple-element.90), channel_id=1, source_target_pairs={{0,8},{4,12},{8,0},{12,4},{16,24},{20,28},{24,16},{28,20},{1,9},{5... | collective-permute-start | bytes 1769480 | tf_op jit(solution)/shard_map/ppermute | solution.py:443
  163.3 16.3 %collective-permute-start.16 = (bf16[1152,256]{1,0:T(8,128)(2,1)S(1)}, bf16[1152,256]{1,0:T(8,128)(2,1)S(1)}, u32[]{:S(2)}, u32[]{:S(2)}) collective-permute-start(bf16[1152,256]{1,0:T(8,128)(2,1)S(1)} %get-tuple-element.95), channel_id=1, source_target_pairs={{0,16},{4,20},{8,24},{12,28},{16,0},{20,4},{24,8},{28,12},{1,17},{... | collective-permute-start | bytes 1769480 | tf_op jit(solution)/shard_map/ppermute | solution.py:443
  165.0 25.7 %collective-permute-start.15 = (bf16[1152,256]{1,0:T(8,128)(2,1)S(1)}, bf16[1152,256]{1,0:T(8,128)(2,1)S(1)}, u32[]{:S(2)}, u32[]{:S(2)}) collective-permute-start(bf16[1152,256]{1,0:T(8,128)(2,1)S(1)} %add_convert_fusion.1), channel_id=1, source_target_pairs={{0,16},{4,20},{8,24},{12,28},{16,0},{20,4},{24,8},{28,12},{1,17},{... | collective-permute-start | bytes 1769480 | tf_op jit(solution)/shard_map/ppermute | solution.py:443
  176.8 14.1 %collective-permute-start.18 = (bf16[1152,256]{1,0:T(8,128)(2,1)S(1)}, bf16[1152,256]{1,0:T(8,128)(2,1)S(1)}, u32[]{:S(2)}, u32[]{:S(2)}) collective-permute-start(bf16[1152,256]{1,0:T(8,128)(2,1)S(1)} %add_convert_fusion), channel_id=1, source_target_pairs={{0,8},{4,12},{8,0},{12,4},{16,24},{20,28},{24,16},{28,20},{1,9},{5... | collective-permute-start | bytes 1769480 | tf_op jit(solution)/shard_map/ppermute | solution.py:443
  191.0 1.7 copy-start.25

commit v3 on v2

--- a/solution.py
+++ b/solution.py
@@ -256,12 +256,12 @@
     )(*arrays, w_pair, w_pair, *before)
 
 
-def inner_kernel(sizes, tiles, rows, *refs):
-    count, sources = sum(sizes), len(sizes)
+def inner_kernel(sizes, rows, tiles, *refs):
+    count = sum(sizes)
     down_w, gate_d, up_d, w_ref = refs[count : count + 4]
-    outs, (grads, gate_out, up_out, grad_pre) = refs[-4 - sources : -4], refs[-4:]
+    last, grads, gate_out, up_out, grad_pre = refs[-5:]
     step = pl.program_id(0)
-    units = grad_pre.shape[1] // 2
+    units, capacity = grad_pre.shape[1] // 2, last.shape[0]
 
     @pl.when(step == 0)
     def _():
@@ -275,17 +275,14 @@
             tile = grad_hidden.shape[1]
             for at, slope, out in ((0, gate_d, gate_out), (units, up_d, up_out)):
                 value = (grad_hidden * slope[:rows, :].astype(F32)).astype(BF16)
-                grad_pre[:, at + j * tile : at + (j + 1) * tile] = value
+                grad_pre[:, at + j * tile : at + (j + 1) * tile] = value[rows - capacity :, :]
                 out[:rows, :] = value
                 if rows < out.shape[0]:
                     out[rows:, :] = jnp.zeros((out.shape[0] - rows, tile), BF16)
 
     @pl.when(step >= tiles)
     def _():
-        back = dot_nt(grad_pre[...], w_ref[...])
-        capacity = rows // sources
-        for m, out in enumerate(outs):
-            out[...] = back[m * capacity : (m + 1) * capacity, :].astype(BF16)
+        last[...] = dot_nt(grad_pre[...], w_ref[...]).astype(BF16)
 
 
 def inner(group, sources, w_down, gate_d, up_d, w_pair, before):
@@ -295,7 +292,6 @@
     tile = math.gcd(units, 256)
     tiles = units // tile
     block = min(width, 512)
-    rows = len(sources) * capacity
     total, parts = parts_of(capacity, group)
     held, part = parts[not before]
 
@@ -305,9 +301,9 @@
     def block_at(i):
         return jnp.maximum(i - tiles, 0)
 
-    first, outs = len(arrays) + 4, len(sources)
+    first = len(arrays) + 4
     return pl.pallas_call(
-        functools.partial(inner_kernel, sizes, tiles, rows),
+        functools.partial(inner_kernel, sizes, len(sources) * capacity, tiles),
         grid=(tiles + width // block,),
         in_specs=[part_spec(a, capacity) for a in arrays]
         + [
@@ -317,24 +313,54 @@
             pl.BlockSpec((block, 2 * units), lambda i: (block_at(i), 0)),
         ]
         + [pl.BlockSpec(memory_space=pl.ANY) for _ in before],
-        out_specs=[pl.BlockSpec((capacity, block), lambda i: (0, block_at(i)))] * outs
-        + [
+        out_specs=[
+            pl.BlockSpec((capacity, block), lambda i: (0, block_at(i))),
             pl.BlockSpec((held, width), lambda i: (part, 0)),
             pl.BlockSpec((held, tile), lambda i: (part, tile_at(i))),
             pl.BlockSpec((held, tile), lambda i: (part, tile_at(i))),
         ],
-        out_shape=[jax.ShapeDtypeStruct((capacity, width), BF16)] * outs
-        + [
+        out_shape=[
+            jax.ShapeDtypeStruct((capacity, width), BF16),
             jax.ShapeDtypeStruct((total, width), BF16),
             jax.ShapeDtypeStruct((total, units), BF16),
             jax.ShapeDtypeStruct((total, units), BF16),
         ],
-        scratch_shapes=[pltpu.VMEM((rows, 2 * units), BF16)],
-        input_output_aliases={first + i: outs + i for i in range(len(before))},
+        scratch_shapes=[pltpu.VMEM((capacity, 2 * units), BF16)],
+        input_output_aliases={first + i: 1 + i for i in range(len(before))},
         compiler_params=params(1, 20),
         cost_estimate=FREE,
         name="inner",
     )(*arrays, w_down, gate_d, up_d, w_pair, *before)
+
+
+def back_kernel(sources, gate_ref, up_ref, w_ref, *outs):
+    units, capacity = gate_ref.shape[1], outs[0].shape[0]
+    rows = sources * capacity
+    value = dot_nt(gate_ref[:rows, :], w_ref[:, :units])
+    value += dot_nt(up_ref[:rows, :], w_ref[:, units:])
+    for m, out in enumerate(outs):
+        out[...] = value[m * capacity : (m + 1) * capacity, :].astype(BF16)
+
+
+def back(group, capacity, gate, up, w_pair):
+    width, units = w_pair.shape[0], gate.shape[1]
+    held, part = parts_of(capacity, group)[1][False]
+    sources = group - 2
+    block = min(width, 512)
+    return pl.pallas_call(
+        functools.partial(back_kernel, sources),
+        grid=(width // block,),
+        in_specs=[
+            pl.BlockSpec((held, units), lambda i: (part, 0)),
+            pl.BlockSpec((held, units), lambda i: (part, 0)),
+            pl.BlockSpec((block, 2 * units), lambda i: (i, 0)),
+        ],
+        out_specs=[pl.BlockSpec((capacity, block), lambda i: (0, i))] * sources,
+        out_shape=[jax.ShapeDtypeStruct((capacity, width), BF16)] * sources,
+        compiler_params=params(1, 18),
+        cost_estimate=FREE,
+        name="back",
+    )(gate, up, w_pair)
 
 
 def pair_chunks(flipped_rows, sides, chunk):
@@ -510,12 +536,11 @@
 
     if group == 4 and tok_rows < 2 * capacity:
         far, near, cross = [(0, 2), (3, 1)], [(1, 2), (2, 1)], [(1, 3), (2, 0)]
-        far_meta = move(meta, far)
-        far_rows = move(after(tokens_in, far_meta), far)
+        far_rows, far_meta = move(tokens_in, far), move(meta, far)
         x0, g0, x1, g1, x2, g2, x3, g3 = pack(
             place, meta, dict(tokens=tokens_in, grads=out_grad), [0, 1, 2, 3], [], capacity, top
         )
-        x1, x3, x2 = swap(x1, 1), move(x3, near), move(x2, cross)
+        x1, x3, x2 = swap(x1, 1), move(after(x3, far_meta), near), move(x2, cross)
         cx, onward = pack(place, far_meta, dict(tokens=far_rows), [0, 1], [], capacity + 16, top)
         onward = move(onward, [(2, 3), (1, 0)])
         g1 = swap(after(g1, x1), 1)
@@ -534,15 +559,15 @@
     own_d = forward(group, inputs[:1], w_pair, [])
     others_d = forward(group, inputs[1:], w_pair, own_d[2:])
     own_back, *own_grads = inner(group, grads[:1], w_lower, *own_d[:2], w_pair, [])
-    late = inner(group, grads[1:], w_lower, *others_d[:2], w_pair, own_grads)
-    returned = [own_back, *late[: group - 1]]
+    last, *late = inner(group, grads[1:], w_lower, *others_d[:2], w_pair, own_grads)
+    returned = [own_back, *back(group, capacity, *late[1:], w_pair), last]
     for m in range(group - 1, 0, -1):
         ahead = returned[m + 1 :] if 2 * m >= group else []
         returned[m] = swap(after(returned[m], *ahead), m)
 
     shares = replicas // 2
     own = [replica ^ (2 * r) for r in range(shares)]
-    operands = (others_d[3], others_d[2], *late[group - 1 :])
+    operands = (others_d[3], others_d[2], *late)
     first_own = jnp.stack(own) ^ 1
     given = give(first_own, *operands, replicas, chunk)
     came = lax.ppermute(given, "dp", [(i, i ^ 1) for i in range(replicas)])
@@ -551,8 +576,9 @@
     middle = len(bits) // 2
     first_bits, second_bits = bits, bits[middle:] + bits[:middle]
     first, second = split(mine, came)
-    firsts = halvings(first, first_bits, returned[-1])
-    seconds = halvings(second, second_bits, returned[-1])
+    ahead = (returned[1], returned[-1])
+    firsts = halvings(first, first_bits, ahead)
+    seconds = halvings(second, second_bits, ahead)
     pair_sum, lower_sum = finish(
         firsts, seconds, (width // replicas, 2 * units), (units // replicas, width)
     )

time: 197 us -> 193 us (0.980)
  starting transfers between devices: 51 us -> 46.6 us
    ppermute x12, starting transfers between devices: 42.8 us -> 37.3 us  [move(): return lax.ppermute(array, 'expert', pairs)]
    ppermute x6, waiting for transfers between devices: 23.8 us -> 20.6 us  [halvings(): terms[r ^ 1 << bit].append(lax.ppermute(mine[0], 'dp', pairs))]
    ppermute x12, waiting for transfers between devices: 44.3 us -> 46.7 us  [move(): return lax.ppermute(array, 'expert', pairs)]
    pallas_call x2 -> x3, Pallas kernels: 13.3 us -> 14.9 us  [the longest x2 11.9 us: inner(): pl.pallas_call(functools.partial(inner_kernel, sizes, len(sources) * capa...]
    unnamed x52 -> x56, local copies, waits for them, and re-layouts: 26.2 us -> 26.1 us
  transfers between devices with their start and end apart: 19 -> 19, of which waited for: 10 -> 10; matrix products, arithmetic and copies ran while one was open for 0% -> 1% of each run, Pallas kernels for 16% -> 17%
where the time goes in v3:
time: 193 us; the launch traced here: 192 us
  waiting for transfers between devices  67.6 us (35%)
  Pallas kernels  49.2 us (25%)
  starting transfers between devices  46.6 us (24%)
  local copies, waits for them, and re-layouts  26.1 us (14%)
    ppermute x12, waiting for transfers between devices, move(): return lax.ppermute(array, 'expert', pairs)  46.7 us
    ppermute x12, starting transfers between devices, move(): return lax.ppermute(array, 'expert', pairs)  37.3 us
    unnamed x56, local copies, waits for them, and re-layouts  26.1 us
    ppermute x6, waiting for transfers between devices, halvings(): terms[r ^ 1 << bit].append(lax.ppermute(mine[0], 'dp', pairs))  20.6 us
    pallas_call x2, Pallas kernels, inner(): pl.pallas_call(functools.partial(inner_kernel, sizes, len(sources) * capa...  11.9 us
    pallas_call x2, Pallas kernels, forward(): pl.pallas_call(functools.partial(forward_kernel, sizes), grid=(tiles,), i...  10.3 us
    pallas_call x2, Pallas kernels, give(): pl.pallas_call(functools.partial(give_kernel, shares, chunk), grid_spec=p...  10.2 us
    ppermute x6, starting transfers between devices, halvings(): terms[r ^ 1 << bit].append(lax.ppermute(mine[0], 'dp', pairs))  9.22 us
  transfers between devices with their start and end apart: 19, of which 10 were waited for; matrix products, arithmetic and copies ran while one was open for 1% of the time, Pallas kernels for 17%

profile of v3, /device:TPU:0, one launch (start us, length us, event | category | flops | bytes accessed | tf_op | source)
XLA Modules:
  0.0 192.2 jit_solution(53147378246428905)
XLA Ops:
  0.6 6.0 %collective-permute-start.7 = (bf16[256,2048]{1,0:T(8,128)(2,1)}, bf16[256,2048]{1,0:T(8,128)(2,1)S(1)}, u32[]{:S(2)}, u32[]{:S(2)}) collective-permute-start(bf16[256,2048]{1,0:T(8,128)(2,1)} %rest_0_.1), channel_id=1, source_target_pairs={{0,2},{3,1},{4,6},{7,5},{8,10},{11,9},{12,14},{15,13},{16,18},{19,... | collective-permute-start | bytes 3145736 | tf_op jit(solution)/shard_map/ppermute | solution.py:529
  8.0 1.3 collective-permute-start.2
  9.3 1.2 copy-done.14
  10.6 1.2 copy-done.15
  11.8 3.9 %pack.2 = (bf16[160,2048]{1,0:T(8,128)(2,1)S(1)}, bf16[160,2048]{1,0:T(8,128)(2,1)S(1)}, bf16[160,2048]{1,0:T(8,128)(2,1)S(1)}, bf16[160,2048]{1,0:T(8,128)(2,1)...) custom-call(s32[1]{0:T(128)} %bitcast.me_ref, ...), custom_call_target="tpu_custom_call" | custom-call | flops 1 | bytes 1 | tf_op jit(solution)/shard_map/pack/pallas_call | solution.py:118
  15.7 1.3 collective-permute-start.5
  17.0 13.6 %collective-permute-done.2.meta_ref = bf16[16,256]{1,0:T(8,128)(2,1)S(1)} collective-permute-done((bf16[16,256]{1,0:T(8,128)(2,1)S(1)}, bf16[16,256]{1,0:T(8,128)(2,1)S(1)}, u32[]{:S(2)}, u32[]{:S(2)}) %collective-permute-start.2) | collective-permute-done | bytes 8224 | tf_op jit(solution)/shard_map/ppermute | solution.py:529
  31.3 2.4 %pack.3 = (bf16[176,2048]{1,0:T(8,128)(2,1)S(1)}, bf16[176,2048]{1,0:T(8,128)(2,1)}) custom-call(s32[1]{0:T(128)} %bitcast.me_ref, bf16[16,256]{1,0:T(8,128)(2,1)S(1)} %collective-permute-done.2.meta_ref, bf16[256,2048]{1,0:T(8,128)(2,1)S(1)} %collective-permute-done.7.rest_0_), custom_call_target="tpu_custom_call" | custom-call | flops 1 | bytes 1 | tf_op jit(solution)/shard_map/pack/pallas_call | solution.py:118
  34.5 1.3 collective-permute-start.8
  35.8 10.6 %collective-permute-done.refs_0_ = bf16[160,2048]{1,0:T(8,128)(2,1)S(1)} collective-permute-done((bf16[160,2048]{1,0:T(8,128)(2,1)S(1)}, bf16[160,2048]{1,0:T(8,128)(2,1)S(1)}, u32[]{:S(2)}, u32[]{:S(2)}) %collective-permute-start) | collective-permute-done | bytes 655392 | tf_op jit(solution)/shard_map/ppermute | solution.py:529
  49.9 12.1 %collective-permute-start.4 = (bf16[160,2048]{1,0:T(8,128)(2,1)}, bf16[160,2048]{1,0:T(8,128)(2,1)}, u32[]{:S(2)}, u32[]{:S(2)}) collective-permute-start(bf16[160,2048]{1,0:T(8,128)(2,1)} %get-tuple-element.66), channel_id=1, source_target_pairs={{0,2},{1,3},{2,0},{3,1},{4,6},{5,7},{6,4},{7,5},{8,10},{9,11},{10,... | collective-permute-start | bytes 1966088 | tf_op jit(solution)/shard_map/ppermute | solution.py:529
  62.0 2.8 %copy-done = bf16[1,2048,1536]{2,1,0:T(8,128)(2,1)S(1)} copy-done((bf16[1,2048,1536]{2,1,0:T(8,128)(2,1)S(1)}, bf16[1,2048,1536]{2,1,0:T(8,128)(2,1)}, u32[]{:S(2)}) %copy-start) | copy-done | bytes 6291480
  64.7 3.4 %forward.2 = (bf16[256,768]{1,0:T(8,128)(2,1)S(1)}, bf16[256,768]{1,0:T(8,128)(2,1)S(1)}, bf16[768,768]{1,0:T(8,128)(2,1)S(1)}, bf16[2048,768]{1,0:T(8,128)(2,1)S(1)}) custom-call(bf16[160,2048]{1,0:T(8,128)(2,1)S(1)} %get-tuple-element.56.refs_0_, bf16[2048,1536]{1,0:T(8,128)(2,1)S(1)} %bitcast.18, bf16[2048,1536]{1,0:T(8,128)(2,1)S(1)} %bitcast.19), custom_call_target="tpu_custom_call" | custom-call | flops 805306368 | bytes 1 | tf_op jit(solution)/shard_map/forward/pallas_call | solution.py:235
  68.2 1.6 copy-done.2
  69.8 1.0 copy-done.12
  70.8 4.7 %inner.2 = (bf16[160,2048]{1,0:T(8,128)(2,1)S(1)}, bf16[768,2048]{1,0:T(8,128)(2,1)S(1)}, bf16[768,768]{1,0:T(8,128)(2,1)S(1)}, bf16[768,768]{1,0:T(8,128)(2,1)S(1)}) custom-call(bf16[160,2048]{1,0:T(8,128)(2,1)S(1)} %get-tuple-element.55.refs_0_, bf16[768,2048]{1,0:T(8,128)(2,1)S(1)} %bitcast.29, bf16[256,768]{1,0:T(8,128)(2,1)S(1)} %get-tuple-element.57.refs_2_, ...), custom_call_target="tpu_custom_call" | custom-call | flops 1 | bytes 1 | tf_op jit(solution)/shard_map/inner/pallas_call | solution.py:305
  76.5 1.0 copy-done.8
  78.5 2.8 %copy-done.1 = bf16[1,2048,1536]{2,1,0:T(8,128)(2,1)S(1)} copy-done((bf16[1,2048,1536]{2,1,0:T(8,128)(2,1)S(1)}, bf16[1,2048,1536]{2,1,0:T(8,128)(2,1)}, u32[]{:S(2)}) %copy-start.1) | copy-done | bytes 6291480
  81.3 1.9 copy-done.3
  83.2 1.3 copy-done.13
  84.4 1.1 copy-done.17
  85.6 1.1 copy-done.19
  86.6 1.1 copy-done.21
  87.7 1.1 copy-done.23
  88.8 6.9 %forward.3 = (bf16[512,768]{1,0:T(8,128)(2,1)S(1)}, bf16[512,768]{1,0:T(8,128)(2,1)S(1)}, bf16[768,768]{1,0:T(8,128)(2,1)S(1)}, bf16[2048,768]{1,0:T(8,128)(2,1)S(1)}) custom-call(bf16[160,2048]{1,0:T(8,128)(2,1)S(1)} %copy-done.19, bf16[176,2048]{1,0:T(8,128)(2,1)S(1)} %copy-done.17, ...), custom_call_target="tpu_custom_call", output_to_operand_aliasing={{2}: (7, {}), {3}: (8, {})} | custom-call | flops 1610612736 | bytes 1 | tf_op jit(solution)/shard_map/forward/pallas_call | solution.py:235
  95.7 1.6 copy-done.4
  97.4 18.2 %collective-permute-done.4.refs_1_ = bf16[160,2048]{1,0:T(8,128)(2,1)} collective-permute-done((bf16[160,2048]{1,0:T(8,128)(2,1)}, bf16[160,2048]{1,0:T(8,128)(2,1)}, u32[]{:S(2)}, u32[]{:S(2)}) %collective-permute-start.4) | collective-permute-done | bytes 655392 | tf_op jit(solution)/shard_map/ppermute | solution.py:529
  115.6 7.3 %inner.3 = (bf16[160,2048]{1,0:T(8,128)(2,1)S(1)}, bf16[768,2048]{1,0:T(8,128)(2,1)S(1)}, bf16[768,768]{1,0:T(8,128)(2,1)S(1)}, bf16[768,768]{1,0:T(8,128)(2,1)S(1)}) custom-call(bf16[160,2048]{1,0:T(8,128)(2,1)} %collective-permute-done.1.refs_0_, ...), custom_call_target="tpu_custom_call", output_to_operand_aliasing={{1}: (7, {}), {2}: (8, {}), {3}: (9, {})} | custom-call | flops 1 | bytes 1 | tf_op jit(solution)/shard_map/inner/pallas_call | solution.py:305
  122.9 5.1 %give.2 = bf16[4,2304,256]{2,1,0:T(8,128)(2,1)S(1)} custom-call(s32[4]{0:T(128)S(1)} %get-tuple-element.107.which_ref, bf16[8,256,768]{2,1,0:T(8,128)(2,1)S(1)} %bitcast.27, bf16[8,96,768]{2,1,0:T(8,128)(2,1)S(1)} %bitcast.31, bf16[768,2048]{1,0:T(8,128)(2,1)S(1)} %get-tuple-element.87.grads, bf16[768,768]{1,0:T(8,128)(2,1)S(1)} %get-tuple-element.79.gate_ref.gate, ...), custom_call_target="tpu_custom_call" | custom-call | flops 1 | bytes 1 | tf_op jit(solution)/shard_map/give/pallas_call | solution.py:413
  128.1 2.5 %collective-permute-start.10 = (bf16[160,2048]{1,0:T(8,128)(2,1)S(1)}, bf16[160,2048]{1,0:T(8,128)(2,1)S(1)}, u32[]{:S(2)}, u32[]{:S(2)}) collective-permute-start(bf16[160,2048]{1,0:T(8,128)(2,1)S(1)} %get-tuple-element.83), channel_id=1, source_target_pairs={{0,3},{1,2},{2,1},{3,0},{4,7},{5,6},{6,5},{7,4},{8,11},{9,10},{10,... | collective-permute-start | bytes 1966088 | tf_op jit(solution)/shard_map/ppermute | solution.py:529
  130.7 5.1 %give.3.own = bf16[4,2304,256]{2,1,0:T(8,128)(2,1)S(1)} custom-call(s32[4]{0:T(128)S(1)} %get-tuple-element.88.which_ref, bf16[8,256,768]{2,1,0:T(8,128)(2,1)S(1)} %bitcast.28, bf16[8,96,768]{2,1,0:T(8,128)(2,1)S(1)} %bitcast.32, bf16[768,2048]{1,0:T(8,128)(2,1)S(1)} %get-tuple-element.87.grads, bf16[768,768]{1,0:T(8,128)(2,1)S(1)} %get-tuple-element.79.gate_ref.gate, ...), custom_call_target="tpu_custom_call" | custom-call | flops 1 | bytes 1 | tf_op jit(solution)/shard_map/give/pallas_call | solution.py:413
  136.0 2.6 %split.1 = (bf16[1152,256]{1,0:T(8,128)(2,1)S(1)}, bf16[1152,256]{1,0:T(8,128)(2,1)S(1)}, bf16[1152,256]{1,0:T(8,128)(2,1)S(1)}, bf16[1152,256]{1,0:T(8,128)(2,1...) custom-call(bf16[4,2304,256]{2,1,0:T(8,128)(2,1)S(1)} %give.3.own, ...), custom_call_target="tpu_custom_call" | custom-call | flops 1 | bytes 1 | tf_op jit(solution)/shard_map/split/pallas_call | solution.py:446
  138.6 1.6 collective-permute-start.17
  140.2 2.9 %back.1 = (bf16[160,2048]{1,0:T(8,128)(2,1)S(1)}, bf16[160,2048]{1,0:T(8,128)(2,1)S(1)}) custom-call(bf16[768,768]{1,0:T(8,128)(2,1)S(1)} %get-tuple-element.79.gate_ref.gate, bf16[768,768]{1,0:T(8,128)(2,1)S(1)} %get-tuple-element.80.up_ref.up, bf16[2048,1536]{1,0:T(8,128)(2,1)S(1)} %bitcast.26), custom_call_target="tpu_custom_call" | custom-call | flops 1 | bytes 1 | tf_op jit(solution)/shard_map/back/pallas_call | solution.py:350
  143.2 1.6 collective-permute-start.14
  144.7 2.8 %collective-permute-done.10.refs_3_ = bf16[160,2048]{1,0:T(8,128)(2,1)S(1)} collective-permute-done((bf16[160,2048]{1,0:T(8,128)(2,1)S(1)}, bf16[160,2048]{1,0:T(8,128)(2,1)S(1)}, u32[]{:S(2)}, u32[]{:S(2)}) %collective-permute-start.10) | collective-permute-done | bytes 655392 | tf_op jit(solution)/shard_map/ppermute | solution.py:529
  147.6 11.3 %collective-permute-start.11 = (bf16[160,2048]{1,0:T(8,128)(2,1)S(1)}, bf16[160,2048]{1,0:T(8,128)(2,1)S(1)}, u32[]{:S(2)}, u32[]{:S(2)}) collective-permute-start(bf16[160,2048]{1,0:T(8,128)(2,1)S(1)} %get-tuple-element.84), channel_id=1, source_target_pairs={{0,2},{1,3},{2,0},{3,1},{4,6},{5,7},{6,4},{7,5},{8,10},{9,11},{10,... | collective-permute-start | bytes 1966088 | tf_op jit(solution)/shard_map/ppermute | solution.py:529
  158.9 1.5 collective-permute-start.13
  160.3 1.5 collective-permute-start.16
  162.0 1.5 collective-permute-done.9.refs_1_
  163.5 1.5 collective-permute-start.18
  165.1 1.6 collective-permute-start.15
  166.7 8.4 %collective-permute-done.13.refs_1_ = bf16[1152,256]{1,0:T(8,128)(2,1)S(1)} collective-permute-done((bf16[1152,256]{1,0:T(8,128)(2,1)S(1)}, bf16[1152,256]{1,0:T(8,128)(2,1)S(1)}, u32[]{:S(2)}, u32[]{:S(2)}) %collective-permute-start.13) | collective-permute-done | bytes 589856 | tf_op jit(solution)/shard_map/ppermute | solution.py:469
  175.1 1.5 collective-permute-done.16.refs_4_
  176.6 9.5 %collective-permute-done.18.refs_5_ = bf16[1152,256]{1,0:T(8,128)(2,1)S(1)} collective-permute-done((bf16[1152,256]{1,0:T(8,128)(2,1)S(1)}, bf16[1152,256]{1,0:T(8,128)(2,1)S(1)}, u32[]{:S(2)}, u32[]{:S(2)}) %collective-permute-start.18) | collective-permute-done | bytes 589856 | tf_op jit(solution)/shard_map/ppermute | solution.py:469
  186.1 1.2 collective-permute-done.15.refs_2_
  187.3 1.7 finish.1
  189.0 3.2 %combine.1 = bf16[256,2048]{1,0:T(8,128)(2,1)} custom-call(s32[1]{0:T(128)} %bitcast.me_ref, bf16[16,256]{1,0:T(8,128)(2,1)S(1)} %fusion.6.meta_ref, bf16[160,2048]{1,0:T(8,128)(2,1)S(1)} %copy-done.25, bf16[160,2048]{1,0:T(8,128)(2,1)S(1)} %collective-permute-done.9.refs_1_, bf16[160,2048]{1,0:T(8,128)(2,1)S(1)} %collective-permute-done.11.refs_2_, ...), custom_call_target="tpu_custom_call" | custom-call | flops 1 | bytes 1 | tf_op jit(solution)/shard_map/combine/pallas_call | solution.py:159
  (65 shorter events, 9.0 us)
Async XLA Ops:
  0.6 30.6 %collective-permute-start.7 = (bf16[256,2048]{1,0:T(8,128)(2,1)}, bf16[256,2048]{1,0:T(8,128)(2,1)S(1)}, u32[]{:S(2)}, u32[]{:S(2)}) collective-permute-start(bf16[256,2048]{1,0:T(8,128)(2,1)} %rest_0_.1), channel_id=1, source_target_pairs={{0,2},{3,1},{4,6},{7,5},{8,10},{11,9},{12,14},{15,13},{16,18},{19,... | collective-permute-start | bytes 3145736 | tf_op jit(solution)/shard_map/ppermute | solution.py:529
  8.0 22.5 %collective-permute-start.2 = (bf16[16,256]{1,0:T(8,128)(2,1)S(1)}, bf16[16,256]{1,0:T(8,128)(2,1)S(1)}, u32[]{:S(2)}, u32[]{:S(2)}) collective-permute-start(bf16[16,256]{1,0:T(8,128)(2,1)S(1)} %fusion.6.meta_ref), channel_id=1, source_target_pairs={{0,2},{3,1},{4,6},{7,5},{8,10},{11,9},{12,14},{15,13},{16,18},{19,... | collective-permute-start | bytes 24584 | tf_op jit(solution)/shard_map/ppermute | solution.py:529
  9.3 1.2 copy-start.14
  10.6 1.2 copy-start.15
  15.7 30.8 %collective-permute-start = (bf16[160,2048]{1,0:T(8,128)(2,1)S(1)}, bf16[160,2048]{1,0:T(8,128)(2,1)S(1)}, u32[]{:S(2)}, u32[]{:S(2)}) collective-permute-start(bf16[160,2048]{1,0:T(8,128)(2,1)S(1)} %get-tuple-element.61), channel_id=1, source_target_pairs={{0,1},{1,0},{2,3},{3,2},{4,5},{5,4},{6,7},{7,6},{8,9},{9,8},{10,11... | collective-permute-start | bytes 1966088 | tf_op jit(solution)/shard_map/ppermute | solution.py:529
  15.7 31.6 %collective-permute-start.5 = (bf16[160,2048]{1,0:T(8,128)(2,1)S(1)}, bf16[160,2048]{1,0:T(8,128)(2,1)S(1)}, u32[]{:S(2)}, u32[]{:S(2)}) collective-permute-start(bf16[160,2048]{1,0:T(8,128)(2,1)S(1)} %get-tuple-element.68), channel_id=1, source_target_pairs={{1,3},{2,0},{5,7},{6,4},{9,11},{10,8},{13,15},{14,12},{17,19},{18,... | collective-permute-start | bytes 1966088 | tf_op jit(solution)/shard_map/ppermute | solution.py:529
  30.6 18.4 %collective-permute-start.3 = (bf16[160,2048]{1,0:T(8,128)(2,1)S(1)}, bf16[160,2048]{1,0:T(8,128)(2,1)S(1)}, u32[]{:S(2)}, u32[]{:S(2)}) collective-permute-start(bf16[160,2048]{1,0:T(8,128)(2,1)S(1)} %get-tuple-element.65), channel_id=1, source_target_pairs={{1,2},{2,1},{5,6},{6,5},{9,10},{10,9},{13,14},{14,13},{17,18},{18,... | collective-permute-start | bytes 1966088 | tf_op jit(solution)/shard_map/ppermute | solution.py:529
  33.7 0.9 copy-start.16
  34.5 43.9 %collective-permute-start.8 = (bf16[176,2048]{1,0:T(8,128)(2,1)}, bf16[176,2048]{1,0:T(8,128)(2,1)}, u32[]{:S(2)}, u32[]{:S(2)}) collective-permute-start(bf16[176,2048]{1,0:T(8,128)(2,1)} %get-tuple-element.71), channel_id=1, source_target_pairs={{2,3},{1,0},{6,7},{5,4},{10,11},{9,8},{14,15},{13,12},{18,19},{17,... | collective-permute-start | bytes 2162696 | tf_op jit(solution)/shard_map/ppermute | solution.py:529
  46.5 0.8 copy-start.18
  47.3 50.1 %collective-permute-start.1 = (bf16[160,2048]{1,0:T(8,128)(2,1)}, bf16[160,2048]{1,0:T(8,128)(2,1)}, u32[]{:S(2)}, u32[]{:S(2)}) collective-permute-start(bf16[160,2048]{1,0:T(8,128)(2,1)} %get-tuple-element.62), channel_id=1, source_target_pairs={{0,1},{1,0},{2,3},{3,2},{4,5},{5,4},{6,7},{7,6},{8,9},{9,8},{10,11... | collective-permute-start | bytes 1966088 | tf_op jit(solution)/shard_map/ppermute | solution.py:529
  47.3 0.9 copy-start.20
  48.2 49.2 %collective-permute-start.6 = (bf16[160,2048]{1,0:T(8,128)(2,1)}, bf16[160,2048]{1,0:T(8,128)(2,1)}, u32[]{:S(2)}, u32[]{:S(2)}) collective-permute-start(bf16[160,2048]{1,0:T(8,128)(2,1)} %get-tuple-element.69), channel_id=1, source_target_pairs={{0,3},{1,2},{2,1},{3,0},{4,7},{5,6},{6,5},{7,4},{8,11},{9,10},{10,... | collective-permute-start | bytes 1966088 | tf_op jit(solution)/shard_map/ppermute | solution.py:529
  49.0 0.9 copy-start.22
  49.9 65.7 %collective-permute-start.4 = (bf16[160,2048]{1,0:T(8,128)(2,1)}, bf16[160,2048]{1,0:T(8,128)(2,1)}, u32[]{:S(2)}, u32[]{:S(2)}) collective-permute-start(bf16[160,2048]{1,0:T(8,128)(2,1)} %get-tuple-element.66), channel_id=1, source_target_pairs={{0,2},{1,3},{2,0},{3,1},{4,6},{5,7},{6,4},{7,5},{8,10},{9,11},{10,... | collective-permute-start | bytes 1966088 | tf_op jit(solution)/shard_map/ppermute | solution.py:529
  61.9 2.8 %copy-start = (bf16[1,2048,1536]{2,1,0:T(8,128)(2,1)S(1)}, bf16[1,2048,1536]{2,1,0:T(8,128)(2,1)}, u32[]{:S(2)}) copy-start(bf16[1,2048,1536]{2,1,0:T(8,128)(2,1)} %param.10) | copy-start | bytes 18874372
  64.7 6.1 %copy-start.10 = (bf16[1,768,2048]{2,1,0:T(8,128)(2,1)S(1)}, bf16[1,768,2048]{2,1,0:T(8,128)(2,1)}, u32[]{:S(2)}) copy-start(bf16[1,768,2048]{2,1,0:T(8,128)(2,1)} %param.11) | copy-start | bytes 9437188
  68.2 1.6 copy-start.2
  69.8 1.0 copy-start.12
  75.5 1.0 copy-start.6
  76.5 1.0 copy-start.8
  77.6 0.8 copy-start.24
  78.5 2.8 %copy-start.1 = (bf16[1,2048,1536]{2,1,0:T(8,128)(2,1)S(1)}, bf16[1,2048,1536]{2,1,0:T(8,128)(2,1)}, u32[]{:S(2)}) copy-start(bf16[1,2048,1536]{2,1,0:T(8,128)(2,1)} %param.10) | copy-start | bytes 18874372
  81.3 1.9 copy-start.3
  83.2 1.3 copy-start.13
  84.4 1.1 copy-start.17
  85.5 1.1 copy-start.19
  86.6 1.1 copy-start.21
  87.7 1.1 copy-start.23
  88.8 26.8 %copy-start.7 = (bf16[768,768]{1,0:T(8,128)(2,1)S(1)}, bf16[768,768]{1,0:T(8,128)(2,1)}, u32[]{:S(2)}) copy-start(bf16[768,768]{1,0:T(8,128)(2,1)} %copy-done.6) | copy-start | bytes 3538948
  88.8 26.8 %copy-start.9 = (bf16[768,768]{1,0:T(8,128)(2,1)S(1)}, bf16[768,768]{1,0:T(8,128)(2,1)}, u32[]{:S(2)}) copy-start(bf16[768,768]{1,0:T(8,128)(2,1)} %copy-done.8) | copy-start | bytes 3538948
  88.8 26.8 %copy-start.11 = (bf16[1,768,2048]{2,1,0:T(8,128)(2,1)S(1)}, bf16[1,768,2048]{2,1,0:T(8,128)(2,1)}, u32[]{:S(2)}) copy-start(bf16[1,768,2048]{2,1,0:T(8,128)(2,1)} %param.11) | copy-start | bytes 9437188
  95.7 1.6 copy-start.4
  115.6 7.3 %copy-start.5 = (bf16[2048,768]{1,0:T(8,128)(2,1)S(1)}, bf16[2048,768]{1,0:T(8,128)(2,1)}, u32[]{:S(2)}) copy-start(bf16[2048,768]{1,0:T(8,128)(2,1)} %copy-done.4) | copy-start | bytes 9437188
  122.9 17.3 %slice-start = ((s8[6291456]{0:T(1024)(128)(4,1)}), s8[4194304]{0:T(1024)(128)(4,1)S(1)}, s32[]{:S(2)}) async-start(s8[6291456]{0:T(1024)(128)(4,1)} %bitcast.24), calls=%async_computation | async-start | bytes 8388608
  128.0 8.0 %collective-permute-start.12 = (bf16[4,2304,256]{2,1,0:T(8,128)(2,1)S(1)}, bf16[4,2304,256]{2,1,0:T(8,128)(2,1)S(1)}, u32[]{:S(2)}, u32[]{:S(2)}) collective-permute-start(bf16[4,2304,256]{2,1,0:T(8,128)(2,1)S(1)} %give.2), channel_id=1, source_target_pairs={{0,4},{4,0},{8,12},{12,8},{16,20},{20,16},{24,28},{28,24},{1,5},{5... | collective-permute-start | bytes 14155784 | tf_op jit(solution)/shard_map/ppermute | solution.py:573
  128.1 19.4 %collective-permute-start.10 = (bf16[160,2048]{1,0:T(8,128)(2,1)S(1)}, bf16[160,2048]{1,0:T(8,128)(2,1)S(1)}, u32[]{:S(2)}, u32[]{:S(2)}) collective-permute-start(bf16[160,2048]{1,0:T(8,128)(2,1)S(1)} %get-tuple-element.83), channel_id=1, source_target_pairs={{0,3},{1,2},{2,1},{3,0},{4,7},{5,6},{6,5},{7,4},{8,11},{9,10},{10,... | collective-permute-start | bytes 1966088 | tf_op jit(solution)/shard_map/ppermute | solution.py:529
  130.7 9.5 %slice-start.1 = ((s8[6291456]{0:T(1024)(128)(4,1)}), s8[2097152]{0:T(1024)(128)(4,1)S(1)}, s32[]{:S(2)}) async-start(s8[6291456]{0:T(1024)(128)(4,1)} %bitcast.24), calls=%async_computation.1 | async-start | bytes 4194304
  138.6 21.7 %collective-permute-start.17 = (bf16[1152,256]{1,0:T(8,128)(2,1)S(1)}, bf16[1152,256]{1,0:T(8,128)(2,1)S(1)}, u32[]{:S(2)}, u32[]{:S(2)}) collective-permute-start(bf16[1152,256]{1,0:T(8,128)(2,1)S(1)} %get-tuple-element.97), channel_id=1, source_target_pairs={{0,16},{4,20},{8,24},{12,28},{16,0},{20,4},{24,8},{28,12},{1,17},{... | collective-permute-start | bytes 1769480 | tf_op jit(solution)/shard_map/ppermute | solution.py:469
  143.1 20.4 %collective-permute-start.9 = (bf16[160,2048]{1,0:T(8,128)(2,1)S(1)}, bf16[160,2048]{1,0:T(8,128)(2,1)S(1)}, u32[]{:S(2)}, u32[]{:S(2)}) collective-permute-start(bf16[160,2048]{1,0:T(8,128)(2,1)S(1)} %get-tuple-element.81), channel_id=1, source_target_pairs={{0,1},{1,0},{2,3},{3,2},{4,5},{5,4},{6,7},{7,6},{8,9},{9,8},{10,11... | collective-permute-start | bytes 1966088 | tf_op jit(solution)/shard_map/ppermute | solution.py:529
  143.2 21.8 %collective-permute-start.14 = (bf16[1152,256]{1,0:T(8,128)(2,1)S(1)}, bf16[1152,256]{1,0:T(8,128)(2,1)S(1)}, u32[]{:S(2)}, u32[]{:S(2)}) collective-permute-start(bf16[1152,256]{1,0:T(8,128)(2,1)S(1)} %get-tuple-element.92), channel_id=1, source_target_pairs={{0,8},{4,12},{8,0},{12,4},{16,24},{20,28},{24,16},{28,20},{1,9},{5... | collective-permute-start | bytes 1769480 | tf_op jit(solution)/shard_map/ppermute | solution.py:469
  147.6 41.4 %collective-permute-start.11 = (bf16[160,2048]{1,0:T(8,128)(2,1)S(1)}, bf16[160,2048]{1,0:T(8,128)(2,1)S(1)}, u32[]{:S(2)}, u32[]{:S(2)}) collective-permute-start(bf16[160,2048]{1,0:T(8,128)(2,1)S(1)} %get-tuple-element.84), channel_id=1, source_target_pairs={{0,2},{1,3},{2,0},{3,1},{4,6},{5,7},{6,4},{7,5},{8,10},{9,11},{10,... | collective-permute-start | bytes 1966088 | tf_op jit(solution)/shard_map/ppermute | solution.py:529
  158.9 16.3 %collective-permute-start.13 = (bf16[1152,256]{1,0:T(8,128)(2,1)S(1)}, bf16[1152,256]{1,0:T(8,128)(2,1)S(1)}, u32[]{:S(2)}, u32[]{:S(2)}) collective-permute-start(bf16[1152,256]{1,0:T(8,128)(2,1)S(1)} %get-tuple-element.90), channel_id=1, source_target_pairs={{0,8},{4,12},{8,0},{12,4},{16,24},{20,28},{24,16},{28,20},{1,9},{5... | collective-permute-start | bytes 1769480 | tf_op jit(solution)/shard_map/ppermute | solution.py:469
  160.3 16.3 %collective-permute-start.16 = (bf16[1152,256]{1,0:T(8,128)(2,1)S(1)}, bf16[1152,256]{1,0:T(8,128)(2,1)S(1)}, u32[]{:S(2)}, u32[]{:S(2)}) collective-permute-start(bf16[1152,256]{1,0:T(8,128)(2,1)S(1)} %get-tuple-element.95), channel_id=1, source_target_pairs={{0,16},{4,20},{8,24},{12,28},{16,0},{20,4},{24,8},{28,12},{1,17},{... | collective-permute-start | bytes 1769480 | tf_op jit(solution)/shard_map/ppermute | solution.py:469
  163.5 22.6 %collective-permute-start.18 = (bf16[1152,256]{1,0:T(8,128)(2,1)S(1)}, bf16[1152,256]{1,0:T(8,128)(2,1)S(1)}, u32[]{:S(2)}, u32[]{:S(2)}) collective-permute-start(bf16[1152,256]{1,0:T(8,128)(2,1)S(1)} %add_convert_fusion), channel_id=1, source_target_pairs={{0,8},{4,12},{8,0},{12,4},{16,24},{20,28},{24,16},{28,20},{1,9},{5... | collective-permute-start | bytes 1769480 | tf_op jit(solution)/shard_map/ppermute | solution.py:469
  165.1 22.2 %collective-permute-start.15 = (bf16[1152,256]{1,0:T(8,128)(2,1)S(1)}, bf16[1152,256]{1,0:T(8,128)(2,1)S(1)}, u32[]{:S(2)}, u32[]{:S(2)}) collective-permute-start(bf16[1152,256]{1,0:T(8,128)(2,1)S(1)} %add_convert_fusion.1), channel_id=1, source_target_pairs={{0,16},{4,20},{8,24},{12,28},{16,0},{20,4},{24,8},{28,12},{1,17},{... | collective-permute-start | bytes 1769480 | tf_op jit(solution)/shard_map/ppermute | solution.py:469
  187.3 1.7 copy-start.25

commit v4 on v3

--- a/solution.py
+++ b/solution.py
@@ -135,42 +135,72 @@
     )(me, meta, *sources.values())
 
 
-def combine_kernel(group, top, me_ref, meta_ref, *refs):
-    blocks, out, pick = refs[:group], refs[group], refs[group + 1]
-    capacity = blocks[0].shape[0]
+def combine_kernel(offsets, top, me_ref, meta_ref, *refs):
+    count = len(offsets)
+    blocks, total_ref, last_pick, pick = refs[: count - 1], refs[-3], refs[-2], refs[-1]
 
     @pl.when(pl.program_id(0) == 0)
     def _():
         ids, _ = ids_and_gates(meta_ref[...], top)
-        matrices = pick_matrices(me_ref[0], ids, list(range(group)), capacity)
-        for m, matrix in enumerate(matrices):
-            pick[m] = matrix.T.astype(BF16)
+        matrices = pick_matrices(me_ref[0], ids, offsets, last_pick.shape[1])
+        for at, matrix in enumerate(matrices[:-1]):
+            pick[at] = matrix.T.astype(BF16)
+        last_pick[...] = matrices[-1].T.astype(BF16)
 
     total = dot(pick[0], blocks[0][...])
-    for m in range(1, group):
-        total += dot(pick[m], blocks[m][...])
-    out[...] = total.astype(BF16)
-
-
-def combine(me, meta, blocks, top):
-    group, (capacity, width) = len(blocks), blocks[0].shape
-    rows = meta.shape[1]
+    for at in range(1, count - 1):
+        total += dot(pick[at], blocks[at][...])
+    total_ref[...] = total
+
+
+def combine(me, meta, blocks, offsets, top):
+    capacity, width = blocks[0].shape
+    rows, count = meta.shape[1], len(offsets)
     block = min(width, 512)
     return pl.pallas_call(
-        functools.partial(combine_kernel, group, top),
+        functools.partial(combine_kernel, offsets, top),
         grid=(width // block,),
         in_specs=[
             pl.BlockSpec(memory_space=pltpu.SMEM),
             pl.BlockSpec(meta.shape, lambda i: (0, 0)),
         ]
-        + [pl.BlockSpec((capacity, block), lambda i: (0, i))] * group,
-        out_specs=pl.BlockSpec((rows, block), lambda i: (0, i)),
-        out_shape=jax.ShapeDtypeStruct((rows, width), BF16),
-        scratch_shapes=[pltpu.VMEM((group, rows, capacity), BF16)],
+        + [pl.BlockSpec((capacity, block), lambda i: (0, i))] * (count - 1),
+        out_specs=[
+            pl.BlockSpec((rows, block), lambda i: (0, i)),
+            pl.BlockSpec((rows, capacity), lambda i: (0, 0)),
+        ],
+        out_shape=[
+            jax.ShapeDtypeStruct((rows, width), F32),
+            jax.ShapeDtypeStruct((rows, capacity), BF16),
+        ],
+        scratch_shapes=[pltpu.VMEM((count - 1, rows, capacity), BF16)],
         compiler_params=params(1, 10),
         cost_estimate=FREE,
         name="combine",
     )(me, meta, *blocks)
+
+
+def last_sum_kernel(total, pick, block, out):
+    out[...] = (total[...] + dot(pick[...], block[...])).astype(BF16)
+
+
+def last_sum(total, pick, rows):
+    tokens, width = total.shape
+    block = min(width, 1024)
+    return pl.pallas_call(
+        last_sum_kernel,
+        grid=(width // block,),
+        in_specs=[
+            pl.BlockSpec((tokens, block), lambda i: (0, i)),
+            pl.BlockSpec(pick.shape, lambda i: (0, 0)),
+            pl.BlockSpec((rows.shape[0], block), lambda i: (0, i)),
+        ],
+        out_specs=pl.BlockSpec((tokens, block), lambda i: (0, i)),
+        out_shape=jax.ShapeDtypeStruct((tokens, width), BF16),
+        compiler_params=params(1, 10),
+        cost_estimate=FREE,
+        name="last_sum",
+    )(total, pick, rows)
 
 
 def parts_of(capacity, group):
@@ -579,11 +609,18 @@
     ahead = (returned[1], returned[-1])
     firsts = halvings(first, first_bits, ahead)
     seconds = halvings(second, second_bits, ahead)
+    latest = max(1, group // 2)
+    offsets = [m for m in range(group) if m != latest] + [latest]
+    soon = [returned[m] for m in offsets[:-1]]
+    soon, firsts[1], seconds[1] = lax.optimization_barrier((soon, firsts[1], seconds[1]))
+    total, pick = combine(place, meta, soon, offsets, top)
     pair_sum, lower_sum = finish(
         firsts, seconds, (width // replicas, 2 * units), (units // replicas, width)
     )
-    *returned, pair_sum, lower_sum = lax.optimization_barrier((*returned, pair_sum, lower_sum))
-    grad_tokens = combine(place, meta, returned, top)
+    late_rows, pair_sum, lower_sum, total = lax.optimization_barrier(
+        (returned[latest], pair_sum, lower_sum, total)
+    )
+    grad_tokens = last_sum(total, pick, late_rows)
     return (grad_tokens, pair_sum, lower_sum)
 
 

time: 193 us -> 191 us (0.990)
  waiting for transfers between devices: 67.6 us -> 48.3 us
  starting transfers between devices: 46.6 us -> 63.7 us
    ppermute x12, starting transfers between devices: 37.3 us -> 54.5 us  [move(): return lax.ppermute(array, 'expert', pairs)]
    ppermute x12, waiting for transfers between devices: 46.7 us -> 29.6 us  [move(): return lax.ppermute(array, 'expert', pairs)]
    ppermute x6, waiting for transfers between devices: 20.6 us -> 18.5 us  [halvings(): terms[r ^ 1 << bit].append(lax.ppermute(mine[0], 'dp', pairs))]
  transfers between devices with their start and end apart: 19 -> 19, of which waited for: 10 -> 11; matrix products, arithmetic and copies ran while one was open for 1% -> 1% of each run, Pallas kernels for 17% -> 19%
where the time goes in v4:
time: 191 us
  starting transfers between devices  63.7 us (33%)
  Pallas kernels  49.7 us (26%)
  waiting for transfers between devices  48.3 us (25%)
  local copies, waits for them, and re-layouts  26.1 us (14%)
    ppermute x12, starting transfers between devices, move(): return lax.ppermute(array, 'expert', pairs)  54.5 us
    ppermute x12, waiting for transfers between devices, move(): return lax.ppermute(array, 'expert', pairs)  29.6 us
    unnamed x56, local copies, waits for them, and re-layouts  26.1 us
    ppermute x6, waiting for transfers between devices, halvings(): terms[r ^ 1 << bit].append(lax.ppermute(mine[0], 'dp', pairs))  18.5 us
    pallas_call x2, Pallas kernels, inner(): pl.pallas_call(functools.partial(inner_kernel, sizes, len(sources) * capa...  11.9 us
    pallas_call x2, Pallas kernels, forward(): pl.pallas_call(functools.partial(forward_kernel, sizes), grid=(tiles,), i...  10.3 us
    pallas_call x2, Pallas kernels, give(): pl.pallas_call(functools.partial(give_kernel, shares, chunk), grid_spec=p...  10.2 us
    ppermute x6, starting transfers between devices, halvings(): terms[r ^ 1 << bit].append(lax.ppermute(mine[0], 'dp', pairs))  9.22 us
  transfers between devices with their start and end apart: 19, of which 11 were waited for; matrix products, arithmetic and copies ran while one was open for 1% of the time, Pallas kernels for 19%

profile of v4, /device:TPU:0, one launch (start us, length us, event | category | flops | bytes accessed | tf_op | source)
XLA Modules:
  0.0 190.6 jit_solution(4934801520654669350)
XLA Ops:
  0.6 6.0 %collective-permute-start.7 = (bf16[256,2048]{1,0:T(8,128)(2,1)}, bf16[256,2048]{1,0:T(8,128)(2,1)S(1)}, u32[]{:S(2)}, u32[]{:S(2)}) collective-permute-start(bf16[256,2048]{1,0:T(8,128)(2,1)} %rest_0_.1), channel_id=1, source_target_pairs={{0,2},{3,1},{4,6},{7,5},{8,10},{11,9},{12,14},{15,13},{16,18},{19,... | collective-permute-start | bytes 3145736 | tf_op jit(solution)/shard_map/ppermute | solution.py:559
  8.0 1.3 collective-permute-start.2
  9.3 1.2 copy-done.14
  10.6 1.2 copy-done.15
  11.8 3.9 %pack.2 = (bf16[160,2048]{1,0:T(8,128)(2,1)S(1)}, bf16[160,2048]{1,0:T(8,128)(2,1)S(1)}, bf16[160,2048]{1,0:T(8,128)(2,1)S(1)}, bf16[160,2048]{1,0:T(8,128)(2,1)...) custom-call(s32[1]{0:T(128)} %bitcast.me_ref, ...), custom_call_target="tpu_custom_call" | custom-call | flops 1 | bytes 1 | tf_op jit(solution)/shard_map/pack/pallas_call | solution.py:118
  15.7 1.3 collective-permute-start.5
  17.0 2.6 %collective-permute-start = (bf16[160,2048]{1,0:T(8,128)(2,1)S(1)}, bf16[160,2048]{1,0:T(8,128)(2,1)S(1)}, u32[]{:S(2)}, u32[]{:S(2)}) collective-permute-start(bf16[160,2048]{1,0:T(8,128)(2,1)S(1)} %get-tuple-element.61), channel_id=1, source_target_pairs={{0,1},{1,0},{2,3},{3,2},{4,5},{5,4},{6,7},{7,6},{8,9},{9,8},{10,11... | collective-permute-start | bytes 1966088 | tf_op jit(solution)/shard_map/ppermute | solution.py:559
  19.6 10.9 %collective-permute-done.2.meta_ref = bf16[16,256]{1,0:T(8,128)(2,1)S(1)} collective-permute-done((bf16[16,256]{1,0:T(8,128)(2,1)S(1)}, bf16[16,256]{1,0:T(8,128)(2,1)S(1)}, u32[]{:S(2)}, u32[]{:S(2)}) %collective-permute-start.2) | collective-permute-done | bytes 8224 | tf_op jit(solution)/shard_map/ppermute | solution.py:559
  31.3 2.4 %pack.3 = (bf16[176,2048]{1,0:T(8,128)(2,1)S(1)}, bf16[176,2048]{1,0:T(8,128)(2,1)}) custom-call(s32[1]{0:T(128)} %bitcast.me_ref, bf16[16,256]{1,0:T(8,128)(2,1)S(1)} %collective-permute-done.2.meta_ref, bf16[256,2048]{1,0:T(8,128)(2,1)S(1)} %collective-permute-done.7.rest_0_), custom_call_target="tpu_custom_call" | custom-call | flops 1 | bytes 1 | tf_op jit(solution)/shard_map/pack/pallas_call | solution.py:118
  34.5 1.3 collective-permute-start.8
  35.8 9.5 %collective-permute-done.5.refs_2_ = bf16[160,2048]{1,0:T(8,128)(2,1)S(1)} collective-permute-done((bf16[160,2048]{1,0:T(8,128)(2,1)S(1)}, bf16[160,2048]{1,0:T(8,128)(2,1)S(1)}, u32[]{:S(2)}, u32[]{:S(2)}) %collective-permute-start.5) | collective-permute-done | bytes 655392 | tf_op jit(solution)/shard_map/ppermute | solution.py:559
  46.2 2.5 %collective-permute-start.6 = (bf16[160,2048]{1,0:T(8,128)(2,1)}, bf16[160,2048]{1,0:T(8,128)(2,1)}, u32[]{:S(2)}, u32[]{:S(2)}) collective-permute-start(bf16[160,2048]{1,0:T(8,128)(2,1)} %get-tuple-element.69), channel_id=1, source_target_pairs={{0,3},{1,2},{2,1},{3,0},{4,7},{5,6},{6,5},{7,4},{8,11},{9,10},{10,... | collective-permute-start | bytes 1966088 | tf_op jit(solution)/shard_map/ppermute | solution.py:559
  51.0 24.9 %collective-permute-start.4 = (bf16[160,2048]{1,0:T(8,128)(2,1)}, bf16[160,2048]{1,0:T(8,128)(2,1)}, u32[]{:S(2)}, u32[]{:S(2)}) collective-permute-start(bf16[160,2048]{1,0:T(8,128)(2,1)} %get-tuple-element.66), channel_id=1, source_target_pairs={{0,2},{1,3},{2,0},{3,1},{4,6},{5,7},{6,4},{7,5},{8,10},{9,11},{10,... | collective-permute-start | bytes 1966088 | tf_op jit(solution)/shard_map/ppermute | solution.py:559
  75.9 2.8 %copy-done = bf16[1,2048,1536]{2,1,0:T(8,128)(2,1)S(1)} copy-done((bf16[1,2048,1536]{2,1,0:T(8,128)(2,1)S(1)}, bf16[1,2048,1536]{2,1,0:T(8,128)(2,1)}, u32[]{:S(2)}) %copy-start) | copy-done | bytes 6291480
  78.7 3.4 %forward.2 = (bf16[256,768]{1,0:T(8,128)(2,1)S(1)}, bf16[256,768]{1,0:T(8,128)(2,1)S(1)}, bf16[768,768]{1,0:T(8,128)(2,1)S(1)}, bf16[2048,768]{1,0:T(8,128)(2,1)S(1)}) custom-call(bf16[160,2048]{1,0:T(8,128)(2,1)S(1)} %get-tuple-element.72.refs_0_, bf16[2048,1536]{1,0:T(8,128)(2,1)S(1)} %bitcast.18, bf16[2048,1536]{1,0:T(8,128)(2,1)S(1)} %bitcast.19), custom_call_target="tpu_custom_call" | custom-call | flops 805306368 | bytes 1 | tf_op jit(solution)/shard_map/forward/pallas_call | solution.py:265
  82.1 1.6 copy-done.2
  84.8 4.7 %inner.2 = (bf16[160,2048]{1,0:T(8,128)(2,1)S(1)}, bf16[768,2048]{1,0:T(8,128)(2,1)S(1)}, bf16[768,768]{1,0:T(8,128)(2,1)S(1)}, bf16[768,768]{1,0:T(8,128)(2,1)S(1)}) custom-call(bf16[160,2048]{1,0:T(8,128)(2,1)S(1)} %get-tuple-element.77.refs_0_, bf16[768,2048]{1,0:T(8,128)(2,1)S(1)} %bitcast.29, bf16[256,768]{1,0:T(8,128)(2,1)S(1)} %get-tuple-element.78.refs_2_, ...), custom_call_target="tpu_custom_call" | custom-call | flops 1 | bytes 1 | tf_op jit(solution)/shard_map/inner/pallas_call | solution.py:335
  92.4 2.8 %copy-done.1 = bf16[1,2048,1536]{2,1,0:T(8,128)(2,1)S(1)} copy-done((bf16[1,2048,1536]{2,1,0:T(8,128)(2,1)S(1)}, bf16[1,2048,1536]{2,1,0:T(8,128)(2,1)}, u32[]{:S(2)}) %copy-start.1) | copy-done | bytes 6291480
  95.2 1.9 copy-done.3
  97.1 1.3 copy-done.13
  98.4 1.1 copy-done.17
  99.5 1.1 copy-done.19
  100.6 1.1 copy-done.21
  102.8 6.9 %forward.3 = (bf16[512,768]{1,0:T(8,128)(2,1)S(1)}, bf16[512,768]{1,0:T(8,128)(2,1)S(1)}, bf16[768,768]{1,0:T(8,128)(2,1)S(1)}, bf16[2048,768]{1,0:T(8,128)(2,1)S(1)}) custom-call(bf16[160,2048]{1,0:T(8,128)(2,1)S(1)} %copy-done.21, bf16[176,2048]{1,0:T(8,128)(2,1)S(1)} %copy-done.17, ...), custom_call_target="tpu_custom_call", output_to_operand_aliasing={{2}: (7, {}), {3}: (8, {})} | custom-call | flops 1610612736 | bytes 1 | tf_op jit(solution)/shard_map/forward/pallas_call | solution.py:265
  109.7 1.6 copy-done.4
  111.3 4.3 %collective-permute-done.4.refs_1_ = bf16[160,2048]{1,0:T(8,128)(2,1)} collective-permute-done((bf16[160,2048]{1,0:T(8,128)(2,1)}, bf16[160,2048]{1,0:T(8,128)(2,1)}, u32[]{:S(2)}, u32[]{:S(2)}) %collective-permute-start.4) | collective-permute-done | bytes 655392 | tf_op jit(solution)/shard_map/ppermute | solution.py:559
  115.6 7.3 %inner.3 = (bf16[160,2048]{1,0:T(8,128)(2,1)S(1)}, bf16[768,2048]{1,0:T(8,128)(2,1)S(1)}, bf16[768,768]{1,0:T(8,128)(2,1)S(1)}, bf16[768,768]{1,0:T(8,128)(2,1)S(1)}) custom-call(bf16[160,2048]{1,0:T(8,128)(2,1)} %collective-permute-done.1.refs_0_, ...), custom_call_target="tpu_custom_call", output_to_operand_aliasing={{1}: (7, {}), {2}: (8, {}), {3}: (9, {})} | custom-call | flops 1 | bytes 1 | tf_op jit(solution)/shard_map/inner/pallas_call | solution.py:335
  122.9 5.1 %give.2 = bf16[4,2304,256]{2,1,0:T(8,128)(2,1)S(1)} custom-call(s32[4]{0:T(128)S(1)} %get-tuple-element.117.which_ref, bf16[8,256,768]{2,1,0:T(8,128)(2,1)S(1)} %bitcast.27, bf16[8,96,768]{2,1,0:T(8,128)(2,1)S(1)} %bitcast.31, bf16[768,2048]{1,0:T(8,128)(2,1)S(1)} %get-tuple-element.90.grads, bf16[768,768]{1,0:T(8,128)(2,1)S(1)} %get-tuple-element.83.gate_ref.gate, ...), custom_call_target="tpu_custom_call" | custom-call | flops 1 | bytes 1 | tf_op jit(solution)/shard_map/give/pallas_call | solution.py:443
  128.1 2.5 %collective-permute-start.9 = (bf16[160,2048]{1,0:T(8,128)(2,1)S(1)}, bf16[160,2048]{1,0:T(8,128)(2,1)S(1)}, u32[]{:S(2)}, u32[]{:S(2)}) collective-permute-start(bf16[160,2048]{1,0:T(8,128)(2,1)S(1)} %get-tuple-element.86), channel_id=1, source_target_pairs={{0,3},{1,2},{2,1},{3,0},{4,7},{5,6},{6,5},{7,4},{8,11},{9,10},{10,... | collective-permute-start | bytes 1966088 | tf_op jit(solution)/shard_map/ppermute | solution.py:559
  130.7 5.1 %give.3.own = bf16[4,2304,256]{2,1,0:T(8,128)(2,1)S(1)} custom-call(s32[4]{0:T(128)S(1)} %get-tuple-element.91.which_ref, bf16[8,256,768]{2,1,0:T(8,128)(2,1)S(1)} %bitcast.28, bf16[8,96,768]{2,1,0:T(8,128)(2,1)S(1)} %bitcast.32, bf16[768,2048]{1,0:T(8,128)(2,1)S(1)} %get-tuple-element.90.grads, bf16[768,768]{1,0:T(8,128)(2,1)S(1)} %get-tuple-element.83.gate_ref.gate, ...), custom_call_target="tpu_custom_call" | custom-call | flops 1 | bytes 1 | tf_op jit(solution)/shard_map/give/pallas_call | solution.py:443
  136.0 2.6 %split.1 = (bf16[1152,256]{1,0:T(8,128)(2,1)S(1)}, bf16[1152,256]{1,0:T(8,128)(2,1)S(1)}, bf16[1152,256]{1,0:T(8,128)(2,1)S(1)}, bf16[1152,256]{1,0:T(8,128)(2,1...) custom-call(bf16[4,2304,256]{2,1,0:T(8,128)(2,1)S(1)} %give.3.own, ...), custom_call_target="tpu_custom_call" | custom-call | flops 1 | bytes 1 | tf_op jit(solution)/shard_map/split/pallas_call | solution.py:476
  138.6 1.6 collective-permute-start.17
  140.2 2.9 %back.1 = (bf16[160,2048]{1,0:T(8,128)(2,1)S(1)}, bf16[160,2048]{1,0:T(8,128)(2,1)S(1)}) custom-call(bf16[768,768]{1,0:T(8,128)(2,1)S(1)} %get-tuple-element.83.gate_ref.gate, bf16[768,768]{1,0:T(8,128)(2,1)S(1)} %get-tuple-element.84.up_ref.up, bf16[2048,1536]{1,0:T(8,128)(2,1)S(1)} %bitcast.26), custom_call_target="tpu_custom_call" | custom-call | flops 1 | bytes 1 | tf_op jit(solution)/shard_map/back/pallas_call | solution.py:380
  143.2 1.6 collective-permute-start.15
  144.7 2.8 %collective-permute-done.9.refs_2_ = bf16[160,2048]{1,0:T(8,128)(2,1)S(1)} collective-permute-done((bf16[160,2048]{1,0:T(8,128)(2,1)S(1)}, bf16[160,2048]{1,0:T(8,128)(2,1)S(1)}, u32[]{:S(2)}, u32[]{:S(2)}) %collective-permute-start.9) | collective-permute-done | bytes 655392 | tf_op jit(solution)/shard_map/ppermute | solution.py:559
  147.6 11.3 %collective-permute-start.10 = (bf16[160,2048]{1,0:T(8,128)(2,1)S(1)}, bf16[160,2048]{1,0:T(8,128)(2,1)S(1)}, u32[]{:S(2)}, u32[]{:S(2)}) collective-permute-start(bf16[160,2048]{1,0:T(8,128)(2,1)S(1)} %get-tuple-element.87), channel_id=1, source_target_pairs={{0,2},{1,3},{2,0},{3,1},{4,6},{5,7},{6,4},{7,5},{8,10},{9,11},{10,... | collective-permute-start | bytes 1966088 | tf_op jit(solution)/shard_map/ppermute | solution.py:559
  158.9 1.5 collective-permute-start.13
  160.3 1.5 collective-permute-start.14
  162.0 1.4 collective-permute-done.12.refs_1_
  163.5 1.5 collective-permute-start.18
  165.1 1.6 collective-permute-start.16
  166.7 8.4 %collective-permute-done.13.refs_1_ = bf16[1152,256]{1,0:T(8,128)(2,1)S(1)} collective-permute-done((bf16[1152,256]{1,0:T(8,128)(2,1)S(1)}, bf16[1152,256]{1,0:T(8,128)(2,1)S(1)}, u32[]{:S(2)}, u32[]{:S(2)}) %collective-permute-start.13) | collective-permute-done | bytes 589856 | tf_op jit(solution)/shard_map/ppermute | solution.py:499
  175.1 1.5 collective-permute-done.14.refs_4_
  176.6 2.1 %combine.1 = (f32[256,2048]{1,0:T(8,128)S(1)}, bf16[256,160]{1,0:T(8,128)(2,1)S(1)}) custom-call(s32[1]{0:T(128)} %bitcast.me_ref, bf16[16,256]{1,0:T(8,128)(2,1)S(1)} %fusion.6.meta_ref, bf16[160,2048]{1,0:T(8,128)(2,1)S(1)} %copy-done.25, bf16[160,2048]{1,0:T(8,128)(2,1)S(1)} %collective-permute-done.12.refs_1_, ...), custom_call_target="tpu_custom_call" | custom-call | flops 1 | bytes 1 | tf_op jit(solution)/shard_map/combine/pallas_call | solution.py:160
  178.8 7.4 %collective-permute-done.18.refs_5_ = bf16[1152,256]{1,0:T(8,128)(2,1)S(1)} collective-permute-done((bf16[1152,256]{1,0:T(8,128)(2,1)S(1)}, bf16[1152,256]{1,0:T(8,128)(2,1)S(1)}, u32[]{:S(2)}, u32[]{:S(2)}) %collective-permute-start.18) | collective-permute-done | bytes 589856 | tf_op jit(solution)/shard_map/ppermute | solution.py:499
  186.1 1.2 collective-permute-done.16.refs_2_
  187.3 1.7 finish.1
  189.0 1.6 last_sum.1
  (66 shorter events, 11.9 us)
Async XLA Ops:
  0.6 30.6 %collective-permute-start.7 = (bf16[256,2048]{1,0:T(8,128)(2,1)}, bf16[256,2048]{1,0:T(8,128)(2,1)S(1)}, u32[]{:S(2)}, u32[]{:S(2)}) collective-permute-start(bf16[256,2048]{1,0:T(8,128)(2,1)} %rest_0_.1), channel_id=1, source_target_pairs={{0,2},{3,1},{4,6},{7,5},{8,10},{11,9},{12,14},{15,13},{16,18},{19,... | collective-permute-start | bytes 3145736 | tf_op jit(solution)/shard_map/ppermute | solution.py:559
  8.0 22.5 %collective-permute-start.2 = (bf16[16,256]{1,0:T(8,128)(2,1)S(1)}, bf16[16,256]{1,0:T(8,128)(2,1)S(1)}, u32[]{:S(2)}, u32[]{:S(2)}) collective-permute-start(bf16[16,256]{1,0:T(8,128)(2,1)S(1)} %fusion.6.meta_ref), channel_id=1, source_target_pairs={{0,2},{3,1},{4,6},{7,5},{8,10},{11,9},{12,14},{15,13},{16,18},{19,... | collective-permute-start | bytes 24584 | tf_op jit(solution)/shard_map/ppermute | solution.py:559
  9.3 1.2 copy-start.14
  10.6 1.2 copy-start.15
  15.7 29.7 %collective-permute-start.5 = (bf16[160,2048]{1,0:T(8,128)(2,1)S(1)}, bf16[160,2048]{1,0:T(8,128)(2,1)S(1)}, u32[]{:S(2)}, u32[]{:S(2)}) collective-permute-start(bf16[160,2048]{1,0:T(8,128)(2,1)S(1)} %get-tuple-element.68), channel_id=1, source_target_pairs={{1,3},{2,0},{5,7},{6,4},{9,11},{10,8},{13,15},{14,12},{17,19},{18,... | collective-permute-start | bytes 1966088 | tf_op jit(solution)/shard_map/ppermute | solution.py:559
  17.0 32.3 %collective-permute-start = (bf16[160,2048]{1,0:T(8,128)(2,1)S(1)}, bf16[160,2048]{1,0:T(8,128)(2,1)S(1)}, u32[]{:S(2)}, u32[]{:S(2)}) collective-permute-start(bf16[160,2048]{1,0:T(8,128)(2,1)S(1)} %get-tuple-element.61), channel_id=1, source_target_pairs={{0,1},{1,0},{2,3},{3,2},{4,5},{5,4},{6,7},{7,6},{8,9},{9,8},{10,11... | collective-permute-start | bytes 1966088 | tf_op jit(solution)/shard_map/ppermute | solution.py:559
  30.6 19.6 %collective-permute-start.3 = (bf16[160,2048]{1,0:T(8,128)(2,1)S(1)}, bf16[160,2048]{1,0:T(8,128)(2,1)S(1)}, u32[]{:S(2)}, u32[]{:S(2)}) collective-permute-start(bf16[160,2048]{1,0:T(8,128)(2,1)S(1)} %get-tuple-element.65), channel_id=1, source_target_pairs={{1,2},{2,1},{5,6},{6,5},{9,10},{10,9},{13,14},{14,13},{17,18},{18,... | collective-permute-start | bytes 1966088 | tf_op jit(solution)/shard_map/ppermute | solution.py:559
  33.7 0.9 copy-start.16
  34.5 57.9 %collective-permute-start.8 = (bf16[176,2048]{1,0:T(8,128)(2,1)}, bf16[176,2048]{1,0:T(8,128)(2,1)}, u32[]{:S(2)}, u32[]{:S(2)}) collective-permute-start(bf16[176,2048]{1,0:T(8,128)(2,1)} %get-tuple-element.71), channel_id=1, source_target_pairs={{2,3},{1,0},{6,7},{5,4},{10,11},{9,8},{14,15},{13,12},{18,19},{17,... | collective-permute-start | bytes 2162696 | tf_op jit(solution)/shard_map/ppermute | solution.py:559
  45.4 0.8 copy-start.18
  46.2 65.1 %collective-permute-start.6 = (bf16[160,2048]{1,0:T(8,128)(2,1)}, bf16[160,2048]{1,0:T(8,128)(2,1)}, u32[]{:S(2)}, u32[]{:S(2)}) collective-permute-start(bf16[160,2048]{1,0:T(8,128)(2,1)} %get-tuple-element.69), channel_id=1, source_target_pairs={{0,3},{1,2},{2,1},{3,0},{4,7},{5,6},{6,5},{7,4},{8,11},{9,10},{10,... | collective-permute-start | bytes 1966088 | tf_op jit(solution)/shard_map/ppermute | solution.py:559
  49.2 0.9 copy-start.20
  50.1 61.2 %collective-permute-start.1 = (bf16[160,2048]{1,0:T(8,128)(2,1)}, bf16[160,2048]{1,0:T(8,128)(2,1)}, u32[]{:S(2)}, u32[]{:S(2)}) collective-permute-start(bf16[160,2048]{1,0:T(8,128)(2,1)} %get-tuple-element.62), channel_id=1, source_target_pairs={{0,1},{1,0},{2,3},{3,2},{4,5},{5,4},{6,7},{7,6},{8,9},{9,8},{10,11... | collective-permute-start | bytes 1966088 | tf_op jit(solution)/shard_map/ppermute | solution.py:559
  50.1 0.9 copy-start.22
  51.0 64.6 %collective-permute-start.4 = (bf16[160,2048]{1,0:T(8,128)(2,1)}, bf16[160,2048]{1,0:T(8,128)(2,1)}, u32[]{:S(2)}, u32[]{:S(2)}) collective-permute-start(bf16[160,2048]{1,0:T(8,128)(2,1)} %get-tuple-element.66), channel_id=1, source_target_pairs={{0,2},{1,3},{2,0},{3,1},{4,6},{5,7},{6,4},{7,5},{8,10},{9,11},{10,... | collective-permute-start | bytes 1966088 | tf_op jit(solution)/shard_map/ppermute | solution.py:559
  75.9 2.8 %copy-start = (bf16[1,2048,1536]{2,1,0:T(8,128)(2,1)S(1)}, bf16[1,2048,1536]{2,1,0:T(8,128)(2,1)}, u32[]{:S(2)}) copy-start(bf16[1,2048,1536]{2,1,0:T(8,128)(2,1)} %param.10) | copy-start | bytes 18874372
  78.7 6.1 %copy-start.10 = (bf16[1,768,2048]{2,1,0:T(8,128)(2,1)S(1)}, bf16[1,768,2048]{2,1,0:T(8,128)(2,1)}, u32[]{:S(2)}) copy-start(bf16[1,768,2048]{2,1,0:T(8,128)(2,1)} %param.11) | copy-start | bytes 9437188
  82.1 1.6 copy-start.2
  83.8 1.0 copy-start.12
  89.5 1.0 copy-start.6
  90.5 1.0 copy-start.8
  91.5 0.8 copy-start.24
  92.4 2.8 %copy-start.1 = (bf16[1,2048,1536]{2,1,0:T(8,128)(2,1)S(1)}, bf16[1,2048,1536]{2,1,0:T(8,128)(2,1)}, u32[]{:S(2)}) copy-start(bf16[1,2048,1536]{2,1,0:T(8,128)(2,1)} %param.10) | copy-start | bytes 18874372
  95.2 1.9 copy-start.3
  97.1 1.3 copy-start.13
  98.4 1.1 copy-start.17
  99.5 1.1 copy-start.19
  100.6 1.1 copy-start.21
  101.7 1.1 copy-start.23
  102.7 12.8 %copy-start.7 = (bf16[768,768]{1,0:T(8,128)(2,1)S(1)}, bf16[768,768]{1,0:T(8,128)(2,1)}, u32[]{:S(2)}) copy-start(bf16[768,768]{1,0:T(8,128)(2,1)} %copy-done.6) | copy-start | bytes 3538948
  102.7 12.8 %copy-start.9 = (bf16[768,768]{1,0:T(8,128)(2,1)S(1)}, bf16[768,768]{1,0:T(8,128)(2,1)}, u32[]{:S(2)}) copy-start(bf16[768,768]{1,0:T(8,128)(2,1)} %copy-done.8) | copy-start | bytes 3538948
  102.7 12.8 %copy-start.11 = (bf16[1,768,2048]{2,1,0:T(8,128)(2,1)S(1)}, bf16[1,768,2048]{2,1,0:T(8,128)(2,1)}, u32[]{:S(2)}) copy-start(bf16[1,768,2048]{2,1,0:T(8,128)(2,1)} %param.11) | copy-start | bytes 9437188
  109.7 1.6 copy-start.4
  115.6 7.3 %copy-start.5 = (bf16[2048,768]{1,0:T(8,128)(2,1)S(1)}, bf16[2048,768]{1,0:T(8,128)(2,1)}, u32[]{:S(2)}) copy-start(bf16[2048,768]{1,0:T(8,128)(2,1)} %copy-done.4) | copy-start | bytes 9437188
  122.9 17.3 %slice-start = ((s8[6291456]{0:T(1024)(128)(4,1)}), s8[4194304]{0:T(1024)(128)(4,1)S(1)}, s32[]{:S(2)}) async-start(s8[6291456]{0:T(1024)(128)(4,1)} %bitcast.24), calls=%async_computation | async-start | bytes 8388608
  128.0 8.0 %collective-permute-start.11 = (bf16[4,2304,256]{2,1,0:T(8,128)(2,1)S(1)}, bf16[4,2304,256]{2,1,0:T(8,128)(2,1)S(1)}, u32[]{:S(2)}, u32[]{:S(2)}) collective-permute-start(bf16[4,2304,256]{2,1,0:T(8,128)(2,1)S(1)} %give.2), channel_id=1, source_target_pairs={{0,4},{4,0},{8,12},{12,8},{16,20},{20,16},{24,28},{28,24},{1,5},{5... | collective-permute-start | bytes 14155784 | tf_op jit(solution)/shard_map/ppermute | solution.py:603
  128.1 19.4 %collective-permute-start.9 = (bf16[160,2048]{1,0:T(8,128)(2,1)S(1)}, bf16[160,2048]{1,0:T(8,128)(2,1)S(1)}, u32[]{:S(2)}, u32[]{:S(2)}) collective-permute-start(bf16[160,2048]{1,0:T(8,128)(2,1)S(1)} %get-tuple-element.86), channel_id=1, source_target_pairs={{0,3},{1,2},{2,1},{3,0},{4,7},{5,6},{6,5},{7,4},{8,11},{9,10},{10,... | collective-permute-start | bytes 1966088 | tf_op jit(solution)/shard_map/ppermute | solution.py:559
  130.7 9.5 %slice-start.1 = ((s8[6291456]{0:T(1024)(128)(4,1)}), s8[2097152]{0:T(1024)(128)(4,1)S(1)}, s32[]{:S(2)}) async-start(s8[6291456]{0:T(1024)(128)(4,1)} %bitcast.24), calls=%async_computation.1 | async-start | bytes 4194304
  138.6 21.7 %collective-permute-start.17 = (bf16[1152,256]{1,0:T(8,128)(2,1)S(1)}, bf16[1152,256]{1,0:T(8,128)(2,1)S(1)}, u32[]{:S(2)}, u32[]{:S(2)}) collective-permute-start(bf16[1152,256]{1,0:T(8,128)(2,1)S(1)} %get-tuple-element.104), channel_id=1, source_target_pairs={{0,16},{4,20},{8,24},{12,28},{16,0},{20,4},{24,8},{28,12},{1,17},{... | collective-permute-start | bytes 1769480 | tf_op jit(solution)/shard_map/ppermute | solution.py:499
  143.1 20.4 %collective-permute-start.12 = (bf16[160,2048]{1,0:T(8,128)(2,1)S(1)}, bf16[160,2048]{1,0:T(8,128)(2,1)S(1)}, u32[]{:S(2)}, u32[]{:S(2)}) collective-permute-start(bf16[160,2048]{1,0:T(8,128)(2,1)S(1)} %get-tuple-element.94), channel_id=1, source_target_pairs={{0,1},{1,0},{2,3},{3,2},{4,5},{5,4},{6,7},{7,6},{8,9},{9,8},{10,11... | collective-permute-start | bytes 1966088 | tf_op jit(solution)/shard_map/ppermute | solution.py:559
  143.2 21.8 %collective-permute-start.15 = (bf16[1152,256]{1,0:T(8,128)(2,1)S(1)}, bf16[1152,256]{1,0:T(8,128)(2,1)S(1)}, u32[]{:S(2)}, u32[]{:S(2)}) collective-permute-start(bf16[1152,256]{1,0:T(8,128)(2,1)S(1)} %get-tuple-element.99), channel_id=1, source_target_pairs={{0,8},{4,12},{8,0},{12,4},{16,24},{20,28},{24,16},{28,20},{1,9},{5... | collective-permute-start | bytes 1769480 | tf_op jit(solution)/shard_map/ppermute | solution.py:499
  147.6 41.4 %collective-permute-start.10 = (bf16[160,2048]{1,0:T(8,128)(2,1)S(1)}, bf16[160,2048]{1,0:T(8,128)(2,1)S(1)}, u32[]{:S(2)}, u32[]{:S(2)}) collective-permute-start(bf16[160,2048]{1,0:T(8,128)(2,1)S(1)} %get-tuple-element.87), channel_id=1, source_target_pairs={{0,2},{1,3},{2,0},{3,1},{4,6},{5,7},{6,4},{7,5},{8,10},{9,11},{10,... | collective-permute-start | bytes 1966088 | tf_op jit(solution)/shard_map/ppermute | solution.py:559
  158.9 16.3 %collective-permute-start.13 = (bf16[1152,256]{1,0:T(8,128)(2,1)S(1)}, bf16[1152,256]{1,0:T(8,128)(2,1)S(1)}, u32[]{:S(2)}, u32[]{:S(2)}) collective-permute-start(bf16[1152,256]{1,0:T(8,128)(2,1)S(1)} %get-tuple-element.95), channel_id=1, source_target_pairs={{0,8},{4,12},{8,0},{12,4},{16,24},{20,28},{24,16},{28,20},{1,9},{5... | collective-permute-start | bytes 1769480 | tf_op jit(solution)/shard_map/ppermute | solution.py:499
  160.3 16.3 %collective-permute-start.14 = (bf16[1152,256]{1,0:T(8,128)(2,1)S(1)}, bf16[1152,256]{1,0:T(8,128)(2,1)S(1)}, u32[]{:S(2)}, u32[]{:S(2)}) collective-permute-start(bf16[1152,256]{1,0:T(8,128)(2,1)S(1)} %get-tuple-element.96), channel_id=1, source_target_pairs={{0,16},{4,20},{8,24},{12,28},{16,0},{20,4},{24,8},{28,12},{1,17},{... | collective-permute-start | bytes 1769480 | tf_op jit(solution)/shard_map/ppermute | solution.py:499
  162.0 14.6 %copy-start.25 = (bf16[160,2048]{1,0:T(8,128)(2,1)S(1)}, bf16[160,2048]{1,0:T(8,128)(2,1)}, u32[]{:S(2)}) copy-start(bf16[160,2048]{1,0:T(8,128)(2,1)} %copy-done.24) | copy-start | bytes 1966084
  163.5 22.6 %collective-permute-start.18 = (bf16[1152,256]{1,0:T(8,128)(2,1)S(1)}, bf16[1152,256]{1,0:T(8,128)(2,1)S(1)}, u32[]{:S(2)}, u32[]{:S(2)}) collective-permute-start(bf16[1152,256]{1,0:T(8,128)(2,1)S(1)} %add_convert_fusion), channel_id=1, source_target_pairs={{0,8},{4,12},{8,0},{12,4},{16,24},{20,28},{24,16},{28,20},{1,9},{5... | collective-permute-start | bytes 1769480 | tf_op jit(solution)/shard_map/ppermute | solution.py:499
  165.1 22.2 %collective-permute-start.16 = (bf16[1152,256]{1,0:T(8,128)(2,1)S(1)}, bf16[1152,256]{1,0:T(8,128)(2,1)S(1)}, u32[]{:S(2)}, u32[]{:S(2)}) collective-permute-start(bf16[1152,256]{1,0:T(8,128)(2,1)S(1)} %add_convert_fusion.1), channel_id=1, source_target_pairs={{0,16},{4,20},{8,24},{12,28},{16,0},{20,4},{24,8},{28,12},{1,17},{... | collective-permute-start | bytes 1769480 | tf_op jit(solution)/shard_map/ppermute | solution.py:499

commit v5 on v4

--- a/solution.py
+++ b/solution.py
@@ -321,7 +321,7 @@
     units = w_down.shape[0]
     tile = math.gcd(units, 256)
     tiles = units // tile
-    block = min(width, 512)
+    block = min(width, 1024)
     total, parts = parts_of(capacity, group)
     held, part = parts[not before]
 
@@ -376,7 +376,7 @@
     width, units = w_pair.shape[0], gate.shape[1]
     held, part = parts_of(capacity, group)[1][False]
     sources = group - 2
-    block = min(width, 512)
+    block = min(width, 1024)
     return pl.pallas_call(
         functools.partial(back_kernel, sources),
         grid=(width // block,),

time: 191 us -> 191 us (level)
  transfers between devices with their start and end apart: 19 -> 19, of which waited for: 11 -> 11; matrix products, arithmetic and copies ran while one was open for 1% -> 1% of each run, Pallas kernels for 19% -> 18%
where the time goes in v5:
time: 191 us; the launch traced here: 190 us
  starting transfers between devices  63.8 us (33%)
  waiting for transfers between devices  49.1 us (26%)
  Pallas kernels  48.4 us (25%)
  local copies, waits for them, and re-layouts  26.1 us (14%)
    ppermute x12, starting transfers between devices, move(): return lax.ppermute(array, 'expert', pairs)  54.4 us
    ppermute x12, waiting for transfers between devices, move(): return lax.ppermute(array, 'expert', pairs)  30.4 us
    unnamed x56, local copies, waits for them, and re-layouts  26.1 us
    ppermute x6, waiting for transfers between devices, halvings(): terms[r ^ 1 << bit].append(lax.ppermute(mine[0], 'dp', pairs))  18.5 us
    pallas_call x2, Pallas kernels, inner(): pl.pallas_call(functools.partial(inner_kernel, sizes, len(sources) * capa...  11.1 us
    pallas_call x2, Pallas kernels, forward(): pl.pallas_call(functools.partial(forward_kernel, sizes), grid=(tiles,), i...  10.3 us
    pallas_call x2, Pallas kernels, give(): pl.pallas_call(functools.partial(give_kernel, shares, chunk), grid_spec=p...  10.2 us
    ppermute x6, starting transfers between devices, halvings(): terms[r ^ 1 << bit].append(lax.ppermute(mine[0], 'dp', pairs))  9.23 us
  transfers between devices with their start and end apart: 19, of which 11 were waited for; matrix products, arithmetic and copies ran while one was open for 1% of the time, Pallas kernels for 18%

profile of v5, /device:TPU:0, one launch (start us, length us, event | category | flops | bytes accessed | tf_op | source)
XLA Modules:
  0.0 190.1 jit_solution(3590816216753964678)
XLA Ops:
  0.6 6.0 %collective-permute-start.7 = (bf16[256,2048]{1,0:T(8,128)(2,1)}, bf16[256,2048]{1,0:T(8,128)(2,1)S(1)}, u32[]{:S(2)}, u32[]{:S(2)}) collective-permute-start(bf16[256,2048]{1,0:T(8,128)(2,1)} %rest_0_.1), channel_id=1, source_target_pairs={{0,2},{3,1},{4,6},{7,5},{8,10},{11,9},{12,14},{15,13},{16,18},{19,... | collective-permute-start | bytes 3145736 | tf_op jit(solution)/shard_map/ppermute | solution.py:559
  8.0 1.3 collective-permute-start.2
  9.3 1.2 copy-done.14
  10.6 1.2 copy-done.15
  11.8 3.9 %pack.2 = (bf16[160,2048]{1,0:T(8,128)(2,1)S(1)}, bf16[160,2048]{1,0:T(8,128)(2,1)S(1)}, bf16[160,2048]{1,0:T(8,128)(2,1)S(1)}, bf16[160,2048]{1,0:T(8,128)(2,1)...) custom-call(s32[1]{0:T(128)} %bitcast.me_ref, ...), custom_call_target="tpu_custom_call" | custom-call | flops 1 | bytes 1 | tf_op jit(solution)/shard_map/pack/pallas_call | solution.py:118
  15.7 1.3 collective-permute-start.5
  17.0 2.6 %collective-permute-start = (bf16[160,2048]{1,0:T(8,128)(2,1)S(1)}, bf16[160,2048]{1,0:T(8,128)(2,1)S(1)}, u32[]{:S(2)}, u32[]{:S(2)}) collective-permute-start(bf16[160,2048]{1,0:T(8,128)(2,1)S(1)} %get-tuple-element.61), channel_id=1, source_target_pairs={{0,1},{1,0},{2,3},{3,2},{4,5},{5,4},{6,7},{7,6},{8,9},{9,8},{10,11... | collective-permute-start | bytes 1966088 | tf_op jit(solution)/shard_map/ppermute | solution.py:559
  19.6 11.0 %collective-permute-done.2.meta_ref = bf16[16,256]{1,0:T(8,128)(2,1)S(1)} collective-permute-done((bf16[16,256]{1,0:T(8,128)(2,1)S(1)}, bf16[16,256]{1,0:T(8,128)(2,1)S(1)}, u32[]{:S(2)}, u32[]{:S(2)}) %collective-permute-start.2) | collective-permute-done | bytes 8224 | tf_op jit(solution)/shard_map/ppermute | solution.py:559
  31.3 2.4 %pack.3 = (bf16[176,2048]{1,0:T(8,128)(2,1)S(1)}, bf16[176,2048]{1,0:T(8,128)(2,1)}) custom-call(s32[1]{0:T(128)} %bitcast.me_ref, bf16[16,256]{1,0:T(8,128)(2,1)S(1)} %collective-permute-done.2.meta_ref, bf16[256,2048]{1,0:T(8,128)(2,1)S(1)} %collective-permute-done.7.rest_0_), custom_call_target="tpu_custom_call" | custom-call | flops 1 | bytes 1 | tf_op jit(solution)/shard_map/pack/pallas_call | solution.py:118
  34.5 1.3 collective-permute-start.8
  35.8 9.5 %collective-permute-done.5.refs_2_ = bf16[160,2048]{1,0:T(8,128)(2,1)S(1)} collective-permute-done((bf16[160,2048]{1,0:T(8,128)(2,1)S(1)}, bf16[160,2048]{1,0:T(8,128)(2,1)S(1)}, u32[]{:S(2)}, u32[]{:S(2)}) %collective-permute-start.5) | collective-permute-done | bytes 655392 | tf_op jit(solution)/shard_map/ppermute | solution.py:559
  46.2 2.5 %collective-permute-start.6 = (bf16[160,2048]{1,0:T(8,128)(2,1)}, bf16[160,2048]{1,0:T(8,128)(2,1)}, u32[]{:S(2)}, u32[]{:S(2)}) collective-permute-start(bf16[160,2048]{1,0:T(8,128)(2,1)} %get-tuple-element.69), channel_id=1, source_target_pairs={{0,3},{1,2},{2,1},{3,0},{4,7},{5,6},{6,5},{7,4},{8,11},{9,10},{10,... | collective-permute-start | bytes 1966088 | tf_op jit(solution)/shard_map/ppermute | solution.py:559
  51.0 24.9 %collective-permute-start.4 = (bf16[160,2048]{1,0:T(8,128)(2,1)}, bf16[160,2048]{1,0:T(8,128)(2,1)}, u32[]{:S(2)}, u32[]{:S(2)}) collective-permute-start(bf16[160,2048]{1,0:T(8,128)(2,1)} %get-tuple-element.66), channel_id=1, source_target_pairs={{0,2},{1,3},{2,0},{3,1},{4,6},{5,7},{6,4},{7,5},{8,10},{9,11},{10,... | collective-permute-start | bytes 1966088 | tf_op jit(solution)/shard_map/ppermute | solution.py:559
  75.9 2.8 %copy-done = bf16[1,2048,1536]{2,1,0:T(8,128)(2,1)S(1)} copy-done((bf16[1,2048,1536]{2,1,0:T(8,128)(2,1)S(1)}, bf16[1,2048,1536]{2,1,0:T(8,128)(2,1)}, u32[]{:S(2)}) %copy-start) | copy-done | bytes 6291480
  78.7 3.4 %forward.2 = (bf16[256,768]{1,0:T(8,128)(2,1)S(1)}, bf16[256,768]{1,0:T(8,128)(2,1)S(1)}, bf16[768,768]{1,0:T(8,128)(2,1)S(1)}, bf16[2048,768]{1,0:T(8,128)(2,1)S(1)}) custom-call(bf16[160,2048]{1,0:T(8,128)(2,1)S(1)} %get-tuple-element.72.refs_0_, bf16[2048,1536]{1,0:T(8,128)(2,1)S(1)} %bitcast.18, bf16[2048,1536]{1,0:T(8,128)(2,1)S(1)} %bitcast.19), custom_call_target="tpu_custom_call" | custom-call | flops 805306368 | bytes 1 | tf_op jit(solution)/shard_map/forward/pallas_call | solution.py:265
  82.1 1.6 copy-done.2
  84.8 4.3 %inner.2 = (bf16[160,2048]{1,0:T(8,128)(2,1)S(1)}, bf16[768,2048]{1,0:T(8,128)(2,1)S(1)}, bf16[768,768]{1,0:T(8,128)(2,1)S(1)}, bf16[768,768]{1,0:T(8,128)(2,1)S(1)}) custom-call(bf16[160,2048]{1,0:T(8,128)(2,1)S(1)} %get-tuple-element.77.refs_0_, bf16[768,2048]{1,0:T(8,128)(2,1)S(1)} %bitcast.29, bf16[256,768]{1,0:T(8,128)(2,1)S(1)} %get-tuple-element.78.refs_2_, ...), custom_call_target="tpu_custom_call" | custom-call | flops 1 | bytes 1 | tf_op jit(solution)/shard_map/inner/pallas_call | solution.py:335
  92.0 2.8 %copy-done.1 = bf16[1,2048,1536]{2,1,0:T(8,128)(2,1)S(1)} copy-done((bf16[1,2048,1536]{2,1,0:T(8,128)(2,1)S(1)}, bf16[1,2048,1536]{2,1,0:T(8,128)(2,1)}, u32[]{:S(2)}) %copy-start.1) | copy-done | bytes 6291480
  94.8 1.9 copy-done.3
  96.7 1.3 copy-done.13
  98.0 1.1 copy-done.17
  99.1 1.1 copy-done.19
  100.2 1.1 copy-done.21
  102.3 6.9 %forward.3 = (bf16[512,768]{1,0:T(8,128)(2,1)S(1)}, bf16[512,768]{1,0:T(8,128)(2,1)S(1)}, bf16[768,768]{1,0:T(8,128)(2,1)S(1)}, bf16[2048,768]{1,0:T(8,128)(2,1)S(1)}) custom-call(bf16[160,2048]{1,0:T(8,128)(2,1)S(1)} %copy-done.21, bf16[176,2048]{1,0:T(8,128)(2,1)S(1)} %copy-done.17, ...), custom_call_target="tpu_custom_call", output_to_operand_aliasing={{2}: (7, {}), {3}: (8, {})} | custom-call | flops 1610612736 | bytes 1 | tf_op jit(solution)/shard_map/forward/pallas_call | solution.py:265
  109.3 1.6 copy-done.4
  110.9 4.7 %collective-permute-done.4.refs_1_ = bf16[160,2048]{1,0:T(8,128)(2,1)} collective-permute-done((bf16[160,2048]{1,0:T(8,128)(2,1)}, bf16[160,2048]{1,0:T(8,128)(2,1)}, u32[]{:S(2)}, u32[]{:S(2)}) %collective-permute-start.4) | collective-permute-done | bytes 655392 | tf_op jit(solution)/shard_map/ppermute | solution.py:559
  115.6 6.8 %inner.3 = (bf16[160,2048]{1,0:T(8,128)(2,1)S(1)}, bf16[768,2048]{1,0:T(8,128)(2,1)S(1)}, bf16[768,768]{1,0:T(8,128)(2,1)S(1)}, bf16[768,768]{1,0:T(8,128)(2,1)S(1)}) custom-call(bf16[160,2048]{1,0:T(8,128)(2,1)} %collective-permute-done.1.refs_0_, ...), custom_call_target="tpu_custom_call", output_to_operand_aliasing={{1}: (7, {}), {2}: (8, {}), {3}: (9, {})} | custom-call | flops 1 | bytes 1 | tf_op jit(solution)/shard_map/inner/pallas_call | solution.py:335
  122.5 5.1 %give.2 = bf16[4,2304,256]{2,1,0:T(8,128)(2,1)S(1)} custom-call(s32[4]{0:T(128)S(1)} %get-tuple-element.117.which_ref, bf16[8,256,768]{2,1,0:T(8,128)(2,1)S(1)} %bitcast.27, bf16[8,96,768]{2,1,0:T(8,128)(2,1)S(1)} %bitcast.31, bf16[768,2048]{1,0:T(8,128)(2,1)S(1)} %get-tuple-element.90.grads, bf16[768,768]{1,0:T(8,128)(2,1)S(1)} %get-tuple-element.83.gate_ref.gate, ...), custom_call_target="tpu_custom_call" | custom-call | flops 1 | bytes 1 | tf_op jit(solution)/shard_map/give/pallas_call | solution.py:443
  127.7 2.5 %collective-permute-start.9 = (bf16[160,2048]{1,0:T(8,128)(2,1)S(1)}, bf16[160,2048]{1,0:T(8,128)(2,1)S(1)}, u32[]{:S(2)}, u32[]{:S(2)}) collective-permute-start(bf16[160,2048]{1,0:T(8,128)(2,1)S(1)} %get-tuple-element.86), channel_id=1, source_target_pairs={{0,3},{1,2},{2,1},{3,0},{4,7},{5,6},{6,5},{7,4},{8,11},{9,10},{10,... | collective-permute-start | bytes 1966088 | tf_op jit(solution)/shard_map/ppermute | solution.py:559
  130.2 5.1 %give.3.own = bf16[4,2304,256]{2,1,0:T(8,128)(2,1)S(1)} custom-call(s32[4]{0:T(128)S(1)} %get-tuple-element.91.which_ref, bf16[8,256,768]{2,1,0:T(8,128)(2,1)S(1)} %bitcast.28, bf16[8,96,768]{2,1,0:T(8,128)(2,1)S(1)} %bitcast.32, bf16[768,2048]{1,0:T(8,128)(2,1)S(1)} %get-tuple-element.90.grads, bf16[768,768]{1,0:T(8,128)(2,1)S(1)} %get-tuple-element.83.gate_ref.gate, ...), custom_call_target="tpu_custom_call" | custom-call | flops 1 | bytes 1 | tf_op jit(solution)/shard_map/give/pallas_call | solution.py:443
  135.6 2.6 %split.1 = (bf16[1152,256]{1,0:T(8,128)(2,1)S(1)}, bf16[1152,256]{1,0:T(8,128)(2,1)S(1)}, bf16[1152,256]{1,0:T(8,128)(2,1)S(1)}, bf16[1152,256]{1,0:T(8,128)(2,1...) custom-call(bf16[4,2304,256]{2,1,0:T(8,128)(2,1)S(1)} %give.3.own, ...), custom_call_target="tpu_custom_call" | custom-call | flops 1 | bytes 1 | tf_op jit(solution)/shard_map/split/pallas_call | solution.py:476
  138.2 1.6 collective-permute-start.17
  139.8 2.5 %back.1 = (bf16[160,2048]{1,0:T(8,128)(2,1)S(1)}, bf16[160,2048]{1,0:T(8,128)(2,1)S(1)}) custom-call(bf16[768,768]{1,0:T(8,128)(2,1)S(1)} %get-tuple-element.83.gate_ref.gate, bf16[768,768]{1,0:T(8,128)(2,1)S(1)} %get-tuple-element.84.up_ref.up, bf16[2048,1536]{1,0:T(8,128)(2,1)S(1)} %bitcast.26), custom_call_target="tpu_custom_call" | custom-call | flops 1 | bytes 1 | tf_op jit(solution)/shard_map/back/pallas_call | solution.py:380
  142.3 1.6 collective-permute-start.15
  143.9 3.2 %collective-permute-done.9.refs_2_ = bf16[160,2048]{1,0:T(8,128)(2,1)S(1)} collective-permute-done((bf16[160,2048]{1,0:T(8,128)(2,1)S(1)}, bf16[160,2048]{1,0:T(8,128)(2,1)S(1)}, u32[]{:S(2)}, u32[]{:S(2)}) %collective-permute-start.9) | collective-permute-done | bytes 655392 | tf_op jit(solution)/shard_map/ppermute | solution.py:559
  147.1 11.3 %collective-permute-start.10 = (bf16[160,2048]{1,0:T(8,128)(2,1)S(1)}, bf16[160,2048]{1,0:T(8,128)(2,1)S(1)}, u32[]{:S(2)}, u32[]{:S(2)}) collective-permute-start(bf16[160,2048]{1,0:T(8,128)(2,1)S(1)} %get-tuple-element.87), channel_id=1, source_target_pairs={{0,2},{1,3},{2,0},{3,1},{4,6},{5,7},{6,4},{7,5},{8,10},{9,11},{10,... | collective-permute-start | bytes 1966088 | tf_op jit(solution)/shard_map/ppermute | solution.py:559
  158.4 1.5 collective-permute-start.13
  159.9 1.5 collective-permute-start.14
  161.6 1.4 collective-permute-done.12.refs_1_
  163.0 1.5 collective-permute-start.18
  164.7 1.6 collective-permute-start.16
  166.3 8.4 %collective-permute-done.13.refs_1_ = bf16[1152,256]{1,0:T(8,128)(2,1)S(1)} collective-permute-done((bf16[1152,256]{1,0:T(8,128)(2,1)S(1)}, bf16[1152,256]{1,0:T(8,128)(2,1)S(1)}, u32[]{:S(2)}, u32[]{:S(2)}) %collective-permute-start.13) | collective-permute-done | bytes 589856 | tf_op jit(solution)/shard_map/ppermute | solution.py:499
  174.7 1.5 collective-permute-done.14.refs_4_
  176.2 2.1 %combine.1 = (f32[256,2048]{1,0:T(8,128)S(1)}, bf16[256,160]{1,0:T(8,128)(2,1)S(1)}) custom-call(s32[1]{0:T(128)} %bitcast.me_ref, bf16[16,256]{1,0:T(8,128)(2,1)S(1)} %fusion.6.meta_ref, bf16[160,2048]{1,0:T(8,128)(2,1)S(1)} %copy-done.25, bf16[160,2048]{1,0:T(8,128)(2,1)S(1)} %collective-permute-done.12.refs_1_, ...), custom_call_target="tpu_custom_call" | custom-call | flops 1 | bytes 1 | tf_op jit(solution)/shard_map/combine/pallas_call | solution.py:160
  178.3 7.3 %collective-permute-done.18.refs_5_ = bf16[1152,256]{1,0:T(8,128)(2,1)S(1)} collective-permute-done((bf16[1152,256]{1,0:T(8,128)(2,1)S(1)}, bf16[1152,256]{1,0:T(8,128)(2,1)S(1)}, u32[]{:S(2)}, u32[]{:S(2)}) %collective-permute-start.18) | collective-permute-done | bytes 589856 | tf_op jit(solution)/shard_map/ppermute | solution.py:499
  185.7 1.2 collective-permute-done.16.refs_2_
  186.9 1.7 finish.1
  188.5 1.6 last_sum.1
  (66 shorter events, 11.9 us)
Async XLA Ops:
  0.6 30.6 %collective-permute-start.7 = (bf16[256,2048]{1,0:T(8,128)(2,1)}, bf16[256,2048]{1,0:T(8,128)(2,1)S(1)}, u32[]{:S(2)}, u32[]{:S(2)}) collective-permute-start(bf16[256,2048]{1,0:T(8,128)(2,1)} %rest_0_.1), channel_id=1, source_target_pairs={{0,2},{3,1},{4,6},{7,5},{8,10},{11,9},{12,14},{15,13},{16,18},{19,... | collective-permute-start | bytes 3145736 | tf_op jit(solution)/shard_map/ppermute | solution.py:559
  8.0 22.5 %collective-permute-start.2 = (bf16[16,256]{1,0:T(8,128)(2,1)S(1)}, bf16[16,256]{1,0:T(8,128)(2,1)S(1)}, u32[]{:S(2)}, u32[]{:S(2)}) collective-permute-start(bf16[16,256]{1,0:T(8,128)(2,1)S(1)} %fusion.6.meta_ref), channel_id=1, source_target_pairs={{0,2},{3,1},{4,6},{7,5},{8,10},{11,9},{12,14},{15,13},{16,18},{19,... | collective-permute-start | bytes 24584 | tf_op jit(solution)/shard_map/ppermute | solution.py:559
  9.3 1.2 copy-start.14
  10.6 1.2 copy-start.15
  15.7 29.7 %collective-permute-start.5 = (bf16[160,2048]{1,0:T(8,128)(2,1)S(1)}, bf16[160,2048]{1,0:T(8,128)(2,1)S(1)}, u32[]{:S(2)}, u32[]{:S(2)}) collective-permute-start(bf16[160,2048]{1,0:T(8,128)(2,1)S(1)} %get-tuple-element.68), channel_id=1, source_target_pairs={{1,3},{2,0},{5,7},{6,4},{9,11},{10,8},{13,15},{14,12},{17,19},{18,... | collective-permute-start | bytes 1966088 | tf_op jit(solution)/shard_map/ppermute | solution.py:559
  17.0 32.3 %collective-permute-start = (bf16[160,2048]{1,0:T(8,128)(2,1)S(1)}, bf16[160,2048]{1,0:T(8,128)(2,1)S(1)}, u32[]{:S(2)}, u32[]{:S(2)}) collective-permute-start(bf16[160,2048]{1,0:T(8,128)(2,1)S(1)} %get-tuple-element.61), channel_id=1, source_target_pairs={{0,1},{1,0},{2,3},{3,2},{4,5},{5,4},{6,7},{7,6},{8,9},{9,8},{10,11... | collective-permute-start | bytes 1966088 | tf_op jit(solution)/shard_map/ppermute | solution.py:559
  30.6 19.6 %collective-permute-start.3 = (bf16[160,2048]{1,0:T(8,128)(2,1)S(1)}, bf16[160,2048]{1,0:T(8,128)(2,1)S(1)}, u32[]{:S(2)}, u32[]{:S(2)}) collective-permute-start(bf16[160,2048]{1,0:T(8,128)(2,1)S(1)} %get-tuple-element.65), channel_id=1, source_target_pairs={{1,2},{2,1},{5,6},{6,5},{9,10},{10,9},{13,14},{14,13},{17,18},{18,... | collective-permute-start | bytes 1966088 | tf_op jit(solution)/shard_map/ppermute | solution.py:559
  33.7 0.9 copy-start.16
  34.5 57.5 %collective-permute-start.8 = (bf16[176,2048]{1,0:T(8,128)(2,1)}, bf16[176,2048]{1,0:T(8,128)(2,1)}, u32[]{:S(2)}, u32[]{:S(2)}) collective-permute-start(bf16[176,2048]{1,0:T(8,128)(2,1)} %get-tuple-element.71), channel_id=1, source_target_pairs={{2,3},{1,0},{6,7},{5,4},{10,11},{9,8},{14,15},{13,12},{18,19},{17,... | collective-permute-start | bytes 2162696 | tf_op jit(solution)/shard_map/ppermute | solution.py:559
  45.4 0.8 copy-start.18
  46.2 64.7 %collective-permute-start.6 = (bf16[160,2048]{1,0:T(8,128)(2,1)}, bf16[160,2048]{1,0:T(8,128)(2,1)}, u32[]{:S(2)}, u32[]{:S(2)}) collective-permute-start(bf16[160,2048]{1,0:T(8,128)(2,1)} %get-tuple-element.69), channel_id=1, source_target_pairs={{0,3},{1,2},{2,1},{3,0},{4,7},{5,6},{6,5},{7,4},{8,11},{9,10},{10,... | collective-permute-start | bytes 1966088 | tf_op jit(solution)/shard_map/ppermute | solution.py:559
  49.2 0.9 copy-start.20
  50.1 60.8 %collective-permute-start.1 = (bf16[160,2048]{1,0:T(8,128)(2,1)}, bf16[160,2048]{1,0:T(8,128)(2,1)}, u32[]{:S(2)}, u32[]{:S(2)}) collective-permute-start(bf16[160,2048]{1,0:T(8,128)(2,1)} %get-tuple-element.62), channel_id=1, source_target_pairs={{0,1},{1,0},{2,3},{3,2},{4,5},{5,4},{6,7},{7,6},{8,9},{9,8},{10,11... | collective-permute-start | bytes 1966088 | tf_op jit(solution)/shard_map/ppermute | solution.py:559
  50.1 0.9 copy-start.22
  51.0 64.6 %collective-permute-start.4 = (bf16[160,2048]{1,0:T(8,128)(2,1)}, bf16[160,2048]{1,0:T(8,128)(2,1)}, u32[]{:S(2)}, u32[]{:S(2)}) collective-permute-start(bf16[160,2048]{1,0:T(8,128)(2,1)} %get-tuple-element.66), channel_id=1, source_target_pairs={{0,2},{1,3},{2,0},{3,1},{4,6},{5,7},{6,4},{7,5},{8,10},{9,11},{10,... | collective-permute-start | bytes 1966088 | tf_op jit(solution)/shard_map/ppermute | solution.py:559
  75.9 2.8 %copy-start = (bf16[1,2048,1536]{2,1,0:T(8,128)(2,1)S(1)}, bf16[1,2048,1536]{2,1,0:T(8,128)(2,1)}, u32[]{:S(2)}) copy-start(bf16[1,2048,1536]{2,1,0:T(8,128)(2,1)} %param.10) | copy-start | bytes 18874372
  78.7 6.1 %copy-start.10 = (bf16[1,768,2048]{2,1,0:T(8,128)(2,1)S(1)}, bf16[1,768,2048]{2,1,0:T(8,128)(2,1)}, u32[]{:S(2)}) copy-start(bf16[1,768,2048]{2,1,0:T(8,128)(2,1)} %param.11) | copy-start | bytes 9437188
  82.1 1.6 copy-start.2
  83.8 1.0 copy-start.12
  89.0 1.0 copy-start.6
  90.1 1.0 copy-start.8
  91.1 0.8 copy-start.24
  92.0 2.8 %copy-start.1 = (bf16[1,2048,1536]{2,1,0:T(8,128)(2,1)S(1)}, bf16[1,2048,1536]{2,1,0:T(8,128)(2,1)}, u32[]{:S(2)}) copy-start(bf16[1,2048,1536]{2,1,0:T(8,128)(2,1)} %param.10) | copy-start | bytes 18874372
  94.8 1.9 copy-start.3
  96.7 1.3 copy-start.13
  98.0 1.1 copy-start.17
  99.1 1.1 copy-start.19
  100.2 1.1 copy-start.21
  101.2 1.1 copy-start.23
  102.3 13.3 %copy-start.7 = (bf16[768,768]{1,0:T(8,128)(2,1)S(1)}, bf16[768,768]{1,0:T(8,128)(2,1)}, u32[]{:S(2)}) copy-start(bf16[768,768]{1,0:T(8,128)(2,1)} %copy-done.6) | copy-start | bytes 3538948
  102.3 13.3 %copy-start.9 = (bf16[768,768]{1,0:T(8,128)(2,1)S(1)}, bf16[768,768]{1,0:T(8,128)(2,1)}, u32[]{:S(2)}) copy-start(bf16[768,768]{1,0:T(8,128)(2,1)} %copy-done.8) | copy-start | bytes 3538948
  102.3 13.3 %copy-start.11 = (bf16[1,768,2048]{2,1,0:T(8,128)(2,1)S(1)}, bf16[1,768,2048]{2,1,0:T(8,128)(2,1)}, u32[]{:S(2)}) copy-start(bf16[1,768,2048]{2,1,0:T(8,128)(2,1)} %param.11) | copy-start | bytes 9437188
  109.3 1.6 copy-start.4
  115.6 6.9 %copy-start.5 = (bf16[2048,768]{1,0:T(8,128)(2,1)S(1)}, bf16[2048,768]{1,0:T(8,128)(2,1)}, u32[]{:S(2)}) copy-start(bf16[2048,768]{1,0:T(8,128)(2,1)} %copy-done.4) | copy-start | bytes 9437188
  122.5 17.3 %slice-start = ((s8[6291456]{0:T(1024)(128)(4,1)}), s8[4194304]{0:T(1024)(128)(4,1)S(1)}, s32[]{:S(2)}) async-start(s8[6291456]{0:T(1024)(128)(4,1)} %bitcast.24), calls=%async_computation | async-start | bytes 8388608
  127.6 8.0 %collective-permute-start.11 = (bf16[4,2304,256]{2,1,0:T(8,128)(2,1)S(1)}, bf16[4,2304,256]{2,1,0:T(8,128)(2,1)S(1)}, u32[]{:S(2)}, u32[]{:S(2)}) collective-permute-start(bf16[4,2304,256]{2,1,0:T(8,128)(2,1)S(1)} %give.2), channel_id=1, source_target_pairs={{0,4},{4,0},{8,12},{12,8},{16,20},{20,16},{24,28},{28,24},{1,5},{5... | collective-permute-start | bytes 14155784 | tf_op jit(solution)/shard_map/ppermute | solution.py:603
  127.7 19.4 %collective-permute-start.9 = (bf16[160,2048]{1,0:T(8,128)(2,1)S(1)}, bf16[160,2048]{1,0:T(8,128)(2,1)S(1)}, u32[]{:S(2)}, u32[]{:S(2)}) collective-permute-start(bf16[160,2048]{1,0:T(8,128)(2,1)S(1)} %get-tuple-element.86), channel_id=1, source_target_pairs={{0,3},{1,2},{2,1},{3,0},{4,7},{5,6},{6,5},{7,4},{8,11},{9,10},{10,... | collective-permute-start | bytes 1966088 | tf_op jit(solution)/shard_map/ppermute | solution.py:559
  130.2 9.5 %slice-start.1 = ((s8[6291456]{0:T(1024)(128)(4,1)}), s8[2097152]{0:T(1024)(128)(4,1)S(1)}, s32[]{:S(2)}) async-start(s8[6291456]{0:T(1024)(128)(4,1)} %bitcast.24), calls=%async_computation.1 | async-start | bytes 4194304
  138.2 21.7 %collective-permute-start.17 = (bf16[1152,256]{1,0:T(8,128)(2,1)S(1)}, bf16[1152,256]{1,0:T(8,128)(2,1)S(1)}, u32[]{:S(2)}, u32[]{:S(2)}) collective-permute-start(bf16[1152,256]{1,0:T(8,128)(2,1)S(1)} %get-tuple-element.104), channel_id=1, source_target_pairs={{0,16},{4,20},{8,24},{12,28},{16,0},{20,4},{24,8},{28,12},{1,17},{... | collective-permute-start | bytes 1769480 | tf_op jit(solution)/shard_map/ppermute | solution.py:499
  142.3 20.8 %collective-permute-start.12 = (bf16[160,2048]{1,0:T(8,128)(2,1)S(1)}, bf16[160,2048]{1,0:T(8,128)(2,1)S(1)}, u32[]{:S(2)}, u32[]{:S(2)}) collective-permute-start(bf16[160,2048]{1,0:T(8,128)(2,1)S(1)} %get-tuple-element.94), channel_id=1, source_target_pairs={{0,1},{1,0},{2,3},{3,2},{4,5},{5,4},{6,7},{7,6},{8,9},{9,8},{10,11... | collective-permute-start | bytes 1966088 | tf_op jit(solution)/shard_map/ppermute | solution.py:559
  142.3 22.2 %collective-permute-start.15 = (bf16[1152,256]{1,0:T(8,128)(2,1)S(1)}, bf16[1152,256]{1,0:T(8,128)(2,1)S(1)}, u32[]{:S(2)}, u32[]{:S(2)}) collective-permute-start(bf16[1152,256]{1,0:T(8,128)(2,1)S(1)} %get-tuple-element.99), channel_id=1, source_target_pairs={{0,8},{4,12},{8,0},{12,4},{16,24},{20,28},{24,16},{28,20},{1,9},{5... | collective-permute-start | bytes 1769480 | tf_op jit(solution)/shard_map/ppermute | solution.py:499
  147.1 41.4 %collective-permute-start.10 = (bf16[160,2048]{1,0:T(8,128)(2,1)S(1)}, bf16[160,2048]{1,0:T(8,128)(2,1)S(1)}, u32[]{:S(2)}, u32[]{:S(2)}) collective-permute-start(bf16[160,2048]{1,0:T(8,128)(2,1)S(1)} %get-tuple-element.87), channel_id=1, source_target_pairs={{0,2},{1,3},{2,0},{3,1},{4,6},{5,7},{6,4},{7,5},{8,10},{9,11},{10,... | collective-permute-start | bytes 1966088 | tf_op jit(solution)/shard_map/ppermute | solution.py:559
  158.4 16.3 %collective-permute-start.13 = (bf16[1152,256]{1,0:T(8,128)(2,1)S(1)}, bf16[1152,256]{1,0:T(8,128)(2,1)S(1)}, u32[]{:S(2)}, u32[]{:S(2)}) collective-permute-start(bf16[1152,256]{1,0:T(8,128)(2,1)S(1)} %get-tuple-element.95), channel_id=1, source_target_pairs={{0,8},{4,12},{8,0},{12,4},{16,24},{20,28},{24,16},{28,20},{1,9},{5... | collective-permute-start | bytes 1769480 | tf_op jit(solution)/shard_map/ppermute | solution.py:499
  159.9 16.3 %collective-permute-start.14 = (bf16[1152,256]{1,0:T(8,128)(2,1)S(1)}, bf16[1152,256]{1,0:T(8,128)(2,1)S(1)}, u32[]{:S(2)}, u32[]{:S(2)}) collective-permute-start(bf16[1152,256]{1,0:T(8,128)(2,1)S(1)} %get-tuple-element.96), channel_id=1, source_target_pairs={{0,16},{4,20},{8,24},{12,28},{16,0},{20,4},{24,8},{28,12},{1,17},{... | collective-permute-start | bytes 1769480 | tf_op jit(solution)/shard_map/ppermute | solution.py:499
  161.6 14.6 %copy-start.25 = (bf16[160,2048]{1,0:T(8,128)(2,1)S(1)}, bf16[160,2048]{1,0:T(8,128)(2,1)}, u32[]{:S(2)}) copy-start(bf16[160,2048]{1,0:T(8,128)(2,1)} %copy-done.24) | copy-start | bytes 1966084
  163.0 22.6 %collective-permute-start.18 = (bf16[1152,256]{1,0:T(8,128)(2,1)S(1)}, bf16[1152,256]{1,0:T(8,128)(2,1)S(1)}, u32[]{:S(2)}, u32[]{:S(2)}) collective-permute-start(bf16[1152,256]{1,0:T(8,128)(2,1)S(1)} %add_convert_fusion), channel_id=1, source_target_pairs={{0,8},{4,12},{8,0},{12,4},{16,24},{20,28},{24,16},{28,20},{1,9},{5... | collective-permute-start | bytes 1769480 | tf_op jit(solution)/shard_map/ppermute | solution.py:499
  164.7 22.2 %collective-permute-start.16 = (bf16[1152,256]{1,0:T(8,128)(2,1)S(1)}, bf16[1152,256]{1,0:T(8,128)(2,1)S(1)}, u32[]{:S(2)}, u32[]{:S(2)}) collective-permute-start(bf16[1152,256]{1,0:T(8,128)(2,1)S(1)} %add_convert_fusion.1), channel_id=1, source_target_pairs={{0,16},{4,20},{8,24},{12,28},{16,0},{20,4},{24,8},{28,12},{1,17},{... | collective-permute-start | bytes 1769480 | tf_op jit(solution)/shard_map/ppermute | solution.py:499
